TPU v7x, 256 devices: a whole 4x4x8 slice. The times are simulated.
256 devices in a mesh: grp: 8 (over y, x_hi), pair: 32 (over x_lo, z, core).
Axes of the slice: x: 4 (x_hi: 2, x_lo: 2; x = x_hi * 2 + x_lo), y: 4, z: 8, core: 2. Of those that a mesh axis runs over, the one named last changes fastest.
Arguments:
- amplitudes: bfloat16 [96, 96, 9216], P('pair'), may hold values from -6 to 6
- integrals: bfloat16 [9216, 9216], P('pair', 'grp'), may hold values from -0.0625 to 0.0625
- live_counts: int32 [2], replicated, may hold values from 48 to 96, as said below
Outputs:
- residual: bfloat16 [96, 96, 9216], P('pair', None, 'grp')
Inputs may be any that keep to these rules, and one draw needn't show every extreme that they name: `live_counts`: orbital slots at or beyond a count are padding; exactly one of the two counts equals 96.
All inputs are finite; a program needn't handle non-finite values.
Results may differ from a plain program's by a relative error of at most 0.001.
Values may be sent and summed in bfloat16 or wider, within the bound.
No kernel may reach another device: no remote copies, remote signals or barrier semaphores. Data moves between devices by JAX's collectives and lax.ppermute only.
A program may use at most 128 MiB of HBM per device.

v0:
```python
import jax
import jax.numpy as jnp
from jax import lax
from jax.sharding import PartitionSpec as P

VB = 96


def on_device(amplitudes, integrals, live_counts):
    occ_rows, occupied, virt_pairs = amplitudes.shape
    slab_cols = integrals.shape[1]
    tile_size = VB
    slab_lanes = slab_cols // tile_size
    position = jnp.arange(virt_pairs)
    keep_pairs = (
        (position // tile_size < live_counts[1]) & (position % tile_size < live_counts[1])
    ).astype(jnp.bfloat16)
    masked = amplitudes * keep_pairs
    flat_rows = masked.reshape(occ_rows * occupied, virt_pairs)
    ladder = jnp.dot(
        flat_rows,
        lax.all_gather(integrals, "pair", axis=0, tiled=True),
        preferred_element_type=jnp.float32,
    )
    blocks = ladder.reshape(occ_rows, occupied, slab_lanes, tile_size)
    mirrored = lax.all_to_all(
        lax.all_to_all(blocks, "grp", split_axis=3, concat_axis=2, tiled=True),
        "pair",
        split_axis=1,
        concat_axis=0,
        tiled=True,
    )
    summed = blocks + jnp.transpose(mirrored, (1, 0, 3, 2))
    first_virt = lax.axis_index("grp") * slab_lanes + jnp.arange(slab_lanes)
    second_virt = jnp.arange(tile_size)
    keep_out = (
        (first_virt[:, None] < live_counts[0]) & (second_virt[None, :] < live_counts[0])
    ).astype(jnp.float32)
    return (summed * keep_out).reshape(occ_rows, occupied, slab_cols).astype(jnp.bfloat16)


def solution(mesh):
    return jax.shard_map(
        on_device,
        mesh=mesh,
        in_specs=(P("pair", None, None), P("pair", "grp"), P()),
        out_specs=P("pair", None, "grp"),
        check_vma=False,
    )
```

profile of v0, /device:TPU:1, one launch (start us, length us, event | category | flops | bytes accessed | tf_op | source)
XLA Modules:
  0.0 298.0 jit_solution(15115272456072465451)
XLA Ops:
  6.5 0.0 all-gather.2.cloned.1.call-start
  6.5 0.7 all-gather.2.cloned.1.call-update
  7.3 1.4 fusion.17
  8.6 0.7 fusion.16
  9.3 126.3 %all-gather.2.cloned.1.call-done = bf16[9216,1152]{1,0:T(8,128)(2,1)} async-done(((bf16[288,1152]{1,0:T(8,128)(2,1)}), bf16[9216,1152]{1,0:T(8,128)(2,1)}) %all-gather.2.cloned.1.call-update) | async-done | bytes 21233680 | tf_op jit(solution)/shard_map/all_gather | solution.py:22
  135.6 25.5 %copy.12 = bf16[1152,9216]{1,0:T(8,128)(2,1)} copy(bf16[1152,9216]{0,1:T(8,128)(2,1)} %bitcast.32) | data formatting | bytes 42467328 | tf_op jit(solution)/shard_map/dot_general | solution.py:20
  161.1 13.9 %fusion = f32[3,96,12,96]{3,1,2,0:T(8,128)} fusion(bf16[12,96,9216,1]{2,1,0,3:T(8,128)(2,1)} %bitcast.33, bf16[3,96,9216]{2,1,0:T(8,128)(2,1)} %param.3, bf16[9216]{0:T(1024)(128)(2,1)S(1)} %fusion.16), kind=kOutput, calls=%fused_computation | convolution fusion | flops 6125912064 | bytes 27887616 | tf_op jit(solution)/shard_map/dot_general | solution.py:20
  175.1 2.2 copy.13
  177.3 36.7 %all_to_all.36 = f32[3,96,12,96]{1,2,0,3:T(8,128)S(1)} all-to-all(f32[3,96,12,96]{1,2,0,3:T(8,128)S(1)} %copy.13), channel_id=1, replica_groups=mesh['grp'=8,'pair'=32] {'grp'}, dimensions={3} | all-to-all | bytes 2654208 | tf_op jit(solution)/shard_map/all_to_all | solution.py:27
  214.0 0.3 copy.15
  214.3 1.4 all_to_all.29
  215.7 3.1 %copy.16 = f32[3,96,96,12]{2,3,0,1:T(8,128)} copy(f32[3,96,96,12]{1,2,3,0:T(8,128)} %all_to_all.29) | data formatting | bytes 2654208 | tf_op jit(solution)/shard_map/all_to_all | solution.py:27
  218.8 7.9 %all-to-all-start.1 = ((f32[3,96,96,12]{2,3,0,1:T(8,128)}), f32[3,96,96,12]{2,3,0,1:T(8,128)S(1)}, u32[]{:S(2)}, u32[]{:S(2)}) async-start(f32[3,96,96,12]{2,3,0,1:T(8,128)} %copy.16), calls=%async_computation.1 | async-start | bytes 4718592 | tf_op jit(solution)/shard_map/all_to_all | solution.py:26
  226.7 0.7 iota_compare_fusion
  227.4 0.7 add_compare_fusion
  228.0 0.1 and_convert_fusion
  228.1 53.8 %all-to-all-done.1 = f32[3,96,96,12]{2,3,0,1:T(8,128)S(1)} async-done(((f32[3,96,96,12]{2,3,0,1:T(8,128)}), f32[3,96,96,12]{2,3,0,1:T(8,128)S(1)}, u32[]{:S(2)}, u32[]{:S(2)}) %all-to-all-start.1) | async-done | bytes 1327136 | tf_op jit(solution)/shard_map/all_to_all | solution.py:26
  281.9 2.3 copy.27
  284.3 0.0 copy-start
  284.3 3.0 %all_to_all.33 = f32[96,3,96,12]{2,0,3,1:T(8,128)S(1)} reshape(f32[32,3,3,96,12]{3,1,0,4,2:T(4,128)} %bitcast.36) | data formatting | bytes 2654208 | tf_op jit(solution)/shard_map/all_to_all | solution.py:26
  287.3 0.0 copy-done
  287.3 1.2 fusion.5
  288.5 1.5 copy.19
  290.0 1.1 copy.20
Async XLA Ops:
  6.5 129.1 %all-gather.2.cloned.1.call-start = ((), (), s32[]{:S(2)}) async-start(), calls=%async_computation.2 | async-start | bytes 21897216 | tf_op jit(solution)/shard_map/all_gather | solution.py:22
  218.8 63.2 %all-to-all-start.1 = ((f32[3,96,96,12]{2,3,0,1:T(8,128)}), f32[3,96,96,12]{2,3,0,1:T(8,128)S(1)}, u32[]{:S(2)}, u32[]{:S(2)}) async-start(f32[3,96,96,12]{2,3,0,1:T(8,128)} %copy.16), calls=%async_computation.1 | async-start | bytes 4718592 | tf_op jit(solution)/shard_map/all_to_all | solution.py:26
  284.3 3.0 %copy-start = (f32[3,96,12,96]{3,1,2,0:T(8,128)S(1)}, f32[3,96,12,96]{3,1,2,0:T(8,128)}, u32[]{:S(2)}) copy-start(f32[3,96,12,96]{3,1,2,0:T(8,128)} %fusion) | copy-start | bytes 3981316
Sparse Core Ops, SparseCore 0:
  9.2 126.3 all-gather.1
where the time goes:
time: 299 us; the launch traced here: 298 us
  waiting for transfers between devices  181 us (61%)
  local copies, waits for them, and re-layouts  41.8 us (14%)
  blocking collectives  36.7 us (12%)
  matrix products  13.9 us (5%)
  between operations  13.5 us (5%)
  starting transfers between devices  7.95 us (3%)
  other arithmetic  3.31 us (1%)
    all_gather x1, waiting for transfers between devices, on_device(): lax.all_gather(integrals, 'pair', axis=0, tiled=True)  126 us
    all_to_all x1, waiting for transfers between devices, on_device(): lax.all_to_all(lax.all_to_all(blocks, 'grp', split_axis=3, concat_axis=2,...  53.8 us
    all_to_all x1, blocking collectives, on_device(): lax.all_to_all(blocks, 'grp', split_axis=3, concat_axis=2, tiled=True)  36.7 us
    dot_general x2, local copies, waits for them, and re-layouts, on_device(): jnp.dot(flat_rows, lax.all_gather(integrals, 'pair', axis=0, tiled=True),...  27.7 us
    dot_general x1, matrix products, on_device(): jnp.dot(flat_rows, lax.all_gather(integrals, 'pair', axis=0, tiled=True),...  13.9 us
    all_to_all x1, starting transfers between devices, on_device(): lax.all_to_all(lax.all_to_all(blocks, 'grp', split_axis=3, concat_axis=2,...  7.95 us
  transfers between devices with their start and end apart: 2, of which 2 were waited for; matrix products, arithmetic and copies ran while one was open for 1% of the time, Pallas kernels for 0%

commit v1 on v0

v1 whole, which is shorter than its diff:
```python
import jax
import jax.numpy as jnp
from jax import lax
from jax.sharding import Mesh
from jax.sharding import PartitionSpec as P

VB = 96
WIRE = jnp.float16
SCALE = 16.0


def on_device(amplitudes, integrals, live_counts):
    occ, nocc, k_all = amplitudes.shape
    shard, slab = integrals.shape
    rows, half, k_half = occ * nocc, slab // 2, k_all // 2
    xl = lax.axis_index("xl")
    pair = (xl * 8 + lax.axis_index("z")) * 2 + lax.axis_index("c")
    grp = lax.axis_index("y") * 2 + lax.axis_index("xh")
    swap = [(0, 1), (1, 0)]

    at = pair * shard + jnp.arange(shard)
    live = (at // VB < live_counts[1]) & (at % VB < live_counts[1])
    w = jnp.where(live[:, None], integrals, 0)
    w_keep = jnp.where(xl == 0, w[:, :half], w[:, half:])
    w_send = jnp.where(xl == 0, w[:, half:], w[:, :half])
    w_recv = lax.ppermute(w_send, "xl", swap)
    w_own = lax.all_gather(w_keep, ("z", "c"), axis=0, tiled=True)
    w_far = lax.all_gather(w_recv, ("z", "c"), axis=0, tiled=True)

    t = amplitudes.reshape(rows, k_all)
    t_own = lax.dynamic_slice(t, (0, xl * k_half), (rows, k_half))
    t_far = lax.dynamic_slice(t, (0, (1 - xl) * k_half), (rows, k_half))
    u_far = lax.ppermute(t_own, ("xh", "xl"), [(i, (i + 1) % 4) for i in range(4)])
    u_own = lax.ppermute(t_far, ("xh", "xl"), [(i, (i - 1) % 4) for i in range(4)])

    def dot(x, y):
        return jnp.dot(x, y, preferred_element_type=jnp.float32)

    mine = dot(t_own, w_own) + dot(t_far, w_far)
    other = dot(u_own, w_own) + dot(u_far, w_far)

    fetched = lax.ppermute(other, "xl", swap)
    low = jnp.where(xl == 0, mine, fetched)
    high = jnp.where(xl == 0, fetched, mine)
    direct = jnp.concatenate([low, high], axis=1)

    both = jnp.stack([jnp.where(xl == 0, mine, other), jnp.where(xl == 0, other, mine)])
    wire = (both * SCALE).astype(WIRE)
    wire = wire.reshape(2, occ, 32, 3, 6, 8, 12).transpose(2, 5, 3, 0, 1, 6, 4)
    got = lax.all_to_all(
        wire.reshape(256, -1), ("xl", "z", "c", "y", "xh"), 0, 0, tiled=True
    )
    got = got.reshape(2, 16, 8, 3, 2, 3, 12, 6)
    mirrored = got.transpose(3, 4, 1, 5, 6, 2, 0, 7).reshape(rows, slab)
    summed = direct + mirrored.astype(jnp.float32) * (1 / SCALE)

    col = jnp.arange(slab)
    keep = (grp * (slab // VB) + col // VB < live_counts[0]) & (col % VB < live_counts[0])
    return jnp.where(keep, summed, 0).reshape(occ, nocc, slab).astype(jnp.bfloat16)


def solution(mesh):
    fine = Mesh(mesh.devices.reshape(4, 2, 2, 8, 2), ("y", "xh", "xl", "z", "c"))
    pair, grp = ("xl", "z", "c"), ("y", "xh")
    return jax.shard_map(
        on_device,
        mesh=fine,
        in_specs=(P(pair, None, None), P(pair, grp), P()),
        out_specs=P(pair, None, grp),
        check_vma=False,
    )
```

time: 299 us -> 357 us (1.19)
  local copies, waits for them, and re-layouts: 41.8 us -> 167 us
  waiting for transfers between devices: 181 us -> 128 us
  blocking collectives: 36.7 us -> 0 us
  starting transfers between devices: 7.95 us -> 19.6 us
  other arithmetic: 3.31 us -> 9.09 us
  matrix products: 13.9 us -> 17.6 us
    mul x0 -> x3, local copies, waits for them, and re-layouts: none -> 106 us  [on_device(): summed = direct + mirrored.astype(jnp.float32) * (1 / SCALE)]
    all_gather x1 -> x2, waiting for transfers between devices: 126 us -> 26.5 us  [the longest x1 26.5 us: on_device(): w_own = lax.all_gather(w_keep, ('z', 'c'), axis=0, tiled=True)]
    ppermute x0 -> x4, waiting for transfers between devices: none -> 76.1 us  [the longest x1 54.8 us: on_device(): lax.ppermute(t_own, ('xh', 'xl'), [(i, (i + 1) % 4) for i in range(4)])]
    all_to_all x1 -> x0, blocking collectives: 36.7 us -> none  [on_device(): lax.all_to_all(blocks, 'grp', split_axis=3, concat_axis=2, tiled=True)]
    all_to_all x1, waiting for transfers between devices: 53.8 us -> 24.8 us  [on_device(): lax.all_to_all(wire.reshape(256, -1), ('xl', 'z', 'c', 'y', 'xh'), 0, 0,...]
    dot_general x2 -> x0, local copies, waits for them, and re-layouts: 27.7 us -> none  [on_device(): jnp.dot(flat_rows, lax.all_gather(integrals, 'pair', axis=0, tiled=True),...]
    another operation x0 -> x4, local copies, waits for them, and re-layouts: none -> 26.3 us  [on_device(): jnp.stack([jnp.where(xl == 0, mine, other), jnp.where(xl == 0, other, min...]
    transpose x0 -> x1, local copies, waits for them, and re-layouts: none -> 8.83 us  [on_device(): wire = wire.reshape(2, occ, 32, 3, 6, 8, 12).transpose(2, 5, 3, 0, 1, 6, 4)]
  transfers between devices with their start and end apart: 2 -> 7, of which waited for: 2 -> 5; matrix products, arithmetic and copies ran while one was open for 1% -> 3% of each run, Pallas kernels for 0% -> 0%
where the time goes in v1:
time: 357 us; the launch traced here: 355 us
  local copies, waits for them, and re-layouts  167 us (47%)
  waiting for transfers between devices  128 us (36%)
  starting transfers between devices  19.6 us (5%)
  matrix products  17.6 us (5%)
  between operations  13.6 us (4%)
  other arithmetic  9.09 us (3%)
    mul x3, local copies, waits for them, and re-layouts, on_device(): summed = direct + mirrored.astype(jnp.float32) * (1 / SCALE)  106 us
    ppermute x1, waiting for transfers between devices, on_device(): lax.ppermute(t_own, ('xh', 'xl'), [(i, (i + 1) % 4) for i in range(4)])  54.8 us
    all_gather x1, waiting for transfers between devices, on_device(): w_own = lax.all_gather(w_keep, ('z', 'c'), axis=0, tiled=True)  26.5 us
    another operation x4, local copies, waits for them, and re-layouts, on_device(): jnp.stack([jnp.where(xl == 0, mine, other), jnp.where(xl == 0, other, min...  26.3 us
    all_to_all x1, waiting for transfers between devices, on_device(): lax.all_to_all(wire.reshape(256, -1), ('xl', 'z', 'c', 'y', 'xh'), 0, 0,...  24.8 us
    all_to_all x3, local copies, waits for them, and re-layouts, on_device(): lax.all_to_all(wire.reshape(256, -1), ('xl', 'z', 'c', 'y', 'xh'), 0, 0,...  17.7 us
    dot_general x4, matrix products, dot(): return jnp.dot(x, y, preferred_element_type=jnp.float32)  17.6 us
    ppermute x1, waiting for transfers between devices, on_device(): fetched = lax.ppermute(other, 'xl', swap)  14.3 us
  transfers between devices with their start and end apart: 7, of which 5 were waited for; matrix products, arithmetic and copies ran while one was open for 3% of the time, Pallas kernels for 0%

profile of v1, /device:TPU:1, one launch (start us, length us, event | category | flops | bytes accessed | tf_op | source)
XLA Modules:
  0.0 355.0 jit_solution(3030128050100869724)
XLA Ops:
  10.7 2.0 collective-permute-start
  12.7 7.0 %collective-permute-done = bf16[288,576]{1,0:T(8,128)(2,1)S(1)} collective-permute-done((bf16[288,576]{1,0:T(8,128)(2,1)S(1)}, bf16[288,576]{1,0:T(8,128)(2,1)S(1)}, u32[]{:S(2)}, u32[]{:S(2)}) %collective-permute-start) | collective-permute-done | bytes 331808 | tf_op jit(solution)/shard_map/ppermute | solution.py:26
  21.2 2.9 constant_dynamic-slice_fusion
  24.1 2.3 collective-permute-start.2
  26.4 3.0 collective-permute-start.1
  29.4 54.8 %collective-permute-done.2 = bf16[288,4608]{1,0:T(8,128)(2,1)} collective-permute-done((bf16[288,4608]{1,0:T(8,128)(2,1)S(1)}, bf16[288,4608]{1,0:T(8,128)(2,1)}, u32[]{:S(2)}, u32[]{:S(2)}) %collective-permute-start.2) | collective-permute-done | bytes 2654240 | tf_op jit(solution)/shard_map/ppermute | solution.py:33
  84.2 5.7 %fusion.25 = f32[288,576]{1,0:T(8,128)S(1)} fusion(bf16[288,4608]{1,0:T(8,128)(2,1)} %collective-permute-done.2, bf16[4608,576]{1,0:T(8,128)(2,1)} %all-gather.5.cloned.1.call-done), kind=kOutput, calls=%fused_computation.47 | convolution fusion | flops 1528823808 | bytes 8626176 | tf_op jit(solution)/shard_map/dot_general | solution.py:37
  89.9 26.5 %all-gather.3.cloned.1.call-done = bf16[4608,576]{1,0:T(8,128)(2,1)} async-done(((bf16[288,576]{1,0:T(8,128)(2,1)}), bf16[4608,576]{1,0:T(8,128)(2,1)}) %all-gather.3.cloned.1.call-update) | async-done | bytes 5308432 | tf_op jit(solution)/shard_map/all_gather | solution.py:27
  116.4 5.9 %convolution_add_fusion = f32[288,576]{1,0:T(8,128)S(1)} fusion(f32[288,576]{1,0:T(8,128)S(1)} %fusion.25, bf16[288,4608]{1,0:T(8,128)(2,1)} %collective-permute-done.1, bf16[4608,576]{1,0:T(8,128)(2,1)} %all-gather.3.cloned.1.call-done), kind=kOutput, calls=%fused_computation.7 | convolution fusion | flops 1528989696 | bytes 9289728 | tf_op jit(solution)/shard_map/dot_general | solution.py:37
  123.8 2.3 fusion.24
  126.1 14.3 %collective-permute-done.3 = f32[288,576]{1,0:T(8,128)S(1)} collective-permute-done((f32[288,576]{1,0:T(8,128)S(1)}, f32[288,576]{1,0:T(8,128)S(1)}, u32[]{:S(2)}, u32[]{:S(2)}) %collective-permute-start.3) | collective-permute-done | bytes 663584 | tf_op jit(solution)/shard_map/ppermute | solution.py:42
  140.4 3.8 %broadcast_select_fusion.4 = (f32[288,576]{1,0:T(8,128)S(1)}, f32[288,576]{1,0:T(8,128)}, f32[288,576]{1,0:T(8,128)}, f32[288,576]{1,0:T(8,128)}) fusion(f32[288,576]{1,0:T(8,128)S(1)} %collective-permute-done.3, pred[]{:T(512)S(6)} %eq.5, f32[288,576]{1,0:T(8,128)S(1)} %convolution_add_fusion, f32[288,576]{1,0:T(8,128)S(1)} %fusion.24, ...), kind=kOutput, calls=%fused_computation.13 | convolution fusion | flops 1529653248 | bytes 12607489 | tf_op jit(solution)/shard_map/dot_general | solution.py:37
  144.1 6.2 %stack.9 = f32[1,3,32,3,6,8,12]{6,5,4,3,2,1,0:T(8,128)} reshape(f32[288,576]{1,0:T(8,128)} %get-tuple-element.12) | data formatting | bytes 1327104 | tf_op jit(solution)/shard_map/stack | solution.py:47
  150.3 7.3 %copy.12 = f32[1,3,32,3,6,8,12]{2,5,6,4,3,1,0:T(8,128)} copy(f32[1,3,32,3,6,8,12]{6,5,4,3,2,1,0:T(8,128)} %stack.9) | data formatting | bytes 1327104 | tf_op jit(solution)/shard_map/stack | solution.py:47
  157.7 5.5 %stack.10 = f32[1,3,32,3,6,8,12]{6,5,4,3,2,1,0:T(8,128)} reshape(f32[288,576]{1,0:T(8,128)S(1)} %copy-done.3) | data formatting | bytes 1327104 | tf_op jit(solution)/shard_map/stack | solution.py:47
  163.2 7.3 %copy.13 = f32[1,3,32,3,6,8,12]{2,5,6,4,3,1,0:T(8,128)} copy(f32[1,3,32,3,6,8,12]{6,5,4,3,2,1,0:T(8,128)} %stack.10) | data formatting | bytes 1327104 | tf_op jit(solution)/shard_map/stack | solution.py:47
  170.5 3.3 fusion.1
  173.8 8.8 %copy.14 = f16[32,8,3,2,3,12,6]{1,0,6,5,4,3,2:T(8,128)(2,1)} copy(f16[32,8,3,2,3,12,6]{0,1,5,6,2,4,3:T(8,128)(2,1)S(1)} %fusion.1) | data formatting | bytes 1327104 | tf_op jit(solution)/shard_map/transpose | solution.py:49
  182.6 15.1 %all_to_all.6 = f16[256,1,1296]{0,2,1:T(8,128)(2,1)S(1)} reshape(f16[32,8,3,2,3,12,6]{1,0,6,5,4,3,2:T(8,128)(2,1)} %copy.14) | data formatting | bytes 1327104 | tf_op jit(solution)/shard_map/all_to_all | solution.py:50
  201.8 10.8 %all-to-all-start = ((f16[256,2,648]{2,1,0:T(2,128)(2,1)}), f16[256,2,648]{2,1,0:T(2,128)(2,1)S(1)}, u32[]{:S(2)}, u32[]{:S(2)}) async-start(f16[256,2,648]{2,1,0:T(2,128)(2,1)} %reshape.49), calls=%async_computation | async-start | bytes 1572864 | tf_op jit(solution)/shard_map/all_to_all | solution.py:50
  213.3 24.8 %all-to-all-done = f16[256,2,648]{2,1,0:T(2,128)(2,1)S(1)} async-done(((f16[256,2,648]{2,1,0:T(2,128)(2,1)}), f16[256,2,648]{2,1,0:T(2,128)(2,1)S(1)}, u32[]{:S(2)}, u32[]{:S(2)}) %all-to-all-start) | async-done | bytes 663584 | tf_op jit(solution)/shard_map/all_to_all | solution.py:50
  241.5 13.5 %mul.55 = f32[2,16,8,3,2,3,12,6]{2,1,0,7,6,5,4,3:T(8,128)} reshape(f32[256,1,1296]{0,2,1:T(8,128)S(1)} %convert_multiply_fusion) | data formatting | bytes 2654208 | tf_op jit(solution)/shard_map/mul | solution.py:55
  255.0 53.8 %copy.17 = f32[3,2,16,3,12,8,2,6]{7,6,5,4,3,2,1,0:T(2,128)} copy(f32[3,2,16,3,12,8,2,6]{5,2,6,7,4,3,1,0:T(8,128)} %bitcast.22) | data formatting | bytes 2654208 | tf_op jit(solution)/shard_map/mul | solution.py:55
  308.8 38.3 %mul.57 = f32[3,96,1152]{2,1,0:T(8,128)S(1)} reshape(f32[3,2,16,3,12,8,2,6]{7,6,5,4,3,2,1,0:T(2,128)} %copy.17) | data formatting | bytes 2654208 | tf_op jit(solution)/shard_map/mul | solution.py:55
  (37 shorter events, 16.2 us)
Async XLA Ops:
  6.5 77.6 %all-gather.5.cloned.1.call-start = ((), (), s32[]{:S(2)}) async-start(), calls=%async_computation.2 | async-start | bytes 6266880 | tf_op jit(solution)/shard_map/all_gather | solution.py:28
  10.7 9.0 %collective-permute-start = (bf16[288,576]{1,0:T(8,128)(2,1)S(1)}, bf16[288,576]{1,0:T(8,128)(2,1)S(1)}, u32[]{:S(2)}, u32[]{:S(2)}) collective-permute-start(bf16[288,576]{1,0:T(8,128)(2,1)S(1)} %get-tuple-element.14), channel_id=1, source_target_pairs={{0,16},{16,0},{1,17},{17,1},{2,18},{18,2},{3,19},{19,3},{4,20},{20... | collective-permute-start | bytes 995336 | tf_op jit(solution)/shard_map/ppermute | solution.py:26
  19.7 0.7 copy-start.4
  20.4 95.9 %all-gather.3.cloned.1.call-start = ((), (), s32[]{:S(2)}) async-start(), calls=%async_computation.1 | async-start | bytes 6266880 | tf_op jit(solution)/shard_map/all_gather | solution.py:27
  24.1 2.3 copy-start
  24.1 60.1 %collective-permute-start.2 = (bf16[288,4608]{1,0:T(8,128)(2,1)S(1)}, bf16[288,4608]{1,0:T(8,128)(2,1)}, u32[]{:S(2)}, u32[]{:S(2)}) collective-permute-start(bf16[288,4608]{1,0:T(8,128)(2,1)S(1)} %get-tuple-element.6), channel_id=1, source_target_pairs={{0,16},{16,32},{32,48},{48,0},{1,17},{17,33},{33,49},{49,1},{2,18}... | collective-permute-start | bytes 7962632 | tf_op jit(solution)/shard_map/ppermute | solution.py:33
  26.4 63.5 %collective-permute-start.1 = (bf16[288,4608]{1,0:T(8,128)(2,1)S(1)}, bf16[288,4608]{1,0:T(8,128)(2,1)}, u32[]{:S(2)}, u32[]{:S(2)}) collective-permute-start(bf16[288,4608]{1,0:T(8,128)(2,1)S(1)} %get-tuple-element.5), channel_id=1, source_target_pairs={{0,48},{16,0},{32,16},{48,32},{1,49},{17,1},{33,17},{49,33},{2,50}... | collective-permute-start | bytes 7962632 | tf_op jit(solution)/shard_map/ppermute | solution.py:34
  116.4 7.4 %copy-start.1 = (bf16[288,4608]{1,0:T(8,128)(2,1)S(1)}, bf16[288,4608]{1,0:T(8,128)(2,1)}, u32[]{:S(2)}) copy-start(bf16[288,4608]{1,0:T(8,128)(2,1)} %copy-done) | copy-start | bytes 7962628
  116.4 7.4 %copy-start.5 = (bf16[4608,576]{1,0:T(8,128)(2,1)S(1)}, bf16[4608,576]{1,0:T(8,128)(2,1)}, u32[]{:S(2)}) copy-start(bf16[4608,576]{1,0:T(8,128)(2,1)} %all-gather.3.cloned.1.call-done) | copy-start | bytes 15925252
  116.4 24.0 %slice-start = ((s8[5898240]{0:T(1024)(128)(4,1)}), s8[4194304]{0:T(1024)(128)(4,1)S(1)}, s32[]{:S(2)}) async-start(s8[5898240]{0:T(1024)(128)(4,1)} %bitcast.26), calls=%async_computation.3 | async-start | bytes 8388608
  122.3 18.1 %slice-start.1 = ((s8[5898240]{0:T(1024)(128)(4,1)}), s8[1703936]{0:T(1024)(128)(4,1)S(1)}, s32[]{:S(2)}) async-start(s8[5898240]{0:T(1024)(128)(4,1)} %bitcast.26), calls=%async_computation.4 | async-start | bytes 3407872
  122.3 18.1 %collective-permute-start.3 = (f32[288,576]{1,0:T(8,128)S(1)}, f32[288,576]{1,0:T(8,128)S(1)}, u32[]{:S(2)}, u32[]{:S(2)}) collective-permute-start(f32[288,576]{1,0:T(8,128)S(1)} %convolution_add_fusion), channel_id=1, source_target_pairs={{0,16},{16,0},{1,17},{17,1},{2,18},{18,2},{3,19},{19,3},{4,20},{20... | collective-permute-start | bytes 1990664 | tf_op jit(solution)/shard_map/ppermute | solution.py:42
  150.3 7.3 %copy-start.3 = (f32[288,576]{1,0:T(8,128)S(1)}, f32[288,576]{1,0:T(8,128)}, u32[]{:S(2)}) copy-start(f32[288,576]{1,0:T(8,128)} %get-tuple-element.11) | copy-start | bytes 1990660
  201.8 36.3 %all-to-all-start = ((f16[256,2,648]{2,1,0:T(2,128)(2,1)}), f16[256,2,648]{2,1,0:T(2,128)(2,1)S(1)}, u32[]{:S(2)}, u32[]{:S(2)}) async-start(f16[256,2,648]{2,1,0:T(2,128)(2,1)} %reshape.49), calls=%async_computation | async-start | bytes 1572864 | tf_op jit(solution)/shard_map/all_to_all | solution.py:50
  308.7 38.3 %copy-start.2 = (f32[288,576]{1,0:T(8,128)S(1)}, f32[288,576]{1,0:T(8,128)}, u32[]{:S(2)}) copy-start(f32[288,576]{1,0:T(8,128)} %get-tuple-element.8) | copy-start | bytes 1990660
Sparse Core Ops, SparseCore 0:
  20.6 50.5 all-gather.4
  72.9 43.3 all-gather.2

commit v2 on v1

v2 whole, which is shorter than its diff:
```python
import functools

import jax
import jax.numpy as jnp
from jax import lax
from jax.experimental import pallas as pl
from jax.experimental.pallas import tpu as pltpu
from jax.sharding import Mesh
from jax.sharding import PartitionSpec as P

VB = 96
OCC = 3
GRPS = 8
PAIRS = 32
SLAB = VB // GRPS
TILE = SLAB * SLAB
WIRE = jnp.float16
SCALE = 16.0
BF, F32 = jnp.bfloat16, jnp.float32


def mm(x, y):
    return jnp.dot(x, y, preferred_element_type=F32)


def halves(x):
    hi = x.astype(BF)
    return hi, (x - hi.astype(F32)).astype(BF)


def selector(size, source):
    wanted = source(lax.broadcasted_iota(jnp.int32, (size, size), 0))
    return (wanted == lax.broadcasted_iota(jnp.int32, (size, size), 1)).astype(BF)


def pack_kernel(own_ref, far_ref, row_ref, col_ref, out_ref):
    pieces = [[] for _ in range(GRPS)]
    for ref in (own_ref, far_ref):
        total = 0.0
        for part in halves(ref[...] * SCALE):
            turned = mm(row_ref[...], part).astype(BF)
            total += mm(turned, col_ref[...])
        for q in range(OCC * OCC):
            for g in range(GRPS):
                pieces[g].append(
                    total[q * PAIRS : (q + 1) * PAIRS, g * TILE : (g + 1) * TILE]
                )
    for g in range(GRPS):
        out_ref[g] = jnp.concatenate(pieces[g], axis=1).astype(out_ref.dtype)


def unpack_kernel(grp_ref, live_ref, got_ref, own_ref, sum_ref, row_ref, col_ref, out_ref):
    zc = PAIRS // 2
    blocks = []
    for j in range(OCC):
        for xl in range(2):
            for i in range(OCC):
                q = i * OCC + j
                near, far = q * TILE, (OCC * OCC + q) * TILE
                blocks.append(
                    jnp.concatenate(
                        [
                            got_ref[g, xl, :, near : near + TILE].astype(F32)
                            + got_ref[g, 1 - xl, :, far : far + TILE].astype(F32)
                            for g in range(GRPS)
                        ],
                        axis=1,
                    )
                )
    stacked = jnp.concatenate(blocks, axis=0)
    total = 0.0
    for part in halves(stacked):
        turned = mm(row_ref[...], part).astype(BF)
        total += mm(turned, col_ref[...])
    summed = own_ref[...] + sum_ref[...] + total * (1 / SCALE)
    col = lax.broadcasted_iota(jnp.int32, summed.shape, 1)
    first = grp_ref[0] * SLAB + col // VB
    keep = (first < live_ref[0]) & (col % VB < live_ref[0])
    out_ref[...] = jnp.where(keep, summed, 0.0).astype(BF)


def on_device(amplitudes, integrals, live_counts):
    occ, nocc, k_all = amplitudes.shape
    shard, slab = integrals.shape
    rows, k_half = occ * nocc, k_all // 2
    xl = lax.axis_index("xl")
    pair = (xl * 8 + lax.axis_index("z")) * 2 + lax.axis_index("c")
    grp = lax.axis_index("y") * 2 + lax.axis_index("xh")

    at = pair * shard + jnp.arange(shard)
    live = (at // VB < live_counts[1]) & (at % VB < live_counts[1])
    w = jnp.where(live[:, None], integrals, 0)
    w_all = lax.all_gather(w, ("z", "c"), axis=0, tiled=True)

    t = amplitudes.reshape(rows, k_all)
    t_own = lax.dynamic_slice(t, (0, xl * k_half), (rows, k_half))
    t_out = lax.dynamic_slice(t, (0, (1 - xl) * k_half), (rows, k_half))
    up = [(i, (i + 1) % 4) for i in range(4)]
    down = [(i, (i - 1) % 4) for i in range(4)]
    t_far = jnp.concatenate(
        [
            lax.ppermute(t_out[: rows // 2], ("xh", "xl"), up),
            lax.ppermute(t_out[rows // 2 :], ("xh", "xl"), down),
        ],
        axis=0,
    )

    out_cols = selector(slab, lambda r: ((r // SLAB) % GRPS) * TILE + (r % SLAB) * SLAB + r // VB)
    in_cols = selector(slab, lambda r: ((r // SLAB) % SLAB) * VB + (r // TILE) * SLAB + r % SLAB)
    out_rows = selector(rows, lambda r: (r // nocc) * nocc + (r % PAIRS) * OCC + (r // PAIRS) % OCC)
    zc = PAIRS // 2
    in_rows = selector(rows, lambda r: (r // (zc * OCC)) * zc * OCC + (r % OCC) * zc + (r // OCC) % zc)

    p_own = mm(t_own, w_all)
    p_far = mm(t_far, w_all)
    fetched = lax.ppermute(p_far, "xl", [(0, 1), (1, 0)])

    params = pltpu.CompilerParams(vmem_limit_bytes=48 * 2**20)
    wire = pl.pallas_call(
        pack_kernel,
        out_shape=jax.ShapeDtypeStruct((GRPS, PAIRS, 2 * OCC * OCC * TILE), F32),
        compiler_params=params,
    )(p_own, p_far, out_rows, out_cols).astype(WIRE)
    got = lax.all_to_all(
        wire.reshape(GRPS * PAIRS, -1), ("y", "xh", "xl", "z", "c"), 0, 0, tiled=True
    )
    whole = pl.BlockSpec(memory_space=pltpu.VMEM)
    small = pl.BlockSpec(memory_space=pltpu.SMEM)
    out = pl.pallas_call(
        unpack_kernel,
        out_shape=jax.ShapeDtypeStruct((rows, slab), BF),
        in_specs=[small, small, whole, whole, whole, whole, whole],
        compiler_params=params,
    )(
        grp.reshape(1),
        live_counts,
        got.reshape(GRPS, 2, zc, -1).astype(F32),
        p_own,
        fetched,
        in_rows,
        in_cols,
    )
    return out.reshape(occ, nocc, slab)


def solution(mesh):
    fine = Mesh(mesh.devices.reshape(4, 2, 2, 8, 2), ("y", "xh", "xl", "z", "c"))
    pair, grp = ("xl", "z", "c"), ("y", "xh")
    return jax.shard_map(
        on_device,
        mesh=fine,
        in_specs=(P(pair, None, None), P(pair, grp), P()),
        out_specs=P(pair, None, grp),
        check_vma=False,
    )
```

time: 357 us -> 194 us (0.54)
  local copies, waits for them, and re-layouts: 167 us -> 21.8 us
  waiting for transfers between devices: 128 us -> 97.1 us
  Pallas kernels: 0 us -> 13.7 us
  other arithmetic: 9.09 us -> 16.9 us
  starting transfers between devices: 19.6 us -> 15.6 us
    mul x3 -> x0, local copies, waits for them, and re-layouts: 106 us -> none  [on_device(): summed = direct + mirrored.astype(jnp.float32) * (1 / SCALE)]
    ppermute x4 -> x3, waiting for transfers between devices: 76.1 us -> 0.01 us  [the longest x1 0.01 us: on_device(): lax.ppermute(t_out[rows // 2:], ('xh', 'xl'), down)]
    all_gather x2 -> x1, waiting for transfers between devices: 26.5 us -> 59 us  [on_device(): w_all = lax.all_gather(w, ('z', 'c'), axis=0, tiled=True)]
    another operation x4 -> x0, local copies, waits for them, and re-layouts: 26.3 us -> none  [on_device(): jnp.stack([jnp.where(xl == 0, mine, other), jnp.where(xl == 0, other, min...]
    all_to_all x3 -> x2, local copies, waits for them, and re-layouts: 17.7 us -> 2.71 us  [on_device(): lax.all_to_all(wire.reshape(GRPS * PAIRS, -1), ('y', 'xh', 'xl', 'z', 'c'...]
    pallas_call x0 -> x2, Pallas kernels: none -> 13.7 us  [the longest x1 7.1 us: on_device(): pl.pallas_call(pack_kernel, out_shape=jax.ShapeDtypeStruct((GRPS, PAIRS,...]
    all_to_all x1, waiting for transfers between devices: 24.8 us -> 38 us  [on_device(): lax.all_to_all(wire.reshape(GRPS * PAIRS, -1), ('y', 'xh', 'xl', 'z', 'c'...]
    unnamed x19 -> x14, local copies, waits for them, and re-layouts: 4.38 us -> 14.5 us
  transfers between devices with their start and end apart: 7 -> 5, of which waited for: 5 -> 2; matrix products, arithmetic and copies ran while one was open for 3% -> 16% of each run, Pallas kernels for 0% -> 0%
where the time goes in v2:
time: 194 us; the launch traced here: 193 us
  waiting for transfers between devices  97.1 us (50%)
  local copies, waits for them, and re-layouts  21.8 us (11%)
  other arithmetic  16.9 us (9%)
  starting transfers between devices  15.6 us (8%)
  matrix products  14.5 us (7%)
  Pallas kernels  13.7 us (7%)
  between operations  13.6 us (7%)
    all_gather x1, waiting for transfers between devices, on_device(): w_all = lax.all_gather(w, ('z', 'c'), axis=0, tiled=True)  59 us
    all_to_all x1, waiting for transfers between devices, on_device(): lax.all_to_all(wire.reshape(GRPS * PAIRS, -1), ('y', 'xh', 'xl', 'z', 'c'...  38 us
    dot_general x2, matrix products, mm(): return jnp.dot(x, y, preferred_element_type=F32)  14.5 us
    unnamed x14, local copies, waits for them, and re-layouts  14.5 us
    all_to_all x1, starting transfers between devices, on_device(): lax.all_to_all(wire.reshape(GRPS * PAIRS, -1), ('y', 'xh', 'xl', 'z', 'c'...  10.9 us
    pallas_call x1, Pallas kernels, on_device(): pl.pallas_call(pack_kernel, out_shape=jax.ShapeDtypeStruct((GRPS, PAIRS,...  7.1 us
    pallas_call x1, Pallas kernels, on_device(): pl.pallas_call(unpack_kernel, out_shape=jax.ShapeDtypeStruct((rows, slab)...  6.6 us
    convert_element_type x3, other arithmetic, selector(): (wanted == lax.broadcasted_iota(jnp.int32, (size, size), 1)).astype(BF)  5.45 us
  transfers between devices with their start and end apart: 5, of which 2 were waited for; matrix products, arithmetic and copies ran while one was open for 16% of the time, Pallas kernels for 0%

profile of v2, /device:TPU:1, one launch (start us, length us, event | category | flops | bytes accessed | tf_op | source)
XLA Modules:
  0.0 193.2 jit_solution(4171978769314508496)
XLA Ops:
  6.5 1.2 slice.10
  7.8 0.7 fusion.57
  8.4 2.1 %broadcast_select_fusion = bf16[288,1152]{1,0:T(8,128)(2,1)} fusion(bf16[288,1152]{1,0:T(8,128)(2,1)} %param.4, pred[288]{0:T(512)(128)(4,1)S(1)} %fusion.57), kind=kLoop, calls=%fused_computation.35 | loop fusion | flops 331776 | bytes 1327392 | tf_op jit(solution)/shard_map/jit(_where)/select_n | solution.py:92
  10.5 3.4 %constant_dynamic-slice_fusion = (bf16[144,4608]{1,0:T(8,128)(2,1)}, bf16[144,4608]{1,0:T(8,128)(2,1)}) fusion(bf16[288,9216]{1,0:T(8,128)(2,1)} %bitcast.11, s32[]{:T(128)S(6)} %select_n.98, s32[]{:T(128)S(6)} %add.140), kind=kLoop, calls=%fused_computation.107 | loop fusion | bytes 5308424 | tf_op jit(solution)/shard_map/slice | solution.py:102
  13.9 2.0 %collective-permute-start = (bf16[144,4608]{1,0:T(8,128)(2,1)}, bf16[144,4608]{1,0:T(8,128)(2,1)}, u32[]{:S(2)}, u32[]{:S(2)}) collective-permute-start(bf16[144,4608]{1,0:T(8,128)(2,1)} %get-tuple-element.5), channel_id=1, source_target_pairs={{0,16},{16,32},{32,48},{48,0},{1,17},{17,33},{33,49},{49,1},{2,18}... | collective-permute-start | bytes 3981320 | tf_op jit(solution)/shard_map/ppermute | solution.py:102
  16.0 1.3 collective-permute-start.1
  17.4 4.4 %fusion.12 = (bf16[1152,1152]{1,0:T(8,128)(2,1)S(1)}, bf16[1152,1152]{1,0:T(8,128)(2,1)}) fusion(s32[1152]{0:T(1024)S(1)} %get-tuple-element.20, s32[1152]{0:T(1024)S(1)} %get-tuple-element.22, s32[1152]{0:T(1024)S(1)} %get-tuple-element.19, s32[1152]{0:T(1024)S(1)} %get-tuple-element.21, s32[1152]{0:T(1024)S(1)} %get-tuple-element.18, ...), kind=kLoop, calls=%fused_computation.20 | loop fusion | flops 43794432 | bytes 5349888 | tf_op jit(solution)/shard_map/convert_element_type | solution.py:33
  21.8 0.5 fusion.28.row_ref
  22.3 59.0 %all-gather.2.cloned.1.call-done = bf16[4608,1152]{1,0:T(8,128)(2,1)} async-done(((bf16[288,1152]{1,0:T(8,128)(2,1)}), bf16[4608,1152]{1,0:T(8,128)(2,1)}) %all-gather.2.cloned.1.call-update) | async-done | bytes 10616848 | tf_op jit(solution)/shard_map/all_gather | solution.py:93
  81.3 8.5 %fusion.19.own_ref = f32[288,1152]{1,0:T(8,128)S(1)} fusion(bf16[4608,1152]{1,0:T(8,128)(2,1)} %all-gather.2.cloned.1.call-done, bf16[288,9216]{1,0:T(8,128)(2,1)} %bitcast.12, s32[]{:T(128)S(6)} %select_n.94), kind=kOutput, calls=%fused_computation.27 | convolution fusion | flops 3057647616 | bytes 14598148 | tf_op jit(solution)/shard_map/dot_general | solution.py:23
  89.9 5.9 %fusion.15.far_ref = f32[288,1152]{1,0:T(8,128)S(1)} fusion(bf16[4608,1152]{1,0:T(8,128)(2,1)S(1)} %copy-done.5, bf16[144,4608]{1,0:T(8,128)(2,1)} %collective-permute-done.1, bf16[144,4608]{1,0:T(8,128)(2,1)} %collective-permute-done), kind=kOutput, calls=%fused_computation.23 | convolution fusion | flops 3062956032 | bytes 14598144 | tf_op jit(solution)/shard_map/dot_general | solution.py:23
  95.9 7.1 %shard_map.37 = f32[8,32,2592]{2,1,0:T(8,128)} custom-call(f32[288,1152]{1,0:T(8,128)S(1)} %fusion.19.own_ref, f32[288,1152]{1,0:T(8,128)S(1)} %fusion.15.far_ref, bf16[288,288]{1,0:T(8,128)(2,1)S(1)} %fusion.28.row_ref, bf16[1152,1152]{1,0:T(8,128)(2,1)S(1)} %copy-done), custom_call_target="tpu_custom_call" | custom-call | tf_op jit(solution)/shard_map/pallas_call | solution.py:119
  103.0 3.0 %convert_element_type.24 = f16[8,32,2592]{2,1,0:T(8,128)(2,1)} convert(f32[8,32,2592]{2,1,0:T(8,128)} %shard_map.37) | non-fusion elementwise | flops 663552 | bytes 3981312 | tf_op jit(solution)/shard_map/convert_element_type | solution.py:123
  106.0 0.5 broadcast.219
  106.5 3.9 %reduce = f16[256,2592]{1,0:T(8,128)(2,1)} reduce(f16[256,1,2592]{2,0,1:T(8,128)(2,1)} %bitcast.9, f16[]{:T(256)} %broadcast.219), dimensions={1}, to_apply=%copy.5.reduce_sub_computation | reduce | bytes 2654210 | tf_op jit(solution)/shard_map/all_to_all | solution.py:124
  110.3 4.5 %reshape.40 = f16[256,2,1296]{2,1,0:T(2,128)(2,1)} reshape(f16[256,2592]{1,0:T(8,128)(2,1)} %reduce) | data formatting | bytes 2654208
  114.9 10.9 %all-to-all-start = ((f16[256,2,1296]{2,1,0:T(2,128)(2,1)}), f16[256,2,1296]{2,1,0:T(2,128)(2,1)}, u32[]{:S(2)}, u32[]{:S(2)}) async-start(f16[256,2,1296]{2,1,0:T(2,128)(2,1)} %reshape.40), calls=%async_computation | async-start | bytes 2883584 | tf_op jit(solution)/shard_map/all_to_all | solution.py:124
  125.7 1.5 collective-permute-start.2
  127.3 0.6 fusion.30.row_ref
  127.8 38.0 %all-to-all-done = f16[256,2,1296]{2,1,0:T(2,128)(2,1)} async-done(((f16[256,2,1296]{2,1,0:T(2,128)(2,1)}), f16[256,2,1296]{2,1,0:T(2,128)(2,1)}, u32[]{:S(2)}, u32[]{:S(2)}) %all-to-all-start) | async-done | bytes 1327136 | tf_op jit(solution)/shard_map/all_to_all | solution.py:124
  165.9 9.9 %reshape.41 = f16[256,1,2592]{2,1,0:T(2,128)(2,1)} reshape(f16[256,2,1296]{2,1,0:T(2,128)(2,1)} %all-to-all-done) | data formatting | bytes 2654208
  175.8 2.2 %copy.6 = f16[256,1,2592]{2,0,1:T(8,128)(2,1)S(1)} copy(f16[256,1,2592]{2,1,0:T(2,128)(2,1)} %reshape.41) | data formatting | bytes 2654208 | tf_op jit(solution)/shard_map/all_to_all | solution.py:124
  178.0 1.8 convert.1.got_ref
  179.7 6.6 %shard_map.38 = bf16[288,1152]{1,0:T(8,128)(2,1)} custom-call(s32[1]{0:T(128)} %bitcast.grp_ref, s32[2]{0:T(128)S(1)} %copy-done.4, f32[8,2,16,2592]{3,2,1,0:T(8,128)} %convert.1.got_ref, f32[288,1152]{1,0:T(8,128)S(1)} %copy-done.2, f32[288,1152]{1,0:T(8,128)} %collective-permute-done.2.sum_ref, bf16[288,288]{1,0:T(8,128)(2,1)S(1)} %fusion.30.row_ref, ...), custom_call_target="tpu_custom_call" | custom-call | tf_op jit(solution)/shard_map/pallas_call | solution.py:129
  (33 shorter events, 0.2 us)
Async XLA Ops:
  6.5 74.8 %all-gather.2.cloned.1.call-start = ((), (), s32[]{:S(2)}) async-start(), calls=%async_computation.1 | async-start | bytes 11280384 | tf_op jit(solution)/shard_map/all_gather | solution.py:93
  13.9 76.0 %collective-permute-start = (bf16[144,4608]{1,0:T(8,128)(2,1)}, bf16[144,4608]{1,0:T(8,128)(2,1)}, u32[]{:S(2)}, u32[]{:S(2)}) collective-permute-start(bf16[144,4608]{1,0:T(8,128)(2,1)} %get-tuple-element.5), channel_id=1, source_target_pairs={{0,16},{16,32},{32,48},{48,0},{1,17},{17,33},{33,49},{49,1},{2,18}... | collective-permute-start | bytes 3981320 | tf_op jit(solution)/shard_map/ppermute | solution.py:102
  16.0 73.9 %collective-permute-start.1 = (bf16[144,4608]{1,0:T(8,128)(2,1)}, bf16[144,4608]{1,0:T(8,128)(2,1)}, u32[]{:S(2)}, u32[]{:S(2)}) collective-permute-start(bf16[144,4608]{1,0:T(8,128)(2,1)} %get-tuple-element.6), channel_id=1, source_target_pairs={{0,48},{16,0},{32,16},{48,32},{1,49},{17,1},{33,17},{49,33},{2,50}... | collective-permute-start | bytes 3981320 | tf_op jit(solution)/shard_map/ppermute | solution.py:103
  81.3 8.6 %copy-start.5 = (bf16[4608,1152]{1,0:T(8,128)(2,1)S(1)}, bf16[4608,1152]{1,0:T(8,128)(2,1)}, u32[]{:S(2)}) copy-start(bf16[4608,1152]{1,0:T(8,128)(2,1)} %all-gather.2.cloned.1.call-done) | copy-start | bytes 31850500
  89.9 6.0 %copy-start.1 = (f32[288,1152]{1,0:T(8,128)}, f32[288,1152]{1,0:T(8,128)S(1)}, u32[]{:S(2)}) copy-start(f32[288,1152]{1,0:T(8,128)S(1)} %fusion.19.own_ref) | copy-start | bytes 3981316
  89.9 6.0 %copy-start = (bf16[1152,1152]{1,0:T(8,128)(2,1)S(1)}, bf16[1152,1152]{1,0:T(8,128)(2,1)}, u32[]{:S(2)}) copy-start(bf16[1152,1152]{1,0:T(8,128)(2,1)} %get-tuple-element.8.col_ref) | copy-start | bytes 7962628
  95.8 10.1 %copy-start.3 = (f32[288,1152]{1,0:T(8,128)}, f32[288,1152]{1,0:T(8,128)S(1)}, u32[]{:S(2)}) copy-start(f32[288,1152]{1,0:T(8,128)S(1)} %fusion.15.far_ref) | copy-start | bytes 3981316
  114.9 51.0 %all-to-all-start = ((f16[256,2,1296]{2,1,0:T(2,128)(2,1)}), f16[256,2,1296]{2,1,0:T(2,128)(2,1)}, u32[]{:S(2)}, u32[]{:S(2)}) async-start(f16[256,2,1296]{2,1,0:T(2,128)(2,1)} %reshape.40), calls=%async_computation | async-start | bytes 2883584 | tf_op jit(solution)/shard_map/all_to_all | solution.py:124
  125.7 54.0 %collective-permute-start.2 = (f32[288,1152]{1,0:T(8,128)}, f32[288,1152]{1,0:T(8,128)}, u32[]{:S(2)}, u32[]{:S(2)}) collective-permute-start(f32[288,1152]{1,0:T(8,128)} %copy-done.3), channel_id=1, source_target_pairs={{0,16},{16,0},{1,17},{17,1},{2,18},{18,2},{3,19},{19,3},{4,20},{20... | collective-permute-start | bytes 3981320 | tf_op jit(solution)/shard_map/ppermute | solution.py:116
  127.8 51.9 %copy-start.4 = (s32[2]{0:T(128)S(1)}, s32[2]{0:T(128)}, u32[]{:S(2)}) copy-start(s32[2]{0:T(128)} %live_ref.1) | copy-start | bytes 28
  175.8 4.0 %copy-start.2 = (f32[288,1152]{1,0:T(8,128)S(1)}, f32[288,1152]{1,0:T(8,128)}, u32[]{:S(2)}) copy-start(f32[288,1152]{1,0:T(8,128)} %copy-done.1) | copy-start | bytes 3981316
Sparse Core Ops, SparseCore 0:
  10.7 70.6 all-gather.1

commit v3 on v2

v3 whole, which is shorter than its diff:
```python
import jax
import jax.numpy as jnp
from jax import lax
from jax.experimental import pallas as pl
from jax.experimental.pallas import tpu as pltpu
from jax.sharding import Mesh
from jax.sharding import PartitionSpec as P

VB = 96
OCC = 3
GRPS = 8
PAIRS = 32
SLAB = VB // GRPS
PIECE = SLAB // 4 * SLAB
LANES = 384
WIRE = jnp.float16
SCALE = 16.0
BF, F32 = jnp.bfloat16, jnp.float32
ORDER = ("y", "xh", "xl", "c", "z")


def mm(x, y):
    return jnp.dot(x, y, preferred_element_type=F32)


def halves(x):
    hi = x.astype(BF)
    return hi, (x - hi.astype(F32)).astype(BF)


def selector(size, source):
    wanted = source(lax.broadcasted_iota(jnp.int32, (size, size), 0))
    return (wanted == lax.broadcasted_iota(jnp.int32, (size, size), 1)).astype(BF)


def pack_kernel(parts_ref, row_ref, col_ref, out_ref, turned_ref):
    rows = row_ref.shape[0]
    for o in range(4):
        total = 0.0
        for part in halves(parts_ref[o * rows : (o + 1) * rows] * SCALE):
            total += mm(mm(row_ref[...], part).astype(BF), col_ref[...])
        turned_ref[o] = total
    fill = jnp.zeros((PAIRS, LANES - OCC * OCC * PIECE), F32)
    for g in range(GRPS):
        planes = []
        for o in range(4):
            for a in range(2):
                at = (g * 2 + a) * PIECE
                cut = [
                    turned_ref[o, q * PAIRS : (q + 1) * PAIRS, at : at + PIECE]
                    for q in range(OCC * OCC)
                ]
                planes.append(jnp.concatenate([*cut, fill], axis=1))
        message = jnp.swapaxes(jnp.stack(planes, axis=0), 0, 1)
        out_ref[g * PAIRS : (g + 1) * PAIRS] = message


def unpack_kernel(
    place_ref, live_ref, got_ref, own_ref, near_ref, side_ref, row_ref, col_ref, out_ref, v_ref, s_ref
):
    for g in range(GRPS):
        message = got_ref[g * PAIRS : (g + 1) * PAIRS]
        v_ref[g] = jnp.swapaxes(message, 0, 1)
    for xl in range(2):
        for c in range(2):
            for g in range(GRPS):
                for cs in range(2):
                    for a in range(2):
                        oc = (c ^ cs) * 2 + a
                        near, far = (xl * 2 + cs) * 8, ((1 - xl) * 2 + cs) * 8
                        s_ref[xl * 2 + c, (g * 2 + cs) * 2 + a] = (
                            v_ref[g, oc, near : near + 8] + v_ref[g, 4 + oc, far : far + 8]
                        )
    blocks = []
    for j in range(OCC):
        for xc in range(4):
            for i in range(OCC):
                at = (i * OCC + j) * PIECE
                blocks.append(
                    jnp.concatenate(
                        [s_ref[xc, n, :, at : at + PIECE] for n in range(4 * GRPS)], axis=1
                    )
                )
    stacked = jnp.concatenate(blocks, axis=0)
    total = 0.0
    for part in halves(stacked):
        total += mm(mm(row_ref[...], part).astype(BF), col_ref[...])
    mine = own_ref[...] + near_ref[...]
    side = side_ref[...]
    first_core = place_ref[1] == 0
    direct = jnp.concatenate(
        [jnp.where(first_core, mine, side), jnp.where(first_core, side, mine)], axis=1
    )
    summed = direct + total * (1 / SCALE)
    col = lax.broadcasted_iota(jnp.int32, summed.shape, 1)
    first = place_ref[0] * SLAB + col // VB
    keep = (first < live_ref[0]) & (col % VB < live_ref[0])
    out_ref[...] = jnp.where(keep, summed, 0.0).astype(BF)


def gather(block):
    return lax.all_gather(block, "z", axis=0, tiled=True)


def on_device(amplitudes, integrals, live_counts):
    occ, nocc, k_all = amplitudes.shape
    shard, slab = integrals.shape
    rows, k_half, half = occ * nocc, k_all // 2, slab // 2
    xl, c = lax.axis_index("xl"), lax.axis_index("c")
    pair = (xl * 8 + lax.axis_index("z")) * 2 + c
    grp = lax.axis_index("y") * 2 + lax.axis_index("xh")
    swap = [(0, 1), (1, 0)]

    at = pair * shard + jnp.arange(shard)
    live = (at // VB < live_counts[1]) & (at % VB < live_counts[1])
    w = jnp.where(live[:, None], integrals, 0)
    w_keep = jnp.where(c == 0, w[:, :half], w[:, half:])
    w_send = jnp.where(c == 0, w[:, half:], w[:, :half])
    w_recv = lax.ppermute(w_send, "c", swap)
    block = jnp.where(
        c == 0,
        jnp.concatenate([w_keep, w_recv], axis=0),
        jnp.concatenate([w_recv, w_keep], axis=0),
    )
    w_all = gather(block)

    t = amplitudes.reshape(rows, k_all)
    t_own = lax.dynamic_slice(t, (0, xl * k_half), (rows, k_half))
    t_out = lax.dynamic_slice(t, (0, (1 - xl) * k_half), (rows, k_half))
    up = [(i, (i + 1) % 4) for i in range(4)]
    down = [(i, (i - 1) % 4) for i in range(4)]
    t_far = jnp.concatenate(
        [
            lax.ppermute(t_out[: rows // 2], ("xh", "xl"), up),
            lax.ppermute(t_out[rows // 2 :], ("xh", "xl"), down),
        ],
        axis=0,
    )
    near = jnp.concatenate([t_own, lax.ppermute(t_own, "c", swap)], axis=0)
    far = jnp.concatenate([t_far, lax.ppermute(t_far, "c", swap)], axis=0)

    zs = PAIRS // 4
    out_cols = selector(half, lambda r: ((r // SLAB) % GRPS) * (half // GRPS) + r // VB * SLAB + r % SLAB)
    in_cols = selector(slab, lambda r: (r % SLAB) * VB + r // SLAB)
    out_rows = selector(
        rows,
        lambda r: r // nocc * nocc
        + (r % PAIRS // 16) * 48
        + (r % zs) * 6
        + (r // zs % 2) * 3
        + r // PAIRS % OCC,
    )
    in_rows = selector(rows, lambda r: r // 48 * 48 + (r // 3 % 2) * 24 + (r % 3) * 8 + r // 6 % zs)

    p_near = mm(near, w_all)
    p_far = mm(far, w_all)
    fetched = lax.ppermute(p_far, "xl", swap)
    side = lax.ppermute(p_near[rows:] + fetched[rows:], "c", swap)

    params = pltpu.CompilerParams(vmem_limit_bytes=48 * 2**20)
    wire = pl.pallas_call(
        pack_kernel,
        out_shape=jax.ShapeDtypeStruct((GRPS * PAIRS, 8, LANES), F32),
        scratch_shapes=[pltpu.VMEM((4, rows, half), F32)],
        compiler_params=params,
    )(jnp.concatenate([p_near, p_far], axis=0), out_rows, out_cols).astype(WIRE)
    got = lax.all_to_all(wire, ORDER, 0, 0, tiled=True)
    whole = pl.BlockSpec(memory_space=pltpu.VMEM)
    small = pl.BlockSpec(memory_space=pltpu.SMEM)
    out = pl.pallas_call(
        unpack_kernel,
        out_shape=jax.ShapeDtypeStruct((rows, slab), BF),
        in_specs=[small, small] + [whole] * 6,
        scratch_shapes=[
            pltpu.VMEM((GRPS, 8, PAIRS, LANES), F32),
            pltpu.VMEM((4, 4 * GRPS, 8, LANES), F32),
        ],
        compiler_params=params,
    )(
        jnp.stack([grp, c]),
        live_counts,
        got.astype(F32),
        p_near[:rows],
        fetched[:rows],
        side,
        in_rows,
        in_cols,
    )
    return out.reshape(occ, nocc, slab)


def solution(mesh):
    fine = Mesh(mesh.devices.reshape(4, 2, 2, 8, 2), ("y", "xh", "xl", "z", "c"))
    pair, grp = ("xl", "z", "c"), ("y", "xh")
    return jax.shard_map(
        on_device,
        mesh=fine,
        in_specs=(P(pair, None, None), P(pair, grp), P()),
        out_specs=P(pair, None, grp),
        check_vma=False,
    )
```

time: 194 us -> 200 us (1.031)
  local copies, waits for them, and re-layouts: 21.8 us -> 8.22 us
  waiting for transfers between devices: 97.1 us -> 104 us
  starting transfers between devices: 15.6 us -> 20.7 us
  other arithmetic: 16.9 us -> 21.9 us
    ppermute x1 -> x5, waiting for transfers between devices: 0.01 us -> 46.3 us  [the longest x1 45 us: on_device(): fetched = lax.ppermute(p_far, 'xl', swap)]
    all_to_all x1, waiting for transfers between devices: 38 us -> 0.01 us  [on_device(): got = lax.all_to_all(wire, ORDER, 0, 0, tiled=True)]
    all_gather x1, waiting for transfers between devices: 59 us -> 27.2 us  [gather(): return lax.all_gather(block, 'z', axis=0, tiled=True)]
    ppermute x1, waiting for transfers between devices: 0.01 us -> 29.2 us  [on_device(): lax.ppermute(t_out[rows // 2:], ('xh', 'xl'), down)]
    unnamed x14 -> x10, local copies, waits for them, and re-layouts: 14.5 us -> 0.02 us
    ppermute x1 -> x5, starting transfers between devices: 1.47 us -> 7.94 us  [the longest x1 3.33 us: on_device(): w_recv = lax.ppermute(w_send, 'c', swap)]
    all_to_all x1 -> x0, other arithmetic: 3.85 us -> none  [on_device(): lax.all_to_all(wire.reshape(GRPS * PAIRS, -1), ('y', 'xh', 'xl', 'z', 'c'...]
    concatenate x0 -> x2, other arithmetic: none -> 3.59 us  [the longest x1 2.1 us: on_device(): jnp.concatenate([p_near, p_far], axis=0)]
  transfers between devices with their start and end apart: 5 -> 9, of which waited for: 2 -> 5; matrix products, arithmetic and copies ran while one was open for 16% -> 15% of each run, Pallas kernels for 0% -> 0%
where the time goes in v3:
time: 200 us; the launch traced here: 199 us
  waiting for transfers between devices  104 us (52%)
  other arithmetic  21.9 us (11%)
  starting transfers between devices  20.7 us (10%)
  matrix products  16.3 us (8%)
  Pallas kernels  14 us (7%)
  between operations  13.6 us (7%)
  local copies, waits for them, and re-layouts  8.22 us (4%)
    ppermute x1, waiting for transfers between devices, on_device(): fetched = lax.ppermute(p_far, 'xl', swap)  45 us
    ppermute x1, waiting for transfers between devices, on_device(): lax.ppermute(t_out[rows // 2:], ('xh', 'xl'), down)  29.2 us
    all_gather x1, waiting for transfers between devices, gather(): return lax.all_gather(block, 'z', axis=0, tiled=True)  27.2 us
    dot_general x2, matrix products, mm(): return jnp.dot(x, y, preferred_element_type=F32)  16.3 us
    all_to_all x1, starting transfers between devices, on_device(): got = lax.all_to_all(wire, ORDER, 0, 0, tiled=True)  11.3 us
    pallas_call x1, Pallas kernels, on_device(): pl.pallas_call(pack_kernel, out_shape=jax.ShapeDtypeStruct((GRPS * PAIRS,...  7.02 us
    pallas_call x1, Pallas kernels, on_device(): pl.pallas_call(unpack_kernel, out_shape=jax.ShapeDtypeStruct((rows, slab)...  6.99 us
    convert_element_type x4, other arithmetic, selector(): (wanted == lax.broadcasted_iota(jnp.int32, (size, size), 1)).astype(BF)  5.45 us
  transfers between devices with their start and end apart: 9, of which 5 were waited for; matrix products, arithmetic and copies ran while one was open for 15% of the time, Pallas kernels for 0%

profile of v3, /device:TPU:1, one launch (start us, length us, event | category | flops | bytes accessed | tf_op | source)
XLA Modules:
  0.0 199.1 jit_solution(17755274151768696192)
XLA Ops:
  6.5 1.2 slice.30
  9.8 3.3 %collective-permute-start.1 = (bf16[288,576]{1,0:T(8,128)(2,1)S(1)}, bf16[288,576]{1,0:T(8,128)(2,1)S(1)}, u32[]{:S(2)}, u32[]{:S(2)}) collective-permute-start(bf16[288,576]{1,0:T(8,128)(2,1)S(1)} %get-tuple-element.11), channel_id=1, source_target_pairs={{0,1},{1,0},{2,3},{3,2},{4,5},{5,4},{6,7},{7,6},{8,9},{9,8},{10,11... | collective-permute-start | bytes 995336 | tf_op jit(solution)/shard_map/ppermute | solution.py:119
  13.2 1.3 collective-permute-done.1
  15.7 3.5 %constant_dynamic-slice_fusion = (bf16[144,4608]{1,0:T(8,128)(2,1)}, bf16[144,4608]{1,0:T(8,128)(2,1)}) fusion(bf16[288,9216]{1,0:T(8,128)(2,1)} %bitcast.7, s32[]{:T(128)S(6)} %select_n.141, s32[]{:T(128)S(6)} %add.173), kind=kLoop, calls=%fused_computation.158 | loop fusion | bytes 5308424 | tf_op jit(solution)/shard_map/slice | solution.py:134
  20.6 29.2 %collective-permute-done.3 = bf16[144,4608]{1,0:T(8,128)(2,1)S(1)} collective-permute-done((bf16[144,4608]{1,0:T(8,128)(2,1)}, bf16[144,4608]{1,0:T(8,128)(2,1)S(1)}, u32[]{:S(2)}, u32[]{:S(2)}) %collective-permute-start.3) | collective-permute-done | bytes 1327136 | tf_op jit(solution)/shard_map/ppermute | solution.py:135
  49.8 1.6 collective-permute-done.2
  51.4 1.5 pad_maximum_fusion.1
  52.9 1.6 collective-permute-start.4
  54.6 3.5 %constant_dynamic-slice_fusion.1 = bf16[288,4608]{1,0:T(8,128)(2,1)} fusion(bf16[288,9216]{1,0:T(8,128)(2,1)} %bitcast.8, s32[]{:T(128)S(6)} %select_n.132), kind=kLoop, calls=%fused_computation.159 | loop fusion | bytes 5308420 | tf_op jit(solution)/shard_map/dynamic_slice | solution.py:128
  60.3 27.2 %all-gather.2.cloned.1.call-done = bf16[4608,576]{1,0:T(8,128)(2,1)} async-done(((bf16[576,576]{1,0:T(8,128)(2,1)}), bf16[4608,576]{1,0:T(8,128)(2,1)}) %all-gather.2.cloned.1.call-update) | async-done | bytes 5308432 | tf_op jit(solution)/shard_map/all_gather | solution.py:102
  87.6 9.4 %fusion.4 = f32[576,576]{1,0:T(8,128)} fusion(bf16[4608,576]{1,0:T(8,128)(2,1)} %all-gather.2.cloned.1.call-done, bf16[288,4608]{1,0:T(8,128)(2,1)} %collective-permute-done.4, bf16[144,4608]{1,0:T(8,128)(2,1)S(1)} %collective-permute-done.3, bf16[144,4608]{1,0:T(8,128)(2,1)} %collective-permute-done.2), kind=kOutput, calls=%fused_computation.4 | convolution fusion | flops 3073572864 | bytes 11943936 | tf_op jit(solution)/shard_map/dot_general | solution.py:23
  97.0 6.9 %fusion = f32[576,576]{1,0:T(8,128)S(1)} fusion(bf16[4608,576]{1,0:T(8,128)(2,1)S(1)} %copy-done.4, bf16[288,4608]{1,0:T(8,128)(2,1)} %collective-permute-done, bf16[288,4608]{1,0:T(8,128)(2,1)} %constant_dynamic-slice_fusion.1), kind=kOutput, calls=%fused_computation | convolution fusion | flops 3068264448 | bytes 11943936 | tf_op jit(solution)/shard_map/dot_general | solution.py:23
  103.9 2.1 %pad_maximum_fusion.parts_ref = f32[1152,576]{1,0:T(8,128)S(1)} fusion(f32[576,576]{1,0:T(8,128)} %fusion.4, f32[576,576]{1,0:T(8,128)S(1)} %fusion), kind=kLoop, calls=%fused_computation.12 | loop fusion | flops 663552 | bytes 5308416 | tf_op jit(solution)/shard_map/concatenate | solution.py:166
  106.0 7.0 %shard_map.37 = f32[256,8,384]{2,1,0:T(8,128)} custom-call(f32[1152,576]{1,0:T(8,128)S(1)} %pad_maximum_fusion.parts_ref, bf16[288,288]{1,0:T(8,128)(2,1)S(1)} %fusion.41.row_ref, bf16[576,576]{1,0:T(8,128)(2,1)S(1)} %fusion.16.col_ref), custom_call_target="tpu_custom_call" | custom-call | tf_op jit(solution)/shard_map/pallas_call | solution.py:161
  113.0 3.3 %convert_element_type.22 = f16[256,8,384]{2,1,0:T(8,128)(2,1)} convert(f32[256,8,384]{2,1,0:T(8,128)} %shard_map.37) | non-fusion elementwise | flops 786432 | bytes 4718592 | tf_op jit(solution)/shard_map/convert_element_type | solution.py:166
  116.4 11.3 %all-to-all-start = ((f16[256,8,384]{2,1,0:T(8,128)(2,1)}), f16[256,8,384]{2,1,0:T(8,128)(2,1)}, u32[]{:S(2)}, u32[]{:S(2)}) async-start(f16[256,8,384]{2,1,0:T(8,128)(2,1)} %convert_element_type.22), calls=%async_computation | async-start | bytes 3145728 | tf_op jit(solution)/shard_map/all_to_all | solution.py:167
  127.8 1.5 collective-permute-start.5
  129.3 1.6 fusion.10.col_ref
  130.9 45.0 %collective-permute-done.5 = f32[576,576]{1,0:T(8,128)S(1)} collective-permute-done((f32[576,576]{1,0:T(8,128)}, f32[576,576]{1,0:T(8,128)S(1)}, u32[]{:S(2)}, u32[]{:S(2)}) %collective-permute-start.5) | collective-permute-done | bytes 1327136 | tf_op jit(solution)/shard_map/ppermute | solution.py:157
  175.9 2.7 %slice_add_fusion = (f32[288,576]{1,0:T(8,128)}, f32[288,576]{1,0:T(8,128)S(1)}, f32[288,576]{1,0:T(8,128)}) fusion(f32[576,576]{1,0:T(8,128)S(1)} %collective-permute-done.5, f32[576,576]{1,0:T(8,128)} %copy-done.3), kind=kLoop, calls=%fused_computation.38 | loop fusion | flops 165888 | bytes 4644864 | tf_op jit(solution)/shard_map/add | solution.py:158
  178.6 1.4 collective-permute-start.6
  180.1 1.8 fusion.40.row_ref
  181.9 3.3 %convert_element_type.23.got_ref = f32[256,8,384]{2,1,0:T(8,128)} convert(f16[256,8,384]{2,1,0:T(8,128)(2,1)} %all-to-all-done) | non-fusion elementwise | flops 786432 | bytes 4718592 | tf_op jit(solution)/shard_map/convert_element_type | solution.py:182
  185.2 7.0 %shard_map.38 = bf16[288,1152]{1,0:T(8,128)(2,1)} custom-call(s32[2]{0:T(128)S(1)} %pad_add_fusion.place_ref, s32[2]{0:T(128)S(1)} %copy-done.2, f32[256,8,384]{2,1,0:T(8,128)} %convert_element_type.23.got_ref, f32[288,576]{1,0:T(8,128)S(1)} %get-tuple-element.8.own_ref, f32[288,576]{1,0:T(8,128)S(1)} %copy-done, ...), custom_call_target="tpu_custom_call" | custom-call | tf_op jit(solution)/shard_map/pallas_call | solution.py:170
  (48 shorter events, 7.1 us)
Async XLA Ops:
  6.5 81.0 %all-gather.2.cloned.1.call-start = ((), (), s32[]{:S(2)}) async-start(), calls=%async_computation.1 | async-start | bytes 6635520 | tf_op jit(solution)/shard_map/all_gather | solution.py:102
  9.8 4.6 %collective-permute-start.1 = (bf16[288,576]{1,0:T(8,128)(2,1)S(1)}, bf16[288,576]{1,0:T(8,128)(2,1)S(1)}, u32[]{:S(2)}, u32[]{:S(2)}) collective-permute-start(bf16[288,576]{1,0:T(8,128)(2,1)S(1)} %get-tuple-element.11), channel_id=1, source_target_pairs={{0,1},{1,0},{2,3},{3,2},{4,5},{5,4},{6,7},{7,6},{8,9},{9,8},{10,11... | collective-permute-start | bytes 995336 | tf_op jit(solution)/shard_map/ppermute | solution.py:119
  19.1 30.7 %collective-permute-start.3 = (bf16[144,4608]{1,0:T(8,128)(2,1)}, bf16[144,4608]{1,0:T(8,128)(2,1)S(1)}, u32[]{:S(2)}, u32[]{:S(2)}) collective-permute-start(bf16[144,4608]{1,0:T(8,128)(2,1)} %get-tuple-element.6), channel_id=1, source_target_pairs={{0,48},{16,0},{32,16},{48,32},{1,49},{17,1},{33,17},{49,33},{2,50}... | collective-permute-start | bytes 3981320 | tf_op jit(solution)/shard_map/ppermute | solution.py:135
  19.9 31.5 %collective-permute-start.2 = (bf16[144,4608]{1,0:T(8,128)(2,1)}, bf16[144,4608]{1,0:T(8,128)(2,1)}, u32[]{:S(2)}, u32[]{:S(2)}) collective-permute-start(bf16[144,4608]{1,0:T(8,128)(2,1)} %get-tuple-element.5), channel_id=1, source_target_pairs={{0,16},{16,32},{32,48},{48,0},{1,17},{17,33},{33,49},{49,1},{2,18}... | collective-permute-start | bytes 3981320 | tf_op jit(solution)/shard_map/ppermute | solution.py:134
  52.9 7.4 %collective-permute-start.4 = (bf16[288,4608]{1,0:T(8,128)(2,1)S(1)}, bf16[288,4608]{1,0:T(8,128)(2,1)}, u32[]{:S(2)}, u32[]{:S(2)}) collective-permute-start(bf16[288,4608]{1,0:T(8,128)(2,1)S(1)} %pad_maximum_fusion.1), channel_id=1, source_target_pairs={{0,1},{1,0},{2,3},{3,2},{4,5},{5,4},{6,7},{7,6},{8,9},{9,8},{10,11... | collective-permute-start | bytes 7962632 | tf_op jit(solution)/shard_map/ppermute | solution.py:140
  58.1 38.9 %collective-permute-start = (bf16[288,4608]{1,0:T(8,128)(2,1)}, bf16[288,4608]{1,0:T(8,128)(2,1)}, u32[]{:S(2)}, u32[]{:S(2)}) collective-permute-start(bf16[288,4608]{1,0:T(8,128)(2,1)} %constant_dynamic-slice_fusion.1), channel_id=1, source_target_pairs={{0,1},{1,0},{2,3},{3,2},{4,5},{5,4},{6,7},{7,6},{8,9},{9,8},{10,11... | collective-permute-start | bytes 7962632 | tf_op jit(solution)/shard_map/ppermute | solution.py:139
  87.6 9.4 %copy-start.4 = (bf16[4608,576]{1,0:T(8,128)(2,1)S(1)}, bf16[4608,576]{1,0:T(8,128)(2,1)}, u32[]{:S(2)}) copy-start(bf16[4608,576]{1,0:T(8,128)(2,1)} %all-gather.2.cloned.1.call-done) | copy-start | bytes 15925252
  103.9 2.1 %copy-start.3 = (f32[576,576]{1,0:T(8,128)}, f32[576,576]{1,0:T(8,128)S(1)}, u32[]{:S(2)}) copy-start(f32[576,576]{1,0:T(8,128)S(1)} %fusion) | copy-start | bytes 3981316
  116.4 65.5 %all-to-all-start = ((f16[256,8,384]{2,1,0:T(8,128)(2,1)}), f16[256,8,384]{2,1,0:T(8,128)(2,1)}, u32[]{:S(2)}, u32[]{:S(2)}) async-start(f16[256,8,384]{2,1,0:T(8,128)(2,1)} %convert_element_type.22), calls=%async_computation | async-start | bytes 3145728 | tf_op jit(solution)/shard_map/all_to_all | solution.py:167
  127.8 48.1 %collective-permute-start.5 = (f32[576,576]{1,0:T(8,128)}, f32[576,576]{1,0:T(8,128)S(1)}, u32[]{:S(2)}, u32[]{:S(2)}) collective-permute-start(f32[576,576]{1,0:T(8,128)} %fusion.4), channel_id=1, source_target_pairs={{0,16},{16,0},{1,17},{17,1},{2,18},{18,2},{3,19},{19,3},{4,20},{20... | collective-permute-start | bytes 3981320 | tf_op jit(solution)/shard_map/ppermute | solution.py:157
  178.6 6.7 %copy-start.2 = (s32[2]{0:T(128)S(1)}, s32[2]{0:T(128)}, u32[]{:S(2)}) copy-start(s32[2]{0:T(128)} %live_ref.1) | copy-start | bytes 28
  178.6 6.7 %collective-permute-start.6 = (f32[288,576]{1,0:T(8,128)}, f32[288,576]{1,0:T(8,128)}, u32[]{:S(2)}, u32[]{:S(2)}) collective-permute-start(f32[288,576]{1,0:T(8,128)} %get-tuple-element.7), channel_id=1, source_target_pairs={{0,1},{1,0},{2,3},{3,2},{4,5},{5,4},{6,7},{7,6},{8,9},{9,8},{10,11... | collective-permute-start | bytes 1990664 | tf_op jit(solution)/shard_map/ppermute | solution.py:158
  181.9 3.3 %copy-start = (f32[288,576]{1,0:T(8,128)S(1)}, f32[288,576]{1,0:T(8,128)}, u32[]{:S(2)}) copy-start(f32[288,576]{1,0:T(8,128)} %get-tuple-element.9.near_ref) | copy-start | bytes 1990660
  181.9 3.3 %copy-start.1 = (bf16[288,288]{1,0:T(8,128)(2,1)S(1)}, bf16[288,288]{1,0:T(8,128)(2,1)}, u32[]{:S(2)}) copy-start(bf16[288,288]{1,0:T(8,128)(2,1)} %fusion.40.row_ref) | copy-start | bytes 497668
Sparse Core Ops, SparseCore 0:
  15.8 71.7 all-gather.1

commit v4 on v2

v4 whole, which is shorter than its diff:
```python
import jax
import jax.numpy as jnp
from jax import lax
from jax.experimental import pallas as pl
from jax.experimental.pallas import tpu as pltpu
from jax.sharding import Mesh
from jax.sharding import PartitionSpec as P

VB = 96
OCC = 3
GRPS = 8
PAIRS = 32
ZS = 8
SLAB = VB // GRPS
PIECE = SLAB // 4 * SLAB
LANES = 384
CHUNK = 1152
WIRE = jnp.float16
SCALE = 16.0
BF, F32 = jnp.bfloat16, jnp.float32
ORDER = ("y", "xh", "xl", "c", "z")
SWAP = [(0, 1), (1, 0)]


def mm(x, y):
    return jnp.dot(x, y, preferred_element_type=F32)


def halves(x):
    hi = x.astype(BF)
    return hi, (x - hi.astype(F32)).astype(BF)


def selector(size, source):
    wanted = source(lax.broadcasted_iota(jnp.int32, (size, size), 0))
    return (wanted == lax.broadcasted_iota(jnp.int32, (size, size), 1)).astype(BF)


def product_kernel(*refs):
    *t_refs, w_ref, row_ref, col_ref, ladder_ref, out_ref, turned_ref = refs
    step = pl.program_id(0)

    @pl.when(step == 0)
    def _():
        ladder_ref[...] = jnp.zeros_like(ladder_ref)

    at = 0
    for t_ref in t_refs:
        size = t_ref.shape[0]
        ladder_ref[at : at + size] += mm(t_ref[...], w_ref[...])
        at += size

    @pl.when(step == pl.num_programs(0) - 1)
    def _():
        rows = row_ref.shape[0]
        for o in range(4):
            total = 0.0
            for part in halves(ladder_ref[o * rows : (o + 1) * rows] * SCALE):
                total += mm(mm(row_ref[...], part).astype(BF), col_ref[...])
            turned_ref[o] = total
        fill = jnp.zeros((PAIRS, LANES - OCC * OCC * PIECE), F32)
        for g in range(GRPS):
            planes = []
            for o in range(4):
                cut = [
                    turned_ref[o, q * PAIRS : (q + 1) * PAIRS, g * PIECE : (g + 1) * PIECE]
                    for q in range(OCC * OCC)
                ]
                planes.append(jnp.concatenate([*cut, fill], axis=1))
            message = jnp.swapaxes(jnp.stack(planes, axis=0), 0, 1)
            out_ref[g * PAIRS : (g + 1) * PAIRS] = message


def unpack_kernel(
    place_ref, live_ref, got_ref, own_ref, side_ref, far_ref, row_ref, col_ref, out_ref, v_ref
):
    for g in range(GRPS):
        v_ref[g] = jnp.swapaxes(got_ref[g * PAIRS : (g + 1) * PAIRS], 0, 1)
    blocks = []
    for j in range(OCC):
        for xl in range(2):
            for c in range(2):
                for i in range(OCC):
                    at = (i * OCC + j) * PIECE
                    cut = []
                    for g in range(GRPS):
                        for xs in range(2):
                            for cs in range(2):
                                z = (xs * 2 + cs) * ZS
                                o = (xl ^ xs) * 2 + (c ^ cs)
                                cut.append(v_ref[g, o, z : z + ZS, at : at + PIECE])
                    blocks.append(jnp.concatenate(cut, axis=1))
    stacked = jnp.concatenate(blocks, axis=0)
    total = 0.0
    for part in halves(stacked):
        total += mm(mm(row_ref[...], part).astype(BF), col_ref[...])

    def joined(first, x, y):
        return jnp.where(
            first, jnp.concatenate([x, y], axis=1), jnp.concatenate([y, x], axis=1)
        )

    near = joined(place_ref[1] == 0, own_ref[...], side_ref[...])
    far = joined(place_ref[1] == 0, far_ref[0], far_ref[1])
    summed = joined(place_ref[2] == 0, near, far) + total * (1 / SCALE)
    col = lax.broadcasted_iota(jnp.int32, summed.shape, 1)
    first = place_ref[0] * SLAB + col // VB
    keep = (first < live_ref[0]) & (col % VB < live_ref[0])
    out_ref[...] = jnp.where(keep, summed, 0.0).astype(BF)


def shift(x, axis, size, by):
    return lax.ppermute(x, axis, [(i, (i + by) % size) for i in range(size)])


def ring(block):
    half = block.shape[0] // 2
    up, down = [block], [block]
    for _ in range(ZS // 2 - 1):
        up.append(shift(up[-1], "z", ZS, 1))
        down.append(shift(down[-1], "z", ZS, -1))
    pieces = [(k, 0, b) for k, b in enumerate(up)]
    pieces += [(-k, 0, b) for k, b in enumerate(down) if k]
    last = ZS // 2
    pieces.append((last, 0, shift(up[-1][:half], "z", ZS, 1)))
    pieces.append((-last, half, shift(down[-1][half:], "z", ZS, -1)))
    return pieces


def on_device(amplitudes, integrals, live_counts):
    occ, nocc, k_all = amplitudes.shape
    shard, slab = integrals.shape
    rows, k_half, half, quarter = occ * nocc, k_all // 2, slab // 2, slab // 4
    xl, z, c = lax.axis_index("xl"), lax.axis_index("z"), lax.axis_index("c")
    pair = (xl * ZS + z) * 2 + c
    grp = lax.axis_index("y") * 2 + lax.axis_index("xh")

    t = amplitudes.reshape(rows, k_all)
    t_up = shift(t[: rows // 2], ("xh", "xl"), 4, 1)
    t_down = shift(t[rows // 2 :], ("xh", "xl"), 4, -1)

    at = pair * shard + jnp.arange(shard)
    live = (at // VB < live_counts[1]) & (at % VB < live_counts[1])
    w = jnp.where(live[:, None], integrals, 0)
    cols = [w[:, n * quarter : (n + 1) * quarter] for n in range(4)]
    first = c == 0
    w_keep = jnp.concatenate(
        [jnp.where(first, cols[0], cols[1]), jnp.where(first, cols[2], cols[3])], axis=0
    )
    w_send = jnp.concatenate(
        [jnp.where(first, cols[1], cols[0]), jnp.where(first, cols[3], cols[2])], axis=0
    )
    w_side = lax.ppermute(w_send, "c", SWAP)
    both = []
    for n in range(2):
        keep, side = w_keep[n * shard : (n + 1) * shard], w_side[n * shard : (n + 1) * shard]
        both.append(
            jnp.where(
                first,
                jnp.concatenate([keep, side], axis=0),
                jnp.concatenate([side, keep], axis=0),
            )
        )
    near = jnp.where(xl == 0, both[0], both[1])
    far = lax.ppermute(jnp.where(xl == 0, both[1], both[0]), "xl", SWAP)

    w_all = jnp.zeros((k_all, quarter), BF)
    for block, base in ((near, xl * k_half), (far, (1 - xl) * k_half)):
        for back, row, piece in ring(block):
            start = base + (z - back) % ZS * (2 * shard) + row
            w_all = lax.dynamic_update_slice(w_all, piece, (start, 0))

    t_refs = [t, lax.ppermute(t, "c", SWAP), t_up, t_down]
    t_refs += [lax.ppermute(t_up, "c", SWAP), lax.ppermute(t_down, "c", SWAP)]

    out_cols = selector(quarter, lambda r: ((r // SLAB) % GRPS) * PIECE + r // VB * SLAB + r % SLAB)
    in_cols = selector(slab, lambda r: (r % SLAB) * VB + r // SLAB)
    out_rows = selector(
        rows,
        lambda r: r // nocc * nocc
        + (r % PAIRS // 16) * 48
        + (r % ZS) * 6
        + (r // ZS % 2) * 3
        + r // PAIRS % OCC,
    )
    in_rows = selector(rows, lambda r: r // 48 * 48 + (r // 3 % 2) * 24 + (r % 3) * 8 + r // 6 % ZS)

    params = pltpu.CompilerParams(vmem_limit_bytes=48 * 2**20)
    fixed = lambda k: (0, 0)
    ladder, wire = pl.pallas_call(
        product_kernel,
        grid=(k_all // CHUNK,),
        in_specs=[pl.BlockSpec((x.shape[0], CHUNK), lambda k: (0, k)) for x in t_refs]
        + [
            pl.BlockSpec((CHUNK, quarter), lambda k: (k, 0)),
            pl.BlockSpec((rows, rows), fixed),
            pl.BlockSpec((quarter, quarter), fixed),
        ],
        out_specs=[
            pl.BlockSpec((4 * rows, quarter), fixed),
            pl.BlockSpec((GRPS * PAIRS, 4, LANES), lambda k: (0, 0, 0)),
        ],
        out_shape=[
            jax.ShapeDtypeStruct((4 * rows, quarter), F32),
            jax.ShapeDtypeStruct((GRPS * PAIRS, 4, LANES), F32),
        ],
        scratch_shapes=[pltpu.VMEM((4, rows, quarter), F32)],
        compiler_params=params,
    )(*t_refs, w_all, out_rows, out_cols)

    parts = ladder.reshape(2, 2, rows, quarter)
    side = lax.ppermute(parts[:, 1], "c", SWAP)
    fetched = lax.ppermute(jnp.stack([parts[1, 0], side[1]]), "xl", SWAP)

    got = lax.all_to_all(wire.astype(WIRE), ORDER, 0, 0, tiled=True)
    whole = pl.BlockSpec(memory_space=pltpu.VMEM)
    small = pl.BlockSpec(memory_space=pltpu.SMEM)
    out = pl.pallas_call(
        unpack_kernel,
        out_shape=jax.ShapeDtypeStruct((rows, slab), BF),
        in_specs=[small, small] + [whole] * 6,
        scratch_shapes=[pltpu.VMEM((GRPS, 4, PAIRS, LANES), F32)],
        compiler_params=params,
    )(
        jnp.stack([grp, c, xl]),
        live_counts,
        got.astype(F32),
        parts[0, 0],
        side[0],
        fetched,
        in_rows,
        in_cols,
    )
    return out.reshape(occ, nocc, slab)


def solution(mesh):
    fine = Mesh(mesh.devices.reshape(4, 2, 2, 8, 2), ("y", "xh", "xl", "z", "c"))
    pair, grp = ("xl", "z", "c"), ("y", "xh")
    return jax.shard_map(
        on_device,
        mesh=fine,
        in_specs=(P(pair, None, None), P(pair, grp), P()),
        out_specs=P(pair, None, grp),
        check_vma=False,
    )
```

time: 194 us -> 229 us (1.18)
  starting transfers between devices: 15.6 us -> 50.2 us
  matrix products: 14.5 us -> 0 us
  between operations: 13.6 us -> 0.26 us
  Pallas kernels: 13.7 us -> 26 us
  local copies, waits for them, and re-layouts: 21.8 us -> 32.7 us
  other arithmetic: 16.9 us -> 22.6 us
    ppermute x3 -> x25, waiting for transfers between devices: 0.01 us -> 78.4 us  [the longest x18 38.9 us: shift(): return lax.ppermute(x, axis, [(i, (i + by) % size) for i in range(size)])]
    all_gather x1 -> x0, waiting for transfers between devices: 59 us -> none  [on_device(): w_all = lax.all_gather(w, ('z', 'c'), axis=0, tiled=True)]
    ppermute x3 -> x25, starting transfers between devices: 4.78 us -> 39.4 us  [the longest x18 23.1 us: shift(): return lax.ppermute(x, axis, [(i, (i + by) % size) for i in range(size)])]
    all_to_all x1, waiting for transfers between devices: 38 us -> 18.4 us  [on_device(): got = lax.all_to_all(wire.astype(WIRE), ORDER, 0, 0, tiled=True)]
    dynamic_update_slice x0 -> x17, local copies, waits for them, and re-layouts: none -> 16.6 us  [on_device(): w_all = lax.dynamic_update_slice(w_all, piece, (start, 0))]
    dot_general x2 -> x0, matrix products: 14.5 us -> none  [mm(): return jnp.dot(x, y, preferred_element_type=F32)]
    pallas_call x1, Pallas kernels: 7.1 us -> 19.8 us  [on_device(): pl.pallas_call(product_kernel, grid=(k_all // CHUNK,), in_specs=[pl.Block...]
    unnamed x14 -> x22, local copies, waits for them, and re-layouts: 14.5 us -> 3.31 us
  transfers between devices with their start and end apart: 5 -> 26, of which waited for: 2 -> 15; matrix products, arithmetic and copies ran while one was open for 16% -> 22% of each run, Pallas kernels for 0% -> 0%
where the time goes in v4:
time: 229 us; the launch traced here: 228 us
  waiting for transfers between devices  96.7 us (42%)
  starting transfers between devices  50.2 us (22%)
  local copies, waits for them, and re-layouts  32.7 us (14%)
  Pallas kernels  26 us (11%)
  other arithmetic  22.6 us (10%)
    ppermute x18, waiting for transfers between devices, shift(): return lax.ppermute(x, axis, [(i, (i + by) % size) for i in range(size)])  38.9 us
    ppermute x1, waiting for transfers between devices, on_device(): far = lax.ppermute(jnp.where(xl == 0, both[1], both[0]), 'xl', SWAP)  36.9 us
    ppermute x18, starting transfers between devices, shift(): return lax.ppermute(x, axis, [(i, (i + by) % size) for i in range(size)])  23.1 us
    pallas_call x1, Pallas kernels, on_device(): pl.pallas_call(product_kernel, grid=(k_all // CHUNK,), in_specs=[pl.Block...  19.8 us
    all_to_all x1, waiting for transfers between devices, on_device(): got = lax.all_to_all(wire.astype(WIRE), ORDER, 0, 0, tiled=True)  18.4 us
    dynamic_update_slice x17, local copies, waits for them, and re-layouts, on_device(): w_all = lax.dynamic_update_slice(w_all, piece, (start, 0))  16.6 us
    all_to_all x1, starting transfers between devices, on_device(): got = lax.all_to_all(wire.astype(WIRE), ORDER, 0, 0, tiled=True)  10.8 us
    ppermute x1, starting transfers between devices, on_device(): side = lax.ppermute(parts[:, 1], 'c', SWAP)  9.36 us
  transfers between devices with their start and end apart: 26, of which 15 were waited for; matrix products, arithmetic and copies ran while one was open for 22% of the time, Pallas kernels for 0%

profile of v4, /device:TPU:1, one launch (start us, length us, event | category | flops | bytes accessed | tf_op | source)
XLA Modules:
  0.0 228.5 jit_solution(10268926062892696102)
XLA Ops:
  0.0 3.2 %collective-permute-start = (bf16[288,9216]{1,0:T(8,128)(2,1)}, bf16[288,9216]{1,0:T(8,128)(2,1)}, u32[]{:S(2)}, u32[]{:S(2)}) collective-permute-start(bf16[288,9216]{1,0:T(8,128)(2,1)} %bitcast.19), channel_id=1, source_target_pairs={{0,1},{1,0},{2,3},{3,2},{4,5},{5,4},{6,7},{7,6},{8,9},{9,8},{10,11... | collective-permute-start | bytes 15925256 | tf_op jit(solution)/shard_map/ppermute | solution.py:173
  3.2 4.4 %fusion.73 = (bf16[144,9216]{1,0:T(8,128)(2,1)S(1)}, bf16[144,9216]{1,0:T(8,128)(2,1)}) fusion(bf16[288,9216]{1,0:T(8,128)(2,1)} %bitcast.20), kind=kLoop, calls=%fused_computation.169 | loop fusion | bytes 10616832 | tf_op jit(solution)/shard_map/slice | solution.py:140
  7.6 2.7 %collective-permute-start.2 = (bf16[144,9216]{1,0:T(8,128)(2,1)S(1)}, bf16[144,9216]{1,0:T(8,128)(2,1)}, u32[]{:S(2)}, u32[]{:S(2)}) collective-permute-start(bf16[144,9216]{1,0:T(8,128)(2,1)S(1)} %get-tuple-element.11), channel_id=1, source_target_pairs={{0,48},{16,0},{32,16},{48,32},{1,49},{17,1},{33,17},{49,33},{2,50}... | collective-permute-start | bytes 7962632 | tf_op jit(solution)/shard_map/ppermute | solution.py:113
  18.7 3.2 %broadcast_in_dim.16 = bf16[9216,288]{1,0:T(8,128)(2,1)} broadcast(bf16[]{:T(256)} %constant.255.clone.1), dimensions={} | broadcast | bytes 5308418 | tf_op jit(solution)/shard_map/broadcast_in_dim | solution.py:167
  23.6 3.8 %collective-permute-start.9 = (bf16[576,288]{1,0:T(8,128)(2,1)S(1)}, bf16[576,288]{1,0:T(8,128)(2,1)}, u32[]{:S(2)}, u32[]{:S(2)}) collective-permute-start(bf16[576,288]{1,0:T(8,128)(2,1)S(1)} %get-tuple-element.10), channel_id=1, source_target_pairs={{0,14},{2,0},{4,2},{6,4},{8,6},{10,8},{12,10},{14,12},{1,15},{3,1}... | collective-permute-start | bytes 995336 | tf_op jit(solution)/shard_map/ppermute | solution.py:113
  28.3 9.1 %collective-permute-done.6 = bf16[576,288]{1,0:T(8,128)(2,1)} collective-permute-done((bf16[576,288]{1,0:T(8,128)(2,1)S(1)}, bf16[576,288]{1,0:T(8,128)(2,1)}, u32[]{:S(2)}, u32[]{:S(2)}) %collective-permute-start.6) | collective-permute-done | bytes 331808 | tf_op jit(solution)/shard_map/ppermute | solution.py:113
  39.3 36.9 %collective-permute-done.14 = bf16[576,288]{1,0:T(8,128)(2,1)S(1)} collective-permute-done((bf16[576,288]{1,0:T(8,128)(2,1)S(1)}, bf16[576,288]{1,0:T(8,128)(2,1)S(1)}, u32[]{:S(2)}, u32[]{:S(2)}) %collective-permute-start.14) | collective-permute-done | bytes 331808 | tf_op jit(solution)/shard_map/ppermute | solution.py:165
  76.2 4.8 %collective-permute-start.10 = (bf16[576,288]{1,0:T(8,128)(2,1)}, bf16[576,288]{1,0:T(8,128)(2,1)S(1)}, u32[]{:S(2)}, u32[]{:S(2)}) collective-permute-start(bf16[576,288]{1,0:T(8,128)(2,1)} %collective-permute-done.9), channel_id=1, source_target_pairs={{0,14},{2,0},{4,2},{6,4},{8,6},{10,8},{12,10},{14,12},{1,15},{3,1}... | collective-permute-start | bytes 995336 | tf_op jit(solution)/shard_map/ppermute | solution.py:113
  85.1 4.5 %collective-permute-done.10 = bf16[576,288]{1,0:T(8,128)(2,1)S(1)} collective-permute-done((bf16[576,288]{1,0:T(8,128)(2,1)}, bf16[576,288]{1,0:T(8,128)(2,1)S(1)}, u32[]{:S(2)}, u32[]{:S(2)}) %collective-permute-start.10) | collective-permute-done | bytes 331808 | tf_op jit(solution)/shard_map/ppermute | solution.py:113
  89.6 3.3 %collective-permute-start.18 = (bf16[576,288]{1,0:T(8,128)(2,1)S(1)}, bf16[576,288]{1,0:T(8,128)(2,1)S(1)}, u32[]{:S(2)}, u32[]{:S(2)}) collective-permute-start(bf16[576,288]{1,0:T(8,128)(2,1)S(1)} %collective-permute-done.14), channel_id=1, source_target_pairs={{0,14},{2,0},{4,2},{6,4},{8,6},{10,8},{12,10},{14,12},{1,15},{3,1}... | collective-permute-start | bytes 995336 | tf_op jit(solution)/shard_map/ppermute | solution.py:113
  94.6 5.7 %collective-permute-done.18 = bf16[576,288]{1,0:T(8,128)(2,1)S(1)} collective-permute-done((bf16[576,288]{1,0:T(8,128)(2,1)S(1)}, bf16[576,288]{1,0:T(8,128)(2,1)S(1)}, u32[]{:S(2)}, u32[]{:S(2)}) %collective-permute-start.18) | collective-permute-done | bytes 331808 | tf_op jit(solution)/shard_map/ppermute | solution.py:113
  100.2 3.4 %collective-permute-start.11 = (bf16[576,288]{1,0:T(8,128)(2,1)S(1)}, bf16[576,288]{1,0:T(8,128)(2,1)S(1)}, u32[]{:S(2)}, u32[]{:S(2)}) collective-permute-start(bf16[576,288]{1,0:T(8,128)(2,1)S(1)} %collective-permute-done.10), channel_id=1, source_target_pairs={{0,14},{2,0},{4,2},{6,4},{8,6},{10,8},{12,10},{14,12},{1,15},{3,1}... | collective-permute-start | bytes 995336 | tf_op jit(solution)/shard_map/ppermute | solution.py:113
  108.2 1.9 collective-permute-done.11
  111.9 3.1 %collective-permute-done.16 = bf16[576,288]{1,0:T(8,128)(2,1)S(1)} collective-permute-done((bf16[576,288]{1,0:T(8,128)(2,1)S(1)}, bf16[576,288]{1,0:T(8,128)(2,1)S(1)}, u32[]{:S(2)}, u32[]{:S(2)}) %collective-permute-start.16) | collective-permute-done | bytes 331808 | tf_op jit(solution)/shard_map/ppermute | solution.py:113
  116.3 3.5 %collective-permute-done.12 = bf16[288,288]{1,0:T(8,128)(2,1)S(1)} collective-permute-done((bf16[288,288]{1,0:T(8,128)(2,1)S(1)}, bf16[288,288]{1,0:T(8,128)(2,1)S(1)}, u32[]{:S(2)}, u32[]{:S(2)}) %collective-permute-start.12) | collective-permute-done | bytes 165920 | tf_op jit(solution)/shard_map/ppermute | solution.py:113
  124.6 2.6 %collective-permute-start.20 = (bf16[576,288]{1,0:T(8,128)(2,1)S(1)}, bf16[576,288]{1,0:T(8,128)(2,1)S(1)}, u32[]{:S(2)}, u32[]{:S(2)}) collective-permute-start(bf16[576,288]{1,0:T(8,128)(2,1)S(1)} %collective-permute-done.19), channel_id=1, source_target_pairs={{0,14},{2,0},{4,2},{6,4},{8,6},{10,8},{12,10},{14,12},{1,15},{3,1}... | collective-permute-start | bytes 995336 | tf_op jit(solution)/shard_map/ppermute | solution.py:113
  131.0 5.7 %collective-permute-done.20 = bf16[576,288]{1,0:T(8,128)(2,1)S(1)} collective-permute-done((bf16[576,288]{1,0:T(8,128)(2,1)S(1)}, bf16[576,288]{1,0:T(8,128)(2,1)S(1)}, u32[]{:S(2)}, u32[]{:S(2)}) %collective-permute-start.20) | collective-permute-done | bytes 331808 | tf_op jit(solution)/shard_map/ppermute | solution.py:113
  147.3 19.8 %shard_map.37 = (f32[1152,288]{1,0:T(8,128)S(1)}, f32[256,4,384]{2,1,0:T(4,128)S(1)}) custom-call(bf16[288,9216]{1,0:T(8,128)(2,1)} %bitcast.21, bf16[288,9216]{1,0:T(8,128)(2,1)} %collective-permute-done.refs_1_, bf16[144,9216]{1,0:T(8,128)(2,1)} %collective-permute-done.1.refs_2_, bf16[144,9216]{1,0:T(8,128)(2,1)} %collective-permute-done.2.refs_3_, ...), custom_call_target="tpu_custom_call" | custom-call | tf_op jit(solution)/shard_map/pallas_call | solution.py:190
  168.2 9.4 %collective-permute-start.23 = (f32[2,288,288]{2,1,0:T(8,128)}, f32[2,288,288]{2,1,0:T(8,128)}, u32[]{:S(2)}, u32[]{:S(2)}) collective-permute-start(f32[2,288,288]{2,1,0:T(8,128)} %slice_bitcast_fusion), channel_id=1, source_target_pairs={{0,1},{1,0},{2,3},{3,2},{4,5},{5,4},{6,7},{7,6},{8,9},{9,8},{10,11... | collective-permute-start | bytes 1990664 | tf_op jit(solution)/shard_map/ppermute | solution.py:212
  180.4 10.8 %all-to-all-start = ((f16[256,4,384]{2,1,0:T(4,128)(2,1)}), f16[256,4,384]{2,1,0:T(4,128)(2,1)}, u32[]{:S(2)}, u32[]{:S(2)}) async-start(f16[256,4,384]{2,1,0:T(4,128)(2,1)} %convert_element_type.22), calls=%async_computation | async-start | bytes 1572864 | tf_op jit(solution)/shard_map/all_to_all | solution.py:215
  196.7 2.4 %fusion.29.row_ref = bf16[288,288]{1,0:T(8,128)(2,1)} fusion(s32[288]{0:T(512)S(1)} %get-tuple-element.49, s32[288]{0:T(512)S(1)} %get-tuple-element.54, s32[288]{0:T(512)S(1)} %get-tuple-element.51, s32[288]{0:T(512)S(1)} %get-tuple-element.53, s32[288]{0:T(512)S(1)} %get-tuple-element.50, s32[288]{0:T(512)S(1)} %get-tuple-element.55, ...), kind=kLoop, calls=%fused_computation.70 | loop fusion | flops 2820096 | bytes 176256 | tf_op jit(solution)/shard_map/convert_element_type | solution.py:36
  199.1 18.4 %all-to-all-done = f16[256,4,384]{2,1,0:T(4,128)(2,1)} async-done(((f16[256,4,384]{2,1,0:T(4,128)(2,1)}), f16[256,4,384]{2,1,0:T(4,128)(2,1)}, u32[]{:S(2)}, u32[]{:S(2)}) %all-to-all-start) | async-done | bytes 786464 | tf_op jit(solution)/shard_map/all_to_all | solution.py:215
  218.9 2.5 %collective-permute-done.24.far_ref = f32[2,288,288]{2,1,0:T(8,128)} collective-permute-done((f32[2,288,288]{2,1,0:T(8,128)}, f32[2,288,288]{2,1,0:T(8,128)}, u32[]{:S(2)}, u32[]{:S(2)}) %collective-permute-start.24) | collective-permute-done | bytes 663584 | tf_op jit(solution)/shard_map/ppermute | solution.py:213
  222.3 6.2 %shard_map.38 = bf16[288,1152]{1,0:T(8,128)(2,1)} custom-call(s32[3]{0:T(128)S(1)} %pad_add_fusion.place_ref, s32[2]{0:T(128)S(1)} %copy-done.2, f32[256,4,384]{2,1,0:T(4,128)S(1)} %convert_element_type.23.got_ref, f32[288,288]{1,0:T(8,128)S(1)} %get-tuple-element.14.own_ref, f32[288,288]{1,0:T(8,128)S(1)} %get-tuple-element.16.side_ref, ...), custom_call_target="tpu_custom_call" | custom-call | tf_op jit(solution)/shard_map/pallas_call | solution.py:218
  (114 shorter events, 56.9 us)
Async XLA Ops:
  0.0 144.9 %collective-permute-start = (bf16[288,9216]{1,0:T(8,128)(2,1)}, bf16[288,9216]{1,0:T(8,128)(2,1)}, u32[]{:S(2)}, u32[]{:S(2)}) collective-permute-start(bf16[288,9216]{1,0:T(8,128)(2,1)} %bitcast.19), channel_id=1, source_target_pairs={{0,1},{1,0},{2,3},{3,2},{4,5},{5,4},{6,7},{7,6},{8,9},{9,8},{10,11... | collective-permute-start | bytes 15925256 | tf_op jit(solution)/shard_map/ppermute | solution.py:173
  7.6 74.0 %collective-permute-start.1 = (bf16[144,9216]{1,0:T(8,128)(2,1)}, bf16[144,9216]{1,0:T(8,128)(2,1)}, u32[]{:S(2)}, u32[]{:S(2)}) collective-permute-start(bf16[144,9216]{1,0:T(8,128)(2,1)} %get-tuple-element.12), channel_id=1, source_target_pairs={{0,16},{16,32},{32,48},{48,0},{1,17},{17,33},{33,49},{49,1},{2,18}... | collective-permute-start | bytes 7962632 | tf_op jit(solution)/shard_map/ppermute | solution.py:113
  7.6 75.5 %collective-permute-start.2 = (bf16[144,9216]{1,0:T(8,128)(2,1)S(1)}, bf16[144,9216]{1,0:T(8,128)(2,1)}, u32[]{:S(2)}, u32[]{:S(2)}) collective-permute-start(bf16[144,9216]{1,0:T(8,128)(2,1)S(1)} %get-tuple-element.11), channel_id=1, source_target_pairs={{0,48},{16,0},{32,16},{48,32},{1,49},{17,1},{33,17},{49,33},{2,50}... | collective-permute-start | bytes 7962632 | tf_op jit(solution)/shard_map/ppermute | solution.py:113
  23.0 14.5 %collective-permute-start.6 = (bf16[576,288]{1,0:T(8,128)(2,1)S(1)}, bf16[576,288]{1,0:T(8,128)(2,1)}, u32[]{:S(2)}, u32[]{:S(2)}) collective-permute-start(bf16[576,288]{1,0:T(8,128)(2,1)S(1)} %get-tuple-element.10), channel_id=1, source_target_pairs={{0,2},{2,4},{4,6},{6,8},{8,10},{10,12},{12,14},{14,0},{1,3},{3,5},... | collective-permute-start | bytes 995336 | tf_op jit(solution)/shard_map/ppermute | solution.py:113
  23.6 14.5 %collective-permute-start.9 = (bf16[576,288]{1,0:T(8,128)(2,1)S(1)}, bf16[576,288]{1,0:T(8,128)(2,1)}, u32[]{:S(2)}, u32[]{:S(2)}) collective-permute-start(bf16[576,288]{1,0:T(8,128)(2,1)S(1)} %get-tuple-element.10), channel_id=1, source_target_pairs={{0,14},{2,0},{4,2},{6,4},{8,6},{10,8},{12,10},{14,12},{1,15},{3,1}... | collective-permute-start | bytes 995336 | tf_op jit(solution)/shard_map/ppermute | solution.py:113
  37.5 38.7 %collective-permute-start.14 = (bf16[576,288]{1,0:T(8,128)(2,1)S(1)}, bf16[576,288]{1,0:T(8,128)(2,1)S(1)}, u32[]{:S(2)}, u32[]{:S(2)}) collective-permute-start(bf16[576,288]{1,0:T(8,128)(2,1)S(1)} %broadcast_select_fusion.1), channel_id=1, source_target_pairs={{0,16},{16,0},{1,17},{17,1},{2,18},{18,2},{3,19},{19,3},{4,20},{20... | collective-permute-start | bytes 995336 | tf_op jit(solution)/shard_map/ppermute | solution.py:165
  38.1 43.5 %collective-permute-start.7 = (bf16[576,288]{1,0:T(8,128)(2,1)}, bf16[576,288]{1,0:T(8,128)(2,1)}, u32[]{:S(2)}, u32[]{:S(2)}) collective-permute-start(bf16[576,288]{1,0:T(8,128)(2,1)} %collective-permute-done.6), channel_id=1, source_target_pairs={{0,2},{2,4},{4,6},{6,8},{8,10},{10,12},{12,14},{14,0},{1,3},{3,5},... | collective-permute-start | bytes 995336 | tf_op jit(solution)/shard_map/ppermute | solution.py:113
  76.2 13.4 %collective-permute-start.10 = (bf16[576,288]{1,0:T(8,128)(2,1)}, bf16[576,288]{1,0:T(8,128)(2,1)S(1)}, u32[]{:S(2)}, u32[]{:S(2)}) collective-permute-start(bf16[576,288]{1,0:T(8,128)(2,1)} %collective-permute-done.9), channel_id=1, source_target_pairs={{0,14},{2,0},{4,2},{6,4},{8,6},{10,8},{12,10},{14,12},{1,15},{3,1}... | collective-permute-start | bytes 995336 | tf_op jit(solution)/shard_map/ppermute | solution.py:113
  81.6 11.4 %collective-permute-start.15 = (bf16[576,288]{1,0:T(8,128)(2,1)S(1)}, bf16[576,288]{1,0:T(8,128)(2,1)S(1)}, u32[]{:S(2)}, u32[]{:S(2)}) collective-permute-start(bf16[576,288]{1,0:T(8,128)(2,1)S(1)} %collective-permute-done.14), channel_id=1, source_target_pairs={{0,2},{2,4},{4,6},{6,8},{8,10},{10,12},{12,14},{14,0},{1,3},{3,5},... | collective-permute-start | bytes 995336 | tf_op jit(solution)/shard_map/ppermute | solution.py:113
  81.6 63.3 %collective-permute-start.3 = (bf16[144,9216]{1,0:T(8,128)(2,1)}, bf16[144,9216]{1,0:T(8,128)(2,1)S(1)}, u32[]{:S(2)}, u32[]{:S(2)}) collective-permute-start(bf16[144,9216]{1,0:T(8,128)(2,1)} %collective-permute-done.1.refs_2_), channel_id=1, source_target_pairs={{0,1},{1,0},{2,3},{3,2},{4,5},{5,4},{6,7},{7,6},{8,9},{9,8},{10,11... | collective-permute-start | bytes 7962632 | tf_op jit(solution)/shard_map/ppermute | solution.py:174
  83.1 61.8 %collective-permute-start.4 = (bf16[144,9216]{1,0:T(8,128)(2,1)}, bf16[144,9216]{1,0:T(8,128)(2,1)S(1)}, u32[]{:S(2)}, u32[]{:S(2)}) collective-permute-start(bf16[144,9216]{1,0:T(8,128)(2,1)} %collective-permute-done.2.refs_3_), channel_id=1, source_target_pairs={{0,1},{1,0},{2,3},{3,2},{4,5},{5,4},{6,7},{7,6},{8,9},{9,8},{10,11... | collective-permute-start | bytes 7962632 | tf_op jit(solution)/shard_map/ppermute | solution.py:174
  89.6 10.7 %collective-permute-start.18 = (bf16[576,288]{1,0:T(8,128)(2,1)S(1)}, bf16[576,288]{1,0:T(8,128)(2,1)S(1)}, u32[]{:S(2)}, u32[]{:S(2)}) collective-permute-start(bf16[576,288]{1,0:T(8,128)(2,1)S(1)} %collective-permute-done.14), channel_id=1, source_target_pairs={{0,14},{2,0},{4,2},{6,4},{8,6},{10,8},{12,10},{14,12},{1,15},{3,1}... | collective-permute-start | bytes 995336 | tf_op jit(solution)/shard_map/ppermute | solution.py:113
  93.0 12.5 %collective-permute-start.8 = (bf16[576,288]{1,0:T(8,128)(2,1)}, bf16[576,288]{1,0:T(8,128)(2,1)S(1)}, u32[]{:S(2)}, u32[]{:S(2)}) collective-permute-start(bf16[576,288]{1,0:T(8,128)(2,1)} %collective-permute-done.7), channel_id=1, source_target_pairs={{0,2},{2,4},{4,6},{6,8},{8,10},{10,12},{12,14},{14,0},{1,3},{3,5},... | collective-permute-start | bytes 995336 | tf_op jit(solution)/shard_map/ppermute | solution.py:113
  100.2 9.9 %collective-permute-start.11 = (bf16[576,288]{1,0:T(8,128)(2,1)S(1)}, bf16[576,288]{1,0:T(8,128)(2,1)S(1)}, u32[]{:S(2)}, u32[]{:S(2)}) collective-permute-start(bf16[576,288]{1,0:T(8,128)(2,1)S(1)} %collective-permute-done.10), channel_id=1, source_target_pairs={{0,14},{2,0},{4,2},{6,4},{8,6},{10,8},{12,10},{14,12},{1,15},{3,1}... | collective-permute-start | bytes 995336 | tf_op jit(solution)/shard_map/ppermute | solution.py:113
  105.5 9.6 %collective-permute-start.16 = (bf16[576,288]{1,0:T(8,128)(2,1)S(1)}, bf16[576,288]{1,0:T(8,128)(2,1)S(1)}, u32[]{:S(2)}, u32[]{:S(2)}) collective-permute-start(bf16[576,288]{1,0:T(8,128)(2,1)S(1)} %collective-permute-done.15), channel_id=1, source_target_pairs={{0,2},{2,4},{4,6},{6,8},{8,10},{10,12},{12,14},{14,0},{1,3},{3,5},... | collective-permute-start | bytes 995336 | tf_op jit(solution)/shard_map/ppermute | solution.py:113
  110.1 9.7 %collective-permute-start.12 = (bf16[288,288]{1,0:T(8,128)(2,1)S(1)}, bf16[288,288]{1,0:T(8,128)(2,1)S(1)}, u32[]{:S(2)}, u32[]{:S(2)}) collective-permute-start(bf16[288,288]{1,0:T(8,128)(2,1)S(1)} %slice.81), channel_id=1, source_target_pairs={{0,2},{2,4},{4,6},{6,8},{8,10},{10,12},{12,14},{14,0},{1,3},{3,5},... | collective-permute-start | bytes 497672 | tf_op jit(solution)/shard_map/ppermute | solution.py:113
  115.1 7.4 %collective-permute-start.19 = (bf16[576,288]{1,0:T(8,128)(2,1)S(1)}, bf16[576,288]{1,0:T(8,128)(2,1)S(1)}, u32[]{:S(2)}, u32[]{:S(2)}) collective-permute-start(bf16[576,288]{1,0:T(8,128)(2,1)S(1)} %collective-permute-done.18), channel_id=1, source_target_pairs={{0,14},{2,0},{4,2},{6,4},{8,6},{10,8},{12,10},{14,12},{1,15},{3,1}... | collective-permute-start | bytes 995336 | tf_op jit(solution)/shard_map/ppermute | solution.py:113
  122.5 8.4 %collective-permute-start.17 = (bf16[576,288]{1,0:T(8,128)(2,1)S(1)}, bf16[576,288]{1,0:T(8,128)(2,1)S(1)}, u32[]{:S(2)}, u32[]{:S(2)}) collective-permute-start(bf16[576,288]{1,0:T(8,128)(2,1)S(1)} %collective-permute-done.16), channel_id=1, source_target_pairs={{0,2},{2,4},{4,6},{6,8},{8,10},{10,12},{12,14},{14,0},{1,3},{3,5},... | collective-permute-start | bytes 995336 | tf_op jit(solution)/shard_map/ppermute | solution.py:113
  124.6 12.1 %collective-permute-start.20 = (bf16[576,288]{1,0:T(8,128)(2,1)S(1)}, bf16[576,288]{1,0:T(8,128)(2,1)S(1)}, u32[]{:S(2)}, u32[]{:S(2)}) collective-permute-start(bf16[576,288]{1,0:T(8,128)(2,1)S(1)} %collective-permute-done.19), channel_id=1, source_target_pairs={{0,14},{2,0},{4,2},{6,4},{8,6},{10,8},{12,10},{14,12},{1,15},{3,1}... | collective-permute-start | bytes 995336 | tf_op jit(solution)/shard_map/ppermute | solution.py:113
  130.9 10.8 %collective-permute-start.21 = (bf16[288,288]{1,0:T(8,128)(2,1)S(1)}, bf16[288,288]{1,0:T(8,128)(2,1)S(1)}, u32[]{:S(2)}, u32[]{:S(2)}) collective-permute-start(bf16[288,288]{1,0:T(8,128)(2,1)S(1)} %slice.83), channel_id=1, source_target_pairs={{0,2},{2,4},{4,6},{6,8},{8,10},{10,12},{12,14},{14,0},{1,3},{3,5},... | collective-permute-start | bytes 497672 | tf_op jit(solution)/shard_map/ppermute | solution.py:113
  136.8 7.4 %collective-permute-start.22 = (bf16[288,288]{1,0:T(8,128)(2,1)S(1)}, bf16[288,288]{1,0:T(8,128)(2,1)S(1)}, u32[]{:S(2)}, u32[]{:S(2)}) collective-permute-start(bf16[288,288]{1,0:T(8,128)(2,1)S(1)} %slice.84), channel_id=1, source_target_pairs={{0,14},{2,0},{4,2},{6,4},{8,6},{10,8},{12,10},{14,12},{1,15},{3,1}... | collective-permute-start | bytes 497672 | tf_op jit(solution)/shard_map/ppermute | solution.py:113
  168.2 24.8 %collective-permute-start.23 = (f32[2,288,288]{2,1,0:T(8,128)}, f32[2,288,288]{2,1,0:T(8,128)}, u32[]{:S(2)}, u32[]{:S(2)}) collective-permute-start(f32[2,288,288]{2,1,0:T(8,128)} %slice_bitcast_fusion), channel_id=1, source_target_pairs={{0,1},{1,0},{2,3},{3,2},{4,5},{5,4},{6,7},{7,6},{8,9},{9,8},{10,11... | collective-permute-start | bytes 1990664 | tf_op jit(solution)/shard_map/ppermute | solution.py:212
  180.4 37.0 %all-to-all-start = ((f16[256,4,384]{2,1,0:T(4,128)(2,1)}), f16[256,4,384]{2,1,0:T(4,128)(2,1)}, u32[]{:S(2)}, u32[]{:S(2)}) async-start(f16[256,4,384]{2,1,0:T(4,128)(2,1)} %convert_element_type.22), calls=%async_computation | async-start | bytes 1572864 | tf_op jit(solution)/shard_map/all_to_all | solution.py:215
  195.2 26.1 %collective-permute-start.24 = (f32[2,288,288]{2,1,0:T(8,128)}, f32[2,288,288]{2,1,0:T(8,128)}, u32[]{:S(2)}, u32[]{:S(2)}) collective-permute-start(f32[2,288,288]{2,1,0:T(8,128)} %pad_maximum_fusion), channel_id=1, source_target_pairs={{0,16},{16,0},{1,17},{17,1},{2,18},{18,2},{3,19},{19,3},{4,20},{20... | collective-permute-start | bytes 1990664 | tf_op jit(solution)/shard_map/ppermute | solution.py:213
  (13 other events, 210.0 us)

commit v5 on v4

--- a/solution.py
+++ b/solution.py
@@ -1,5 +1,6 @@
 import jax
 import jax.numpy as jnp
+import numpy as np
 from jax import lax
 from jax.experimental import pallas as pl
 from jax.experimental.pallas import tpu as pltpu
@@ -14,12 +15,14 @@
 SLAB = VB // GRPS
 PIECE = SLAB // 4 * SLAB
 LANES = 384
-CHUNK = 1152
+CHUNK = 2304
 WIRE = jnp.float16
 SCALE = 16.0
 BF, F32 = jnp.bfloat16, jnp.float32
 ORDER = ("y", "xh", "xl", "c", "z")
 SWAP = [(0, 1), (1, 0)]
+SPLIT = 208
+RING = [(0, 0, 0), (1, 1, 0), (2, 2, 0), (3, 3, 0), (-1, 4, 0), (-2, 5, 0), (-3, 6, 0), (4, 7, 0), (4, 7, SPLIT)]
 
 
 def mm(x, y):
@@ -32,22 +35,55 @@
 
 
 def selector(size, source):
-    wanted = source(lax.broadcasted_iota(jnp.int32, (size, size), 0))
-    return (wanted == lax.broadcasted_iota(jnp.int32, (size, size), 1)).astype(BF)
-
-
-def product_kernel(*refs):
-    *t_refs, w_ref, row_ref, col_ref, ladder_ref, out_ref, turned_ref = refs
+    rows = np.arange(size)
+    chosen = np.zeros((size, size), np.float32)
+    chosen[rows, source(rows)] = 1
+    return jnp.asarray(chosen, BF)
+
+
+def folded(block):
+    tall, third = block.shape[0] // 4, block.shape[1] // 3
+    rest = [block[3 * tall :, n * third : (n + 1) * third] for n in range(3)]
+    return jnp.concatenate([block[: 3 * tall], jnp.concatenate(rest, axis=0)], axis=1)
+
+
+def product_kernel(place_ref, *refs):
+    t_refs, refs = refs[:6], refs[6:]
+    pieces, refs = refs[: 2 * len(RING)], refs[2 * len(RING) :]
+    row_ref, col_ref, ladder_ref, out_ref, turned_ref, stage_ref, w_ref, sem = refs
     step = pl.program_id(0)
 
     @pl.when(step == 0)
     def _():
         ladder_ref[...] = jnp.zeros_like(ladder_ref)
+        copies = []
+        for n, piece in enumerate(pieces):
+            slot, row = n // len(RING) * ZS + RING[n % len(RING)][1], RING[n % len(RING)][2]
+            copies.append(
+                pltpu.make_async_copy(
+                    piece, stage_ref.at[slot, pl.ds(row, piece.shape[0])], sem.at[n]
+                )
+            )
+        for copy in copies:
+            copy.start()
+        for copy in copies:
+            copy.wait()
+        z, xl = place_ref[0], place_ref[1]
+        tall, width = stage_ref.shape[1] // 3, w_ref.shape[1]
+        for stream in range(2):
+            base = lax.rem(xl + stream, 2) * ZS
+            for back, slot, _ in RING[:ZS]:
+                start = (base + lax.rem(z + ZS - back, ZS)) * (4 * tall)
+                start = pl.multiple_of(start, 4 * tall)
+                slot = stream * ZS + slot
+                w_ref[pl.ds(start, 3 * tall)] = stage_ref[slot, :, :width]
+                rest = [stage_ref[slot, n * tall : (n + 1) * tall, width:] for n in range(3)]
+                w_ref[pl.ds(start + 3 * tall, tall)] = jnp.concatenate(rest, axis=1)
 
     at = 0
     for t_ref in t_refs:
         size = t_ref.shape[0]
-        ladder_ref[at : at + size] += mm(t_ref[...], w_ref[...])
+        ladder_ref[at : at + size] += mm(t_ref[...], w_ref[pl.ds(pl.multiple_of(step * CHUNK, CHUNK), CHUNK)])
         at += size
 
     @pl.when(step == pl.num_programs(0) - 1)
@@ -114,30 +150,21 @@
 
 
 def ring(block):
-    half = block.shape[0] // 2
     up, down = [block], [block]
     for _ in range(ZS // 2 - 1):
         up.append(shift(up[-1], "z", ZS, 1))
         down.append(shift(down[-1], "z", ZS, -1))
-    pieces = [(k, 0, b) for k, b in enumerate(up)]
-    pieces += [(-k, 0, b) for k, b in enumerate(down) if k]
-    last = ZS // 2
-    pieces.append((last, 0, shift(up[-1][:half], "z", ZS, 1)))
-    pieces.append((-last, half, shift(down[-1][half:], "z", ZS, -1)))
-    return pieces
+    last = [shift(up[-1][:SPLIT], "z", ZS, 1), shift(down[-1][SPLIT:], "z", ZS, -1)]
+    return up + down[1:] + last
 
 
 def on_device(amplitudes, integrals, live_counts):
     occ, nocc, k_all = amplitudes.shape
     shard, slab = integrals.shape
-    rows, k_half, half, quarter = occ * nocc, k_all // 2, slab // 2, slab // 4
+    rows, quarter = occ * nocc, slab // 4
     xl, z, c = lax.axis_index("xl"), lax.axis_index("z"), lax.axis_index("c")
     pair = (xl * ZS + z) * 2 + c
     grp = lax.axis_index("y") * 2 + lax.axis_index("xh")
-
-    t = amplitudes.reshape(rows, k_all)
-    t_up = shift(t[: rows // 2], ("xh", "xl"), 4, 1)
-    t_down = shift(t[rows // 2 :], ("xh", "xl"), 4, -1)
 
     at = pair * shard + jnp.arange(shard)
     live = (at // VB < live_counts[1]) & (at % VB < live_counts[1])
@@ -162,14 +189,13 @@
             )
         )
     near = jnp.where(xl == 0, both[0], both[1])
-    far = lax.ppermute(jnp.where(xl == 0, both[1], both[0]), "xl", SWAP)
-
-    w_all = jnp.zeros((k_all, quarter), BF)
-    for block, base in ((near, xl * k_half), (far, (1 - xl) * k_half)):
-        for back, row, piece in ring(block):
-            start = base + (z - back) % ZS * (2 * shard) + row
-            w_all = lax.dynamic_update_slice(w_all, piece, (start, 0))
-
+    far = lax.ppermute(folded(jnp.where(xl == 0, both[1], both[0])), "xl", SWAP)
+    pieces = ring(folded(near)) + ring(far)
+
+    t = amplitudes.reshape(rows, k_all)
+    t_low, t_high, _ = lax.optimization_barrier((t[: rows // 2], t[rows // 2 :], far))
+    t_up = shift(t_low, ("xh", "xl"), 4, 1)
+    t_down = shift(t_high, ("xh", "xl"), 4, -1)
     t_refs = [t, lax.ppermute(t, "c", SWAP), t_up, t_down]
     t_refs += [lax.ppermute(t_up, "c", SWAP), lax.ppermute(t_down, "c", SWAP)]
 
@@ -190,9 +216,10 @@
     ladder, wire = pl.pallas_call(
         product_kernel,
         grid=(k_all // CHUNK,),
-        in_specs=[pl.BlockSpec((x.shape[0], CHUNK), lambda k: (0, k)) for x in t_refs]
+        in_specs=[pl.BlockSpec(memory_space=pltpu.SMEM)]
+        + [pl.BlockSpec((x.shape[0], CHUNK), lambda k: (0, k)) for x in t_refs]
+        + [pl.BlockSpec(memory_space=pl.ANY)] * len(pieces)
         + [
-            pl.BlockSpec((CHUNK, quarter), lambda k: (k, 0)),
             pl.BlockSpec((rows, rows), fixed),
             pl.BlockSpec((quarter, quarter), fixed),
         ],
@@ -204,9 +231,14 @@
             jax.ShapeDtypeStruct((4 * rows, quarter), F32),
             jax.ShapeDtypeStruct((GRPS * PAIRS, 4, LANES), F32),
         ],
-        scratch_shapes=[pltpu.VMEM((4, rows, quarter), F32)],
+        scratch_shapes=[
+            pltpu.VMEM((4, rows, quarter), F32),
+            pltpu.VMEM((2 * ZS, *far.shape), BF),
+            pltpu.VMEM((k_all, quarter), BF),
+            pltpu.SemaphoreType.DMA((len(pieces),)),
+        ],
         compiler_params=params,
-    )(*t_refs, w_all, out_rows, out_cols)
+    )(jnp.stack([z, xl]), *t_refs, *pieces, out_rows, out_cols)
 
     parts = ladder.reshape(2, 2, rows, quarter)
     side = lax.ppermute(parts[:, 1], "c", SWAP)

time: 229 us -> 236 us (1.031)
  waiting for transfers between devices: 96.7 us -> 136 us
  local copies, waits for them, and re-layouts: 32.7 us -> 12.6 us
  other arithmetic: 22.6 us -> 6.52 us
  Pallas kernels: 26 us -> 29.5 us
    ppermute x18, waiting for transfers between devices: 38.9 us -> 105 us  [shift(): return lax.ppermute(x, axis, [(i, (i + by) % size) for i in range(size)])]
    ppermute x1, waiting for transfers between devices: 36.9 us -> 5.91 us  [on_device(): far = lax.ppermute(folded(jnp.where(xl == 0, both[1], both[0])), 'xl', SWAP)]
    dynamic_update_slice x17 -> x0, local copies, waits for them, and re-layouts: 16.6 us -> none  [on_device(): w_all = lax.dynamic_update_slice(w_all, piece, (start, 0))]
    convert_element_type x4 -> x0, other arithmetic: 7.31 us -> none  [selector(): (wanted == lax.broadcasted_iota(jnp.int32, (size, size), 1)).astype(BF)]
    all_to_all x1, waiting for transfers between devices: 18.4 us -> 22.3 us  [on_device(): got = lax.all_to_all(wire.astype(WIRE), ORDER, 0, 0, tiled=True)]
    pallas_call x1, Pallas kernels: 19.8 us -> 23.4 us  [on_device(): pl.pallas_call(product_kernel, grid=(k_all // CHUNK,), in_specs=[pl.Block...]
    broadcast_in_dim x1 -> x0, local copies, waits for them, and re-layouts: 3.21 us -> none  [on_device(): w_all = jnp.zeros((k_all, quarter), BF)]
    ppermute x18, starting transfers between devices: 23.1 us -> 20.1 us  [shift(): return lax.ppermute(x, axis, [(i, (i + by) % size) for i in range(size)])]
  transfers between devices with their start and end apart: 26 -> 26, of which waited for: 15 -> 16; matrix products, arithmetic and copies ran while one was open for 22% -> 4% of each run, Pallas kernels for 0% -> 0%
where the time goes in v5:
time: 236 us; the launch traced here: 235 us
  waiting for transfers between devices  136 us (58%)
  starting transfers between devices  50.2 us (21%)
  Pallas kernels  29.5 us (12%)
  local copies, waits for them, and re-layouts  12.6 us (5%)
  other arithmetic  6.52 us (3%)
    ppermute x18, waiting for transfers between devices, shift(): return lax.ppermute(x, axis, [(i, (i + by) % size) for i in range(size)])  105 us
    pallas_call x1, Pallas kernels, on_device(): pl.pallas_call(product_kernel, grid=(k_all // CHUNK,), in_specs=[pl.Block...  23.4 us
    all_to_all x1, waiting for transfers between devices, on_device(): got = lax.all_to_all(wire.astype(WIRE), ORDER, 0, 0, tiled=True)  22.3 us
    ppermute x18, starting transfers between devices, shift(): return lax.ppermute(x, axis, [(i, (i + by) % size) for i in range(size)])  20.1 us
    ppermute x1, starting transfers between devices, on_device(): side = lax.ppermute(parts[:, 1], 'c', SWAP)  10.9 us
    all_to_all x1, starting transfers between devices, on_device(): got = lax.all_to_all(wire.astype(WIRE), ORDER, 0, 0, tiled=True)  10.4 us
    pallas_call x1, Pallas kernels, on_device(): pl.pallas_call(unpack_kernel, out_shape=jax.ShapeDtypeStruct((rows, slab)...  6.08 us
    ppermute x1, waiting for transfers between devices, on_device(): far = lax.ppermute(folded(jnp.where(xl == 0, both[1], both[0])), 'xl', SWAP)  5.91 us
  transfers between devices with their start and end apart: 26, of which 16 were waited for; matrix products, arithmetic and copies ran while one was open for 4% of the time, Pallas kernels for 0%

profile of v5, /device:TPU:1, one launch (start us, length us, event | category | flops | bytes accessed | tf_op | source)
XLA Modules:
  0.0 234.9 jit_solution(17945328819577408731)
XLA Ops:
  3.5 3.3 %collective-permute-start.1 = (bf16[576,288]{1,0:T(8,128)(2,1)S(1)}, bf16[576,288]{1,0:T(8,128)(2,1)S(1)}, u32[]{:S(2)}, u32[]{:S(2)}) collective-permute-start(bf16[576,288]{1,0:T(8,128)(2,1)S(1)} %pad_maximum_fusion.1), channel_id=1, source_target_pairs={{0,1},{1,0},{2,3},{3,2},{4,5},{5,4},{6,7},{7,6},{8,9},{9,8},{10,11... | collective-permute-start | bytes 995336 | tf_op jit(solution)/shard_map/ppermute | solution.py:180
  9.1 3.0 %fusion.8 = (bf16[144,9216]{1,0:T(8,128)(2,1)S(1)}, bf16[144,9216]{1,0:T(8,128)(2,1)S(1)}) fusion(bf16[288,9216]{1,0:T(8,128)(2,1)} %bitcast.18), kind=kLoop, calls=%fused_computation.31 | loop fusion | bytes 10616832 | tf_op jit(solution)/shard_map/slice | solution.py:196
  12.1 5.9 %collective-permute-done.2.refs_15_ = bf16[432,384]{1,0:T(8,128)(2,1)S(1)} collective-permute-done((bf16[432,384]{1,0:T(8,128)(2,1)S(1)}, bf16[432,384]{1,0:T(8,128)(2,1)S(1)}, u32[]{:S(2)}, u32[]{:S(2)}) %collective-permute-start.2) | collective-permute-done | bytes 331808 | tf_op jit(solution)/shard_map/ppermute | solution.py:192
  18.4 2.4 %collective-permute-start.4 = (bf16[144,9216]{1,0:T(8,128)(2,1)S(1)}, bf16[144,9216]{1,0:T(8,128)(2,1)S(1)}, u32[]{:S(2)}, u32[]{:S(2)}) collective-permute-start(bf16[144,9216]{1,0:T(8,128)(2,1)S(1)} %get-tuple-element.10), channel_id=1, source_target_pairs={{0,48},{16,0},{32,16},{48,32},{1,49},{17,1},{33,17},{49,33},{2,50}... | collective-permute-start | bytes 7962632 | tf_op jit(solution)/shard_map/ppermute | solution.py:149
  22.5 54.6 %collective-permute-done.3.refs_2_ = bf16[144,9216]{1,0:T(8,128)(2,1)S(1)} collective-permute-done((bf16[144,9216]{1,0:T(8,128)(2,1)S(1)}, bf16[144,9216]{1,0:T(8,128)(2,1)S(1)}, u32[]{:S(2)}, u32[]{:S(2)}) %collective-permute-start.3) | collective-permute-done | bytes 2654240 | tf_op jit(solution)/shard_map/ppermute | solution.py:149
  79.5 3.9 %collective-permute-start.10 = (bf16[432,384]{1,0:T(8,128)(2,1)S(1)}, bf16[432,384]{1,0:T(8,128)(2,1)S(1)}, u32[]{:S(2)}, u32[]{:S(2)}) collective-permute-start(bf16[432,384]{1,0:T(8,128)(2,1)S(1)} %maximum_maximum_fusion.1.refs_6_), channel_id=1, source_target_pairs={{0,14},{2,0},{4,2},{6,4},{8,6},{10,8},{12,10},{14,12},{1,15},{3,1}... | collective-permute-start | bytes 995336 | tf_op jit(solution)/shard_map/ppermute | solution.py:149
  83.5 6.8 %collective-permute-done.10.refs_10_ = bf16[432,384]{1,0:T(8,128)(2,1)S(1)} collective-permute-done((bf16[432,384]{1,0:T(8,128)(2,1)S(1)}, bf16[432,384]{1,0:T(8,128)(2,1)S(1)}, u32[]{:S(2)}, u32[]{:S(2)}) %collective-permute-start.10) | collective-permute-done | bytes 331808 | tf_op jit(solution)/shard_map/ppermute | solution.py:149
  90.2 3.4 %collective-permute-start.18 = (bf16[432,384]{1,0:T(8,128)(2,1)S(1)}, bf16[432,384]{1,0:T(8,128)(2,1)S(1)}, u32[]{:S(2)}, u32[]{:S(2)}) collective-permute-start(bf16[432,384]{1,0:T(8,128)(2,1)S(1)} %collective-permute-done.2.refs_15_), channel_id=1, source_target_pairs={{0,14},{2,0},{4,2},{6,4},{8,6},{10,8},{12,10},{14,12},{1,15},{3,1}... | collective-permute-start | bytes 995336 | tf_op jit(solution)/shard_map/ppermute | solution.py:149
  93.7 5.8 %collective-permute-done.18.refs_19_ = bf16[432,384]{1,0:T(8,128)(2,1)S(1)} collective-permute-done((bf16[432,384]{1,0:T(8,128)(2,1)S(1)}, bf16[432,384]{1,0:T(8,128)(2,1)S(1)}, u32[]{:S(2)}, u32[]{:S(2)}) %collective-permute-start.18) | collective-permute-done | bytes 331808 | tf_op jit(solution)/shard_map/ppermute | solution.py:149
  99.5 3.4 %collective-permute-start.11 = (bf16[432,384]{1,0:T(8,128)(2,1)S(1)}, bf16[432,384]{1,0:T(8,128)(2,1)S(1)}, u32[]{:S(2)}, u32[]{:S(2)}) collective-permute-start(bf16[432,384]{1,0:T(8,128)(2,1)S(1)} %collective-permute-done.10.refs_10_), channel_id=1, source_target_pairs={{0,14},{2,0},{4,2},{6,4},{8,6},{10,8},{12,10},{14,12},{1,15},{3,1}... | collective-permute-start | bytes 995336 | tf_op jit(solution)/shard_map/ppermute | solution.py:149
  102.9 4.9 %collective-permute-done.11.refs_11_ = bf16[432,384]{1,0:T(8,128)(2,1)S(1)} collective-permute-done((bf16[432,384]{1,0:T(8,128)(2,1)S(1)}, bf16[432,384]{1,0:T(8,128)(2,1)S(1)}, u32[]{:S(2)}, u32[]{:S(2)}) %collective-permute-start.11) | collective-permute-done | bytes 331808 | tf_op jit(solution)/shard_map/ppermute | solution.py:149
  107.8 3.4 %collective-permute-start.19 = (bf16[432,384]{1,0:T(8,128)(2,1)S(1)}, bf16[432,384]{1,0:T(8,128)(2,1)S(1)}, u32[]{:S(2)}, u32[]{:S(2)}) collective-permute-start(bf16[432,384]{1,0:T(8,128)(2,1)S(1)} %collective-permute-done.18.refs_19_), channel_id=1, source_target_pairs={{0,14},{2,0},{4,2},{6,4},{8,6},{10,8},{12,10},{14,12},{1,15},{3,1}... | collective-permute-start | bytes 995336 | tf_op jit(solution)/shard_map/ppermute | solution.py:149
  111.2 4.1 %collective-permute-done.19.refs_20_ = bf16[432,384]{1,0:T(8,128)(2,1)S(1)} collective-permute-done((bf16[432,384]{1,0:T(8,128)(2,1)S(1)}, bf16[432,384]{1,0:T(8,128)(2,1)S(1)}, u32[]{:S(2)}, u32[]{:S(2)}) %collective-permute-start.19) | collective-permute-done | bytes 331808 | tf_op jit(solution)/shard_map/ppermute | solution.py:149
  115.3 3.1 %collective-permute-done.9.refs_9_ = bf16[432,384]{1,0:T(8,128)(2,1)S(1)} collective-permute-done((bf16[432,384]{1,0:T(8,128)(2,1)S(1)}, bf16[432,384]{1,0:T(8,128)(2,1)S(1)}, u32[]{:S(2)}, u32[]{:S(2)}) %collective-permute-start.9) | collective-permute-done | bytes 331808 | tf_op jit(solution)/shard_map/ppermute | solution.py:149
  118.4 8.3 %collective-permute-done.16.refs_17_ = bf16[432,384]{1,0:T(8,128)(2,1)S(1)} collective-permute-done((bf16[432,384]{1,0:T(8,128)(2,1)S(1)}, bf16[432,384]{1,0:T(8,128)(2,1)S(1)}, u32[]{:S(2)}, u32[]{:S(2)}) %collective-permute-start.16) | collective-permute-done | bytes 331808 | tf_op jit(solution)/shard_map/ppermute | solution.py:149
  128.2 3.9 %collective-permute-done.13.refs_13_ = bf16[208,384]{1,0:T(8,128)(2,1)S(1)} collective-permute-done((bf16[208,384]{1,0:T(8,128)(2,1)S(1)}, bf16[208,384]{1,0:T(8,128)(2,1)S(1)}, u32[]{:S(2)}, u32[]{:S(2)}) %collective-permute-start.13) | collective-permute-done | bytes 159776 | tf_op jit(solution)/shard_map/ppermute | solution.py:149
  132.6 3.8 %collective-permute-done.20.refs_21_ = bf16[432,384]{1,0:T(8,128)(2,1)S(1)} collective-permute-done((bf16[432,384]{1,0:T(8,128)(2,1)S(1)}, bf16[432,384]{1,0:T(8,128)(2,1)S(1)}, u32[]{:S(2)}, u32[]{:S(2)}) %collective-permute-start.20) | collective-permute-done | bytes 331808 | tf_op jit(solution)/shard_map/ppermute | solution.py:149
  141.6 5.6 %collective-permute-done.21.refs_22_ = bf16[208,384]{1,0:T(8,128)(2,1)S(1)} collective-permute-done((bf16[208,384]{1,0:T(8,128)(2,1)S(1)}, bf16[208,384]{1,0:T(8,128)(2,1)S(1)}, u32[]{:S(2)}, u32[]{:S(2)}) %collective-permute-start.21) | collective-permute-done | bytes 159776 | tf_op jit(solution)/shard_map/ppermute | solution.py:149
  150.4 23.4 %shard_map.73 = (f32[1152,288]{1,0:T(8,128)}, f32[256,4,384]{2,1,0:T(4,128)}) custom-call(s32[2]{0:T(128)S(1)} %pad_add_fusion.1.place_ref, bf16[288,9216]{1,0:T(8,128)(2,1)} %bitcast.19, bf16[288,9216]{1,0:T(8,128)(2,1)} %copy-done.5, bf16[144,9216]{1,0:T(8,128)(2,1)} %copy-done.6, bf16[144,9216]{1,0:T(8,128)(2,1)} %copy-done.7, ...), custom_call_target="tpu_custom_call" | custom-call | tf_op jit(solution)/shard_map/pallas_call | solution.py:216
  173.9 2.3 slice_bitcast_fusion
  176.2 10.9 %collective-permute-start.23 = (f32[2,288,288]{2,1,0:T(8,128)}, f32[2,288,288]{2,1,0:T(8,128)}, u32[]{:S(2)}, u32[]{:S(2)}) collective-permute-start(f32[2,288,288]{2,1,0:T(8,128)} %slice_bitcast_fusion), channel_id=1, source_target_pairs={{0,1},{1,0},{2,3},{3,2},{4,5},{5,4},{6,7},{7,6},{8,9},{9,8},{10,11... | collective-permute-start | bytes 1990664 | tf_op jit(solution)/shard_map/ppermute | solution.py:244
  188.2 10.4 %all-to-all-start = ((f16[256,4,384]{2,1,0:T(4,128)(2,1)}), f16[256,4,384]{2,1,0:T(4,128)(2,1)}, u32[]{:S(2)}, u32[]{:S(2)}) async-start(f16[256,4,384]{2,1,0:T(4,128)(2,1)} %convert_element_type.8), calls=%async_computation | async-start | bytes 1572864 | tf_op jit(solution)/shard_map/all_to_all | solution.py:247
  202.5 22.3 %all-to-all-done = f16[256,4,384]{2,1,0:T(4,128)(2,1)} async-done(((f16[256,4,384]{2,1,0:T(4,128)(2,1)}), f16[256,4,384]{2,1,0:T(4,128)(2,1)}, u32[]{:S(2)}, u32[]{:S(2)}) %all-to-all-start) | async-done | bytes 786464 | tf_op jit(solution)/shard_map/all_to_all | solution.py:247
  228.9 6.1 %shard_map.74 = bf16[288,1152]{1,0:T(8,128)(2,1)} custom-call(s32[3]{0:T(128)S(1)} %pad_add_fusion.place_ref, s32[2]{0:T(128)S(1)} %copy-done.4, f32[256,4,384]{2,1,0:T(4,128)S(1)} %convert_element_type.9.got_ref, f32[288,288]{1,0:T(8,128)S(1)} %get-tuple-element.16.own_ref, f32[288,288]{1,0:T(8,128)S(1)} %get-tuple-element.18.side_ref, ...), custom_call_target="tpu_custom_call" | custom-call | tf_op jit(solution)/shard_map/pallas_call | solution.py:250
  (83 shorter events, 29.7 us)
Async XLA Ops:
  8.9 9.1 %collective-permute-start.2 = (bf16[432,384]{1,0:T(8,128)(2,1)S(1)}, bf16[432,384]{1,0:T(8,128)(2,1)S(1)}, u32[]{:S(2)}, u32[]{:S(2)}) collective-permute-start(bf16[432,384]{1,0:T(8,128)(2,1)S(1)} %maximum_maximum_fusion), channel_id=1, source_target_pairs={{0,16},{16,0},{1,17},{17,1},{2,18},{18,2},{3,19},{19,3},{4,20},{20... | collective-permute-start | bytes 995336 | tf_op jit(solution)/shard_map/ppermute | solution.py:192
  18.0 59.1 %collective-permute-start.3 = (bf16[144,9216]{1,0:T(8,128)(2,1)S(1)}, bf16[144,9216]{1,0:T(8,128)(2,1)S(1)}, u32[]{:S(2)}, u32[]{:S(2)}) collective-permute-start(bf16[144,9216]{1,0:T(8,128)(2,1)S(1)} %get-tuple-element.9), channel_id=1, source_target_pairs={{0,16},{16,32},{32,48},{48,0},{1,17},{17,33},{33,49},{49,1},{2,18}... | collective-permute-start | bytes 7962632 | tf_op jit(solution)/shard_map/ppermute | solution.py:149
  18.4 60.9 %collective-permute-start.4 = (bf16[144,9216]{1,0:T(8,128)(2,1)S(1)}, bf16[144,9216]{1,0:T(8,128)(2,1)S(1)}, u32[]{:S(2)}, u32[]{:S(2)}) collective-permute-start(bf16[144,9216]{1,0:T(8,128)(2,1)S(1)} %get-tuple-element.10), channel_id=1, source_target_pairs={{0,48},{16,0},{32,16},{48,32},{1,49},{17,1},{33,17},{49,33},{2,50}... | collective-permute-start | bytes 7962632 | tf_op jit(solution)/shard_map/ppermute | solution.py:149
  20.7 126.5 %collective-permute-start = (bf16[288,9216]{1,0:T(8,128)(2,1)S(1)}, bf16[288,9216]{1,0:T(8,128)(2,1)S(1)}, u32[]{:S(2)}, u32[]{:S(2)}) collective-permute-start(bf16[288,9216]{1,0:T(8,128)(2,1)S(1)} %bitcast.22), channel_id=1, source_target_pairs={{0,1},{1,0},{2,3},{3,2},{4,5},{5,4},{6,7},{7,6},{8,9},{9,8},{10,11... | collective-permute-start | bytes 15925256 | tf_op jit(solution)/shard_map/ppermute | solution.py:199
  77.1 70.1 %collective-permute-start.5 = (bf16[144,9216]{1,0:T(8,128)(2,1)S(1)}, bf16[144,9216]{1,0:T(8,128)(2,1)S(1)}, u32[]{:S(2)}, u32[]{:S(2)}) collective-permute-start(bf16[144,9216]{1,0:T(8,128)(2,1)S(1)} %collective-permute-done.3.refs_2_), channel_id=1, source_target_pairs={{0,1},{1,0},{2,3},{3,2},{4,5},{5,4},{6,7},{7,6},{8,9},{9,8},{10,11... | collective-permute-start | bytes 7962632 | tf_op jit(solution)/shard_map/ppermute | solution.py:200
  79.2 69.5 %collective-permute-start.6 = (bf16[144,9216]{1,0:T(8,128)(2,1)S(1)}, bf16[144,9216]{1,0:T(8,128)(2,1)}, u32[]{:S(2)}, u32[]{:S(2)}) collective-permute-start(bf16[144,9216]{1,0:T(8,128)(2,1)S(1)} %collective-permute-done.4.refs_3_), channel_id=1, source_target_pairs={{0,1},{1,0},{2,3},{3,2},{4,5},{5,4},{6,7},{7,6},{8,9},{9,8},{10,11... | collective-permute-start | bytes 7962632 | tf_op jit(solution)/shard_map/ppermute | solution.py:200
  79.5 10.7 %collective-permute-start.10 = (bf16[432,384]{1,0:T(8,128)(2,1)S(1)}, bf16[432,384]{1,0:T(8,128)(2,1)S(1)}, u32[]{:S(2)}, u32[]{:S(2)}) collective-permute-start(bf16[432,384]{1,0:T(8,128)(2,1)S(1)} %maximum_maximum_fusion.1.refs_6_), channel_id=1, source_target_pairs={{0,14},{2,0},{4,2},{6,4},{8,6},{10,8},{12,10},{14,12},{1,15},{3,1}... | collective-permute-start | bytes 995336 | tf_op jit(solution)/shard_map/ppermute | solution.py:149
  83.5 10.2 %collective-permute-start.7 = (bf16[432,384]{1,0:T(8,128)(2,1)S(1)}, bf16[432,384]{1,0:T(8,128)(2,1)S(1)}, u32[]{:S(2)}, u32[]{:S(2)}) collective-permute-start(bf16[432,384]{1,0:T(8,128)(2,1)S(1)} %maximum_maximum_fusion.1.refs_6_), channel_id=1, source_target_pairs={{0,2},{2,4},{4,6},{6,8},{8,10},{10,12},{12,14},{14,0},{1,3},{3,5},... | collective-permute-start | bytes 995336 | tf_op jit(solution)/shard_map/ppermute | solution.py:149
  90.2 9.3 %collective-permute-start.18 = (bf16[432,384]{1,0:T(8,128)(2,1)S(1)}, bf16[432,384]{1,0:T(8,128)(2,1)S(1)}, u32[]{:S(2)}, u32[]{:S(2)}) collective-permute-start(bf16[432,384]{1,0:T(8,128)(2,1)S(1)} %collective-permute-done.2.refs_15_), channel_id=1, source_target_pairs={{0,14},{2,0},{4,2},{6,4},{8,6},{10,8},{12,10},{14,12},{1,15},{3,1}... | collective-permute-start | bytes 995336 | tf_op jit(solution)/shard_map/ppermute | solution.py:149
  93.6 9.3 %collective-permute-start.15 = (bf16[432,384]{1,0:T(8,128)(2,1)S(1)}, bf16[432,384]{1,0:T(8,128)(2,1)S(1)}, u32[]{:S(2)}, u32[]{:S(2)}) collective-permute-start(bf16[432,384]{1,0:T(8,128)(2,1)S(1)} %collective-permute-done.2.refs_15_), channel_id=1, source_target_pairs={{0,2},{2,4},{4,6},{6,8},{8,10},{10,12},{12,14},{14,0},{1,3},{3,5},... | collective-permute-start | bytes 995336 | tf_op jit(solution)/shard_map/ppermute | solution.py:149
  99.5 8.3 %collective-permute-start.11 = (bf16[432,384]{1,0:T(8,128)(2,1)S(1)}, bf16[432,384]{1,0:T(8,128)(2,1)S(1)}, u32[]{:S(2)}, u32[]{:S(2)}) collective-permute-start(bf16[432,384]{1,0:T(8,128)(2,1)S(1)} %collective-permute-done.10.refs_10_), channel_id=1, source_target_pairs={{0,14},{2,0},{4,2},{6,4},{8,6},{10,8},{12,10},{14,12},{1,15},{3,1}... | collective-permute-start | bytes 995336 | tf_op jit(solution)/shard_map/ppermute | solution.py:149
  102.9 8.3 %collective-permute-start.8 = (bf16[432,384]{1,0:T(8,128)(2,1)S(1)}, bf16[432,384]{1,0:T(8,128)(2,1)S(1)}, u32[]{:S(2)}, u32[]{:S(2)}) collective-permute-start(bf16[432,384]{1,0:T(8,128)(2,1)S(1)} %collective-permute-done.7.refs_7_), channel_id=1, source_target_pairs={{0,2},{2,4},{4,6},{6,8},{8,10},{10,12},{12,14},{14,0},{1,3},{3,5},... | collective-permute-start | bytes 995336 | tf_op jit(solution)/shard_map/ppermute | solution.py:149
  107.8 7.5 %collective-permute-start.19 = (bf16[432,384]{1,0:T(8,128)(2,1)S(1)}, bf16[432,384]{1,0:T(8,128)(2,1)S(1)}, u32[]{:S(2)}, u32[]{:S(2)}) collective-permute-start(bf16[432,384]{1,0:T(8,128)(2,1)S(1)} %collective-permute-done.18.refs_19_), channel_id=1, source_target_pairs={{0,14},{2,0},{4,2},{6,4},{8,6},{10,8},{12,10},{14,12},{1,15},{3,1}... | collective-permute-start | bytes 995336 | tf_op jit(solution)/shard_map/ppermute | solution.py:149
  111.2 7.2 %collective-permute-start.9 = (bf16[432,384]{1,0:T(8,128)(2,1)S(1)}, bf16[432,384]{1,0:T(8,128)(2,1)S(1)}, u32[]{:S(2)}, u32[]{:S(2)}) collective-permute-start(bf16[432,384]{1,0:T(8,128)(2,1)S(1)} %collective-permute-done.8.refs_8_), channel_id=1, source_target_pairs={{0,2},{2,4},{4,6},{6,8},{8,10},{10,12},{12,14},{14,0},{1,3},{3,5},... | collective-permute-start | bytes 995336 | tf_op jit(solution)/shard_map/ppermute | solution.py:149
  115.3 11.4 %collective-permute-start.16 = (bf16[432,384]{1,0:T(8,128)(2,1)S(1)}, bf16[432,384]{1,0:T(8,128)(2,1)S(1)}, u32[]{:S(2)}, u32[]{:S(2)}) collective-permute-start(bf16[432,384]{1,0:T(8,128)(2,1)S(1)} %collective-permute-done.15.refs_16_), channel_id=1, source_target_pairs={{0,2},{2,4},{4,6},{6,8},{8,10},{10,12},{12,14},{14,0},{1,3},{3,5},... | collective-permute-start | bytes 995336 | tf_op jit(solution)/shard_map/ppermute | solution.py:149
  118.4 8.3 %collective-permute-start.12 = (bf16[432,384]{1,0:T(8,128)(2,1)S(1)}, bf16[432,384]{1,0:T(8,128)(2,1)S(1)}, u32[]{:S(2)}, u32[]{:S(2)}) collective-permute-start(bf16[432,384]{1,0:T(8,128)(2,1)S(1)} %collective-permute-done.11.refs_11_), channel_id=1, source_target_pairs={{0,14},{2,0},{4,2},{6,4},{8,6},{10,8},{12,10},{14,12},{1,15},{3,1}... | collective-permute-start | bytes 995336 | tf_op jit(solution)/shard_map/ppermute | solution.py:149
  126.7 9.7 %collective-permute-start.20 = (bf16[432,384]{1,0:T(8,128)(2,1)S(1)}, bf16[432,384]{1,0:T(8,128)(2,1)S(1)}, u32[]{:S(2)}, u32[]{:S(2)}) collective-permute-start(bf16[432,384]{1,0:T(8,128)(2,1)S(1)} %collective-permute-done.19.refs_20_), channel_id=1, source_target_pairs={{0,14},{2,0},{4,2},{6,4},{8,6},{10,8},{12,10},{14,12},{1,15},{3,1}... | collective-permute-start | bytes 995336 | tf_op jit(solution)/shard_map/ppermute | solution.py:149
  126.7 5.3 %collective-permute-start.13 = (bf16[208,384]{1,0:T(8,128)(2,1)S(1)}, bf16[208,384]{1,0:T(8,128)(2,1)S(1)}, u32[]{:S(2)}, u32[]{:S(2)}) collective-permute-start(bf16[208,384]{1,0:T(8,128)(2,1)S(1)} %slice.121), channel_id=1, source_target_pairs={{0,2},{2,4},{4,6},{6,8},{8,10},{10,12},{12,14},{14,0},{1,3},{3,5},... | collective-permute-start | bytes 479240 | tf_op jit(solution)/shard_map/ppermute | solution.py:149
  132.1 7.2 %collective-permute-start.17 = (bf16[432,384]{1,0:T(8,128)(2,1)S(1)}, bf16[432,384]{1,0:T(8,128)(2,1)S(1)}, u32[]{:S(2)}, u32[]{:S(2)}) collective-permute-start(bf16[432,384]{1,0:T(8,128)(2,1)S(1)} %collective-permute-done.16.refs_17_), channel_id=1, source_target_pairs={{0,2},{2,4},{4,6},{6,8},{8,10},{10,12},{12,14},{14,0},{1,3},{3,5},... | collective-permute-start | bytes 995336 | tf_op jit(solution)/shard_map/ppermute | solution.py:149
  139.2 7.9 %collective-permute-start.22 = (bf16[224,384]{1,0:T(8,128)(2,1)S(1)}, bf16[224,384]{1,0:T(8,128)(2,1)S(1)}, u32[]{:S(2)}, u32[]{:S(2)}) collective-permute-start(bf16[224,384]{1,0:T(8,128)(2,1)S(1)} %slice.124), channel_id=1, source_target_pairs={{0,14},{2,0},{4,2},{6,4},{8,6},{10,8},{12,10},{14,12},{1,15},{3,1}... | collective-permute-start | bytes 516104 | tf_op jit(solution)/shard_map/ppermute | solution.py:149
  141.5 5.6 %collective-permute-start.21 = (bf16[208,384]{1,0:T(8,128)(2,1)S(1)}, bf16[208,384]{1,0:T(8,128)(2,1)S(1)}, u32[]{:S(2)}, u32[]{:S(2)}) collective-permute-start(bf16[208,384]{1,0:T(8,128)(2,1)S(1)} %slice.123), channel_id=1, source_target_pairs={{0,2},{2,4},{4,6},{6,8},{8,10},{10,12},{12,14},{14,0},{1,3},{3,5},... | collective-permute-start | bytes 479240 | tf_op jit(solution)/shard_map/ppermute | solution.py:149
  176.2 22.5 %collective-permute-start.23 = (f32[2,288,288]{2,1,0:T(8,128)}, f32[2,288,288]{2,1,0:T(8,128)}, u32[]{:S(2)}, u32[]{:S(2)}) collective-permute-start(f32[2,288,288]{2,1,0:T(8,128)} %slice_bitcast_fusion), channel_id=1, source_target_pairs={{0,1},{1,0},{2,3},{3,2},{4,5},{5,4},{6,7},{7,6},{8,9},{9,8},{10,11... | collective-permute-start | bytes 1990664 | tf_op jit(solution)/shard_map/ppermute | solution.py:244
  188.2 36.6 %all-to-all-start = ((f16[256,4,384]{2,1,0:T(4,128)(2,1)}), f16[256,4,384]{2,1,0:T(4,128)(2,1)}, u32[]{:S(2)}, u32[]{:S(2)}) async-start(f16[256,4,384]{2,1,0:T(4,128)(2,1)} %convert_element_type.8), calls=%async_computation | async-start | bytes 1572864 | tf_op jit(solution)/shard_map/all_to_all | solution.py:247
  201.1 26.8 %collective-permute-start.24 = (f32[2,288,288]{2,1,0:T(8,128)}, f32[2,288,288]{2,1,0:T(8,128)}, u32[]{:S(2)}, u32[]{:S(2)}) collective-permute-start(f32[2,288,288]{2,1,0:T(8,128)} %pad_maximum_fusion), channel_id=1, source_target_pairs={{0,16},{16,0},{1,17},{17,1},{2,18},{18,2},{3,19},{19,3},{4,20},{20... | collective-permute-start | bytes 1990664 | tf_op jit(solution)/shard_map/ppermute | solution.py:245
  (15 other events, 550.1 us)

commit v6 on v5

--- a/solution.py
+++ b/solution.py
@@ -21,8 +21,6 @@
 BF, F32 = jnp.bfloat16, jnp.float32
 ORDER = ("y", "xh", "xl", "c", "z")
 SWAP = [(0, 1), (1, 0)]
-SPLIT = 208
-RING = [(0, 0, 0), (1, 1, 0), (2, 2, 0), (3, 3, 0), (-1, 4, 0), (-2, 5, 0), (-3, 6, 0), (4, 7, 0), (4, 7, SPLIT)]
 
 
 def mm(x, y):
@@ -48,37 +46,31 @@
 
 
 def product_kernel(place_ref, *refs):
-    t_refs, refs = refs[:6], refs[6:]
-    pieces, refs = refs[: 2 * len(RING)], refs[2 * len(RING) :]
+    t_refs, pieces, refs = refs[:4], refs[4 : 4 + 2 * ZS], refs[4 + 2 * ZS :]
     row_ref, col_ref, ladder_ref, out_ref, turned_ref, stage_ref, w_ref, sem = refs
     step = pl.program_id(0)
 
     @pl.when(step == 0)
     def _():
         ladder_ref[...] = jnp.zeros_like(ladder_ref)
-        copies = []
-        for n, piece in enumerate(pieces):
-            slot, row = n // len(RING) * ZS + RING[n % len(RING)][1], RING[n % len(RING)][2]
-            copies.append(
-                pltpu.make_async_copy(
-                    piece, stage_ref.at[slot, pl.ds(row, piece.shape[0])], sem.at[n]
-                )
-            )
+        copies = [
+            pltpu.make_async_copy(piece, stage_ref.at[n], sem.at[n])
+            for n, piece in enumerate(pieces)
+        ]
         for copy in copies:
             copy.start()
         for copy in copies:
             copy.wait()
-        z, xl = place_ref[0], place_ref[1]
+        z, xl, c = place_ref[0], place_ref[1], place_ref[2]
         tall, width = stage_ref.shape[1] // 3, w_ref.shape[1]
-        for stream in range(2):
-            base = lax.rem(xl + stream, 2) * ZS
-            for back, slot, _ in RING[:ZS]:
-                start = (base + lax.rem(z + ZS - back, ZS)) * (4 * tall)
-                start = pl.multiple_of(start, 4 * tall)
-                slot = stream * ZS + slot
-                w_ref[pl.ds(start, 3 * tall)] = stage_ref[slot, :, :width]
-                rest = [stage_ref[slot, n * tall : (n + 1) * tall, width:] for n in range(3)]
-                w_ref[pl.ds(start + 3 * tall, tall)] = jnp.concatenate(rest, axis=1)
+        for n in range(2 * ZS):
+            k = n % ZS
+            back = jnp.where(c == 0, k, ZS - k)
+            of = jnp.where(n < ZS, xl, 1 - xl) * ZS + lax.rem(z + ZS - back, ZS)
+            start = pl.multiple_of(of * (4 * tall), 4 * tall)
+            w_ref[pl.ds(start, 3 * tall)] = stage_ref[n, :, :width]
+            rest = [stage_ref[n, m * tall : (m + 1) * tall, width:] for m in range(3)]
+            w_ref[pl.ds(start + 3 * tall, tall)] = jnp.concatenate(rest, axis=1)
 
     at = 0
     for t_ref in t_refs:
@@ -145,17 +137,17 @@
     out_ref[...] = jnp.where(keep, summed, 0.0).astype(BF)
 
 
-def shift(x, axis, size, by):
-    return lax.ppermute(x, axis, [(i, (i + by) % size) for i in range(size)])
+def around(x, axes, size):
+    moves = [(i * 2, (i + 1) % size * 2) for i in range(size)]
+    moves += [(i * 2 + 1, (i - 1) % size * 2 + 1) for i in range(size)]
+    return lax.ppermute(x, (*axes, "c"), moves)
 
 
 def ring(block):
-    up, down = [block], [block]
-    for _ in range(ZS // 2 - 1):
-        up.append(shift(up[-1], "z", ZS, 1))
-        down.append(shift(down[-1], "z", ZS, -1))
-    last = [shift(up[-1][:SPLIT], "z", ZS, 1), shift(down[-1][SPLIT:], "z", ZS, -1)]
-    return up + down[1:] + last
+    blocks = [block]
+    for _ in range(ZS - 1):
+        blocks.append(around(blocks[-1], ("z",), ZS))
+    return blocks
 
 
 def on_device(amplitudes, integrals, live_counts):
@@ -190,14 +182,13 @@
         )
     near = jnp.where(xl == 0, both[0], both[1])
     far = lax.ppermute(folded(jnp.where(xl == 0, both[1], both[0])), "xl", SWAP)
-    pieces = ring(folded(near)) + ring(far)
-
-    t = amplitudes.reshape(rows, k_all)
-    t_low, t_high, _ = lax.optimization_barrier((t[: rows // 2], t[rows // 2 :], far))
-    t_up = shift(t_low, ("xh", "xl"), 4, 1)
-    t_down = shift(t_high, ("xh", "xl"), 4, -1)
-    t_refs = [t, lax.ppermute(t, "c", SWAP), t_up, t_down]
-    t_refs += [lax.ppermute(t_up, "c", SWAP), lax.ppermute(t_down, "c", SWAP)]
+    ring_near, ring_far = ring(folded(near)), ring(far)
+    pieces = ring_near + ring_far
+
+    t, _ = lax.optimization_barrier((amplitudes.reshape(rows, k_all), (far, ring_near[1])))
+    t_x = around(t, ("xh", "xl"), 4)
+    t_x, *_ = lax.optimization_barrier((t_x, ring_near[-1], ring_far[-1]))
+    t_refs = [t, lax.ppermute(t, "c", SWAP), t_x, lax.ppermute(t_x, "c", SWAP)]
 
     out_cols = selector(quarter, lambda r: ((r // SLAB) % GRPS) * PIECE + r // VB * SLAB + r % SLAB)
     in_cols = selector(slab, lambda r: (r % SLAB) * VB + r // SLAB)
@@ -238,7 +229,7 @@
             pltpu.SemaphoreType.DMA((len(pieces),)),
         ],
         compiler_params=params,
-    )(jnp.stack([z, xl]), *t_refs, *pieces, out_rows, out_cols)
+    )(jnp.stack([z, xl, c]), *t_refs, *pieces, out_rows, out_cols)
 
     parts = ladder.reshape(2, 2, rows, quarter)
     side = lax.ppermute(parts[:, 1], "c", SWAP)

time: 236 us -> 165 us (0.70)
  waiting for transfers between devices: 136 us -> 48.5 us
  starting transfers between devices: 50.2 us -> 72.2 us
  local copies, waits for them, and re-layouts: 12.6 us -> 8.55 us
    ppermute x21 -> x17, waiting for transfers between devices: 105 us -> 19.3 us  [the longest x15 13.2 us: around(): return lax.ppermute(x, (*axes, 'c'), moves)]
    ppermute x21 -> x17, starting transfers between devices: 24.1 us -> 55.8 us  [the longest x15 49.4 us: around(): return lax.ppermute(x, (*axes, 'c'), moves)]
    ppermute x1, starting transfers between devices: 10.9 us -> 0.4 us  [on_device(): side = lax.ppermute(parts[:, 1], 'c', SWAP)]
    slice x5 -> x0, local copies, waits for them, and re-layouts: 3.11 us -> none  [the longest x1 3.04 us: on_device(): t[rows // 2:]]
  transfers between devices with their start and end apart: 26 -> 22, of which waited for: 16 -> 19; matrix products, arithmetic and copies ran while one was open for 4% -> 3% of each run, Pallas kernels for 0% -> 0%
where the time goes in v6:
time: 165 us
  starting transfers between devices  72.2 us (44%)
  waiting for transfers between devices  48.5 us (29%)
  Pallas kernels  28.7 us (17%)
  local copies, waits for them, and re-layouts  8.55 us (5%)
  other arithmetic  6.47 us (4%)
    ppermute x15, starting transfers between devices, around(): return lax.ppermute(x, (*axes, 'c'), moves)  49.4 us
    pallas_call x1, Pallas kernels, on_device(): pl.pallas_call(product_kernel, grid=(k_all // CHUNK,), in_specs=[pl.Block...  22.6 us
    all_to_all x1, waiting for transfers between devices, on_device(): got = lax.all_to_all(wire.astype(WIRE), ORDER, 0, 0, tiled=True)  22.3 us
    ppermute x15, waiting for transfers between devices, around(): return lax.ppermute(x, (*axes, 'c'), moves)  13.2 us
    all_to_all x1, starting transfers between devices, on_device(): got = lax.all_to_all(wire.astype(WIRE), ORDER, 0, 0, tiled=True)  11.2 us
    ppermute x2, starting transfers between devices, on_device(): t_refs = [t, lax.ppermute(t, 'c', SWAP), t_x, lax.ppermute(t_x, 'c', SWAP)]  6.43 us
    ppermute x2, waiting for transfers between devices, on_device(): t_refs = [t, lax.ppermute(t, 'c', SWAP), t_x, lax.ppermute(t_x, 'c', SWAP)]  6.12 us
    pallas_call x1, Pallas kernels, on_device(): pl.pallas_call(unpack_kernel, out_shape=jax.ShapeDtypeStruct((rows, slab)...  6.08 us
  transfers between devices with their start and end apart: 22, of which 19 were waited for; matrix products, arithmetic and copies ran while one was open for 3% of the time, Pallas kernels for 0%

profile of v6, /device:TPU:1, one launch (start us, length us, event | category | flops | bytes accessed | tf_op | source)
XLA Modules:
  0.0 164.6 jit_solution(17486392285039406531)
XLA Ops:
  3.5 3.3 %collective-permute-start = (bf16[576,288]{1,0:T(8,128)(2,1)S(1)}, bf16[576,288]{1,0:T(8,128)(2,1)S(1)}, u32[]{:S(2)}, u32[]{:S(2)}) collective-permute-start(bf16[576,288]{1,0:T(8,128)(2,1)S(1)} %pad_maximum_fusion.1), channel_id=1, source_target_pairs={{0,1},{1,0},{2,3},{3,2},{4,5},{5,4},{6,7},{7,6},{8,9},{9,8},{10,11... | collective-permute-start | bytes 995336 | tf_op jit(solution)/shard_map/ppermute | solution.py:172
  9.3 5.1 %collective-permute-start.2 = (bf16[432,384]{1,0:T(8,128)(2,1)S(1)}, bf16[432,384]{1,0:T(8,128)(2,1)S(1)}, u32[]{:S(2)}, u32[]{:S(2)}) collective-permute-start(bf16[432,384]{1,0:T(8,128)(2,1)S(1)} %maximum_maximum_fusion.1.refs_4_), channel_id=1, source_target_pairs={{0,2},{2,4},{4,6},{6,8},{8,10},{10,12},{12,14},{14,0},{1,15},{3,1}... | collective-permute-start | bytes 995336 | tf_op jit(solution)/shard_map/ppermute | solution.py:143
  14.4 3.8 %collective-permute-done.1.refs_12_ = bf16[432,384]{1,0:T(8,128)(2,1)S(1)} collective-permute-done((bf16[432,384]{1,0:T(8,128)(2,1)S(1)}, bf16[432,384]{1,0:T(8,128)(2,1)S(1)}, u32[]{:S(2)}, u32[]{:S(2)}) %collective-permute-start.1) | collective-permute-done | bytes 331808 | tf_op jit(solution)/shard_map/ppermute | solution.py:184
  20.3 4.2 %collective-permute-start.11 = (bf16[432,384]{1,0:T(8,128)(2,1)S(1)}, bf16[432,384]{1,0:T(8,128)(2,1)S(1)}, u32[]{:S(2)}, u32[]{:S(2)}) collective-permute-start(bf16[432,384]{1,0:T(8,128)(2,1)S(1)} %collective-permute-done.1.refs_12_), channel_id=1, source_target_pairs={{0,2},{2,4},{4,6},{6,8},{8,10},{10,12},{12,14},{14,0},{1,15},{3,1}... | collective-permute-start | bytes 995336 | tf_op jit(solution)/shard_map/ppermute | solution.py:143
  25.2 3.3 %collective-permute-done.11.refs_13_ = bf16[432,384]{1,0:T(8,128)(2,1)S(1)} collective-permute-done((bf16[432,384]{1,0:T(8,128)(2,1)S(1)}, bf16[432,384]{1,0:T(8,128)(2,1)S(1)}, u32[]{:S(2)}, u32[]{:S(2)}) %collective-permute-start.11) | collective-permute-done | bytes 331808 | tf_op jit(solution)/shard_map/ppermute | solution.py:143
  28.6 3.4 %collective-permute-start.12 = (bf16[432,384]{1,0:T(8,128)(2,1)S(1)}, bf16[432,384]{1,0:T(8,128)(2,1)S(1)}, u32[]{:S(2)}, u32[]{:S(2)}) collective-permute-start(bf16[432,384]{1,0:T(8,128)(2,1)S(1)} %collective-permute-done.11.refs_13_), channel_id=1, source_target_pairs={{0,2},{2,4},{4,6},{6,8},{8,10},{10,12},{12,14},{14,0},{1,15},{3,1}... | collective-permute-start | bytes 995336 | tf_op jit(solution)/shard_map/ppermute | solution.py:143
  32.1 3.4 %collective-permute-start.6 = (bf16[432,384]{1,0:T(8,128)(2,1)S(1)}, bf16[432,384]{1,0:T(8,128)(2,1)S(1)}, u32[]{:S(2)}, u32[]{:S(2)}) collective-permute-start(bf16[432,384]{1,0:T(8,128)(2,1)S(1)} %collective-permute-done.5.refs_6_), channel_id=1, source_target_pairs={{0,2},{2,4},{4,6},{6,8},{8,10},{10,12},{12,14},{14,0},{1,15},{3,1}... | collective-permute-start | bytes 995336 | tf_op jit(solution)/shard_map/ppermute | solution.py:143
  36.0 3.4 %collective-permute-start.13 = (bf16[432,384]{1,0:T(8,128)(2,1)S(1)}, bf16[432,384]{1,0:T(8,128)(2,1)S(1)}, u32[]{:S(2)}, u32[]{:S(2)}) collective-permute-start(bf16[432,384]{1,0:T(8,128)(2,1)S(1)} %collective-permute-done.12.refs_14_), channel_id=1, source_target_pairs={{0,2},{2,4},{4,6},{6,8},{8,10},{10,12},{12,14},{14,0},{1,15},{3,1}... | collective-permute-start | bytes 995336 | tf_op jit(solution)/shard_map/ppermute | solution.py:143
  39.6 3.4 %collective-permute-start.7 = (bf16[432,384]{1,0:T(8,128)(2,1)S(1)}, bf16[432,384]{1,0:T(8,128)(2,1)S(1)}, u32[]{:S(2)}, u32[]{:S(2)}) collective-permute-start(bf16[432,384]{1,0:T(8,128)(2,1)S(1)} %collective-permute-done.6.refs_7_), channel_id=1, source_target_pairs={{0,2},{2,4},{4,6},{6,8},{8,10},{10,12},{12,14},{14,0},{1,15},{3,1}... | collective-permute-start | bytes 995336 | tf_op jit(solution)/shard_map/ppermute | solution.py:143
  43.5 3.4 %collective-permute-start.14 = (bf16[432,384]{1,0:T(8,128)(2,1)S(1)}, bf16[432,384]{1,0:T(8,128)(2,1)S(1)}, u32[]{:S(2)}, u32[]{:S(2)}) collective-permute-start(bf16[432,384]{1,0:T(8,128)(2,1)S(1)} %collective-permute-done.13.refs_15_), channel_id=1, source_target_pairs={{0,2},{2,4},{4,6},{6,8},{8,10},{10,12},{12,14},{14,0},{1,15},{3,1}... | collective-permute-start | bytes 995336 | tf_op jit(solution)/shard_map/ppermute | solution.py:143
  47.1 3.4 %collective-permute-start.8 = (bf16[432,384]{1,0:T(8,128)(2,1)S(1)}, bf16[432,384]{1,0:T(8,128)(2,1)S(1)}, u32[]{:S(2)}, u32[]{:S(2)}) collective-permute-start(bf16[432,384]{1,0:T(8,128)(2,1)S(1)} %collective-permute-done.7.refs_8_), channel_id=1, source_target_pairs={{0,2},{2,4},{4,6},{6,8},{8,10},{10,12},{12,14},{14,0},{1,15},{3,1}... | collective-permute-start | bytes 995336 | tf_op jit(solution)/shard_map/ppermute | solution.py:143
  51.0 3.4 %collective-permute-start.15 = (bf16[432,384]{1,0:T(8,128)(2,1)S(1)}, bf16[432,384]{1,0:T(8,128)(2,1)S(1)}, u32[]{:S(2)}, u32[]{:S(2)}) collective-permute-start(bf16[432,384]{1,0:T(8,128)(2,1)S(1)} %collective-permute-done.14.refs_16_), channel_id=1, source_target_pairs={{0,2},{2,4},{4,6},{6,8},{8,10},{10,12},{12,14},{14,0},{1,15},{3,1}... | collective-permute-start | bytes 995336 | tf_op jit(solution)/shard_map/ppermute | solution.py:143
  54.5 3.4 %collective-permute-start.9 = (bf16[432,384]{1,0:T(8,128)(2,1)S(1)}, bf16[432,384]{1,0:T(8,128)(2,1)S(1)}, u32[]{:S(2)}, u32[]{:S(2)}) collective-permute-start(bf16[432,384]{1,0:T(8,128)(2,1)S(1)} %collective-permute-done.8.refs_9_), channel_id=1, source_target_pairs={{0,2},{2,4},{4,6},{6,8},{8,10},{10,12},{12,14},{14,0},{1,15},{3,1}... | collective-permute-start | bytes 995336 | tf_op jit(solution)/shard_map/ppermute | solution.py:143
  58.5 3.4 %collective-permute-start.16 = (bf16[432,384]{1,0:T(8,128)(2,1)S(1)}, bf16[432,384]{1,0:T(8,128)(2,1)S(1)}, u32[]{:S(2)}, u32[]{:S(2)}) collective-permute-start(bf16[432,384]{1,0:T(8,128)(2,1)S(1)} %collective-permute-done.15.refs_17_), channel_id=1, source_target_pairs={{0,2},{2,4},{4,6},{6,8},{8,10},{10,12},{12,14},{14,0},{1,15},{3,1}... | collective-permute-start | bytes 995336 | tf_op jit(solution)/shard_map/ppermute | solution.py:143
  62.0 3.4 %collective-permute-start.10 = (bf16[432,384]{1,0:T(8,128)(2,1)S(1)}, bf16[432,384]{1,0:T(8,128)(2,1)S(1)}, u32[]{:S(2)}, u32[]{:S(2)}) collective-permute-start(bf16[432,384]{1,0:T(8,128)(2,1)S(1)} %collective-permute-done.9.refs_10_), channel_id=1, source_target_pairs={{0,2},{2,4},{4,6},{6,8},{8,10},{10,12},{12,14},{14,0},{1,15},{3,1}... | collective-permute-start | bytes 995336 | tf_op jit(solution)/shard_map/ppermute | solution.py:143
  65.9 3.4 %collective-permute-start.17 = (bf16[432,384]{1,0:T(8,128)(2,1)S(1)}, bf16[432,384]{1,0:T(8,128)(2,1)S(1)}, u32[]{:S(2)}, u32[]{:S(2)}) collective-permute-start(bf16[432,384]{1,0:T(8,128)(2,1)S(1)} %collective-permute-done.16.refs_18_), channel_id=1, source_target_pairs={{0,2},{2,4},{4,6},{6,8},{8,10},{10,12},{12,14},{14,0},{1,15},{3,1}... | collective-permute-start | bytes 995336 | tf_op jit(solution)/shard_map/ppermute | solution.py:143
  69.3 2.4 %collective-permute-start.3 = (bf16[288,9216]{1,0:T(8,128)(2,1)S(1)}, bf16[288,9216]{1,0:T(8,128)(2,1)S(1)}, u32[]{:S(2)}, u32[]{:S(2)}) collective-permute-start(bf16[288,9216]{1,0:T(8,128)(2,1)S(1)} %bitcast.20), channel_id=1, source_target_pairs={{0,1},{1,0},{2,3},{3,2},{4,5},{5,4},{6,7},{7,6},{8,9},{9,8},{10,11... | collective-permute-start | bytes 15925256 | tf_op jit(solution)/shard_map/ppermute | solution.py:191
  73.4 4.6 %collective-permute-done.4.refs_2_ = bf16[288,9216]{1,0:T(8,128)(2,1)S(1)} collective-permute-done((bf16[288,9216]{1,0:T(8,128)(2,1)S(1)}, bf16[288,9216]{1,0:T(8,128)(2,1)S(1)}, u32[]{:S(2)}, u32[]{:S(2)}) %collective-permute-start.4) | collective-permute-done | bytes 5308448 | tf_op jit(solution)/shard_map/ppermute | solution.py:143
  78.0 4.0 %collective-permute-start.18 = (bf16[288,9216]{1,0:T(8,128)(2,1)S(1)}, bf16[288,9216]{1,0:T(8,128)(2,1)}, u32[]{:S(2)}, u32[]{:S(2)}) collective-permute-start(bf16[288,9216]{1,0:T(8,128)(2,1)S(1)} %collective-permute-done.4.refs_2_), channel_id=1, source_target_pairs={{0,1},{1,0},{2,3},{3,2},{4,5},{5,4},{6,7},{7,6},{8,9},{9,8},{10,11... | collective-permute-start | bytes 15925256 | tf_op jit(solution)/shard_map/ppermute | solution.py:191
  84.5 6.1 %collective-permute-done.18.refs_3_ = bf16[288,9216]{1,0:T(8,128)(2,1)} collective-permute-done((bf16[288,9216]{1,0:T(8,128)(2,1)S(1)}, bf16[288,9216]{1,0:T(8,128)(2,1)}, u32[]{:S(2)}, u32[]{:S(2)}) %collective-permute-start.18) | collective-permute-done | bytes 5308448 | tf_op jit(solution)/shard_map/ppermute | solution.py:191
  90.6 22.6 %shard_map.73 = (f32[1152,288]{1,0:T(8,128)}, f32[256,4,384]{2,1,0:T(4,128)}) custom-call(s32[3]{0:T(128)S(1)} %pad_add_fusion.1.place_ref, bf16[288,9216]{1,0:T(8,128)(2,1)} %bitcast.18, bf16[288,9216]{1,0:T(8,128)(2,1)} %copy-done.7, bf16[288,9216]{1,0:T(8,128)(2,1)} %copy-done.6, bf16[288,9216]{1,0:T(8,128)(2,1)} %collective-permute-done.18.refs_3_, ...), custom_call_target="tpu_custom_call" | custom-call | tf_op jit(solution)/shard_map/pallas_call | solution.py:207
  117.1 11.2 %all-to-all-start = ((f16[256,4,384]{2,1,0:T(4,128)(2,1)}), f16[256,4,384]{2,1,0:T(4,128)(2,1)}, u32[]{:S(2)}, u32[]{:S(2)}) async-start(f16[256,4,384]{2,1,0:T(4,128)(2,1)} %convert_element_type.8), calls=%async_computation | async-start | bytes 1572864 | tf_op jit(solution)/shard_map/all_to_all | solution.py:238
  132.2 22.3 %all-to-all-done = f16[256,4,384]{2,1,0:T(4,128)(2,1)} async-done(((f16[256,4,384]{2,1,0:T(4,128)(2,1)}), f16[256,4,384]{2,1,0:T(4,128)(2,1)}, u32[]{:S(2)}, u32[]{:S(2)}) %all-to-all-start) | async-done | bytes 786464 | tf_op jit(solution)/shard_map/all_to_all | solution.py:238
  158.5 6.1 %shard_map.74 = bf16[288,1152]{1,0:T(8,128)(2,1)} custom-call(s32[3]{0:T(128)S(1)} %pad_add_fusion.place_ref, s32[2]{0:T(128)S(1)} %copy-done.4, f32[256,4,384]{2,1,0:T(4,128)S(1)} %convert_element_type.9.got_ref, f32[288,288]{1,0:T(8,128)S(1)} %get-tuple-element.14.own_ref, f32[288,288]{1,0:T(8,128)S(1)} %get-tuple-element.16.side_ref, ...), custom_call_target="tpu_custom_call" | custom-call | tf_op jit(solution)/shard_map/pallas_call | solution.py:241
  (63 shorter events, 27.7 us)
Async XLA Ops:
  3.5 4.7 %collective-permute-start = (bf16[576,288]{1,0:T(8,128)(2,1)S(1)}, bf16[576,288]{1,0:T(8,128)(2,1)S(1)}, u32[]{:S(2)}, u32[]{:S(2)}) collective-permute-start(bf16[576,288]{1,0:T(8,128)(2,1)S(1)} %pad_maximum_fusion.1), channel_id=1, source_target_pairs={{0,1},{1,0},{2,3},{3,2},{4,5},{5,4},{6,7},{7,6},{8,9},{9,8},{10,11... | collective-permute-start | bytes 995336 | tf_op jit(solution)/shard_map/ppermute | solution.py:172
  8.3 82.3 %copy-start.2 = (bf16[288,288]{1,0:T(8,128)(2,1)S(1)}, bf16[288,288]{1,0:T(8,128)(2,1)}, u32[]{:S(2)}) copy-start(bf16[288,288]{1,0:T(8,128)(2,1)} %constant.61.clone.refs_20_) | copy-start | bytes 497668
  8.3 82.3 %copy-start.3 = (bf16[288,288]{1,0:T(8,128)(2,1)S(1)}, bf16[288,288]{1,0:T(8,128)(2,1)}, u32[]{:S(2)}) copy-start(bf16[288,288]{1,0:T(8,128)(2,1)} %constant.59.clone.refs_21_) | copy-start | bytes 497668
  9.1 9.1 %collective-permute-start.1 = (bf16[432,384]{1,0:T(8,128)(2,1)S(1)}, bf16[432,384]{1,0:T(8,128)(2,1)S(1)}, u32[]{:S(2)}, u32[]{:S(2)}) collective-permute-start(bf16[432,384]{1,0:T(8,128)(2,1)S(1)} %maximum_maximum_fusion), channel_id=1, source_target_pairs={{0,16},{16,0},{1,17},{17,1},{2,18},{18,2},{3,19},{19,3},{4,20},{20... | collective-permute-start | bytes 995336 | tf_op jit(solution)/shard_map/ppermute | solution.py:184
  9.3 9.2 %collective-permute-start.2 = (bf16[432,384]{1,0:T(8,128)(2,1)S(1)}, bf16[432,384]{1,0:T(8,128)(2,1)S(1)}, u32[]{:S(2)}, u32[]{:S(2)}) collective-permute-start(bf16[432,384]{1,0:T(8,128)(2,1)S(1)} %maximum_maximum_fusion.1.refs_4_), channel_id=1, source_target_pairs={{0,2},{2,4},{4,6},{6,8},{8,10},{10,12},{12,14},{14,0},{1,15},{3,1}... | collective-permute-start | bytes 995336 | tf_op jit(solution)/shard_map/ppermute | solution.py:143
  18.5 59.6 %collective-permute-start.4 = (bf16[288,9216]{1,0:T(8,128)(2,1)S(1)}, bf16[288,9216]{1,0:T(8,128)(2,1)S(1)}, u32[]{:S(2)}, u32[]{:S(2)}) collective-permute-start(bf16[288,9216]{1,0:T(8,128)(2,1)S(1)} %bitcast.19), channel_id=1, source_target_pairs={{0,16},{16,32},{32,48},{48,0},{1,49},{17,1},{33,17},{49,33},{2,18}... | collective-permute-start | bytes 15925256 | tf_op jit(solution)/shard_map/ppermute | solution.py:143
  20.3 8.3 %collective-permute-start.11 = (bf16[432,384]{1,0:T(8,128)(2,1)S(1)}, bf16[432,384]{1,0:T(8,128)(2,1)S(1)}, u32[]{:S(2)}, u32[]{:S(2)}) collective-permute-start(bf16[432,384]{1,0:T(8,128)(2,1)S(1)} %collective-permute-done.1.refs_12_), channel_id=1, source_target_pairs={{0,2},{2,4},{4,6},{6,8},{8,10},{10,12},{12,14},{14,0},{1,15},{3,1}... | collective-permute-start | bytes 995336 | tf_op jit(solution)/shard_map/ppermute | solution.py:143
  24.5 7.6 %collective-permute-start.5 = (bf16[432,384]{1,0:T(8,128)(2,1)S(1)}, bf16[432,384]{1,0:T(8,128)(2,1)S(1)}, u32[]{:S(2)}, u32[]{:S(2)}) collective-permute-start(bf16[432,384]{1,0:T(8,128)(2,1)S(1)} %collective-permute-done.2.refs_5_), channel_id=1, source_target_pairs={{0,2},{2,4},{4,6},{6,8},{8,10},{10,12},{12,14},{14,0},{1,15},{3,1}... | collective-permute-start | bytes 995336 | tf_op jit(solution)/shard_map/ppermute | solution.py:143
  28.6 7.5 %collective-permute-start.12 = (bf16[432,384]{1,0:T(8,128)(2,1)S(1)}, bf16[432,384]{1,0:T(8,128)(2,1)S(1)}, u32[]{:S(2)}, u32[]{:S(2)}) collective-permute-start(bf16[432,384]{1,0:T(8,128)(2,1)S(1)} %collective-permute-done.11.refs_13_), channel_id=1, source_target_pairs={{0,2},{2,4},{4,6},{6,8},{8,10},{10,12},{12,14},{14,0},{1,15},{3,1}... | collective-permute-start | bytes 995336 | tf_op jit(solution)/shard_map/ppermute | solution.py:143
  32.1 7.5 %collective-permute-start.6 = (bf16[432,384]{1,0:T(8,128)(2,1)S(1)}, bf16[432,384]{1,0:T(8,128)(2,1)S(1)}, u32[]{:S(2)}, u32[]{:S(2)}) collective-permute-start(bf16[432,384]{1,0:T(8,128)(2,1)S(1)} %collective-permute-done.5.refs_6_), channel_id=1, source_target_pairs={{0,2},{2,4},{4,6},{6,8},{8,10},{10,12},{12,14},{14,0},{1,15},{3,1}... | collective-permute-start | bytes 995336 | tf_op jit(solution)/shard_map/ppermute | solution.py:143
  36.0 7.5 %collective-permute-start.13 = (bf16[432,384]{1,0:T(8,128)(2,1)S(1)}, bf16[432,384]{1,0:T(8,128)(2,1)S(1)}, u32[]{:S(2)}, u32[]{:S(2)}) collective-permute-start(bf16[432,384]{1,0:T(8,128)(2,1)S(1)} %collective-permute-done.12.refs_14_), channel_id=1, source_target_pairs={{0,2},{2,4},{4,6},{6,8},{8,10},{10,12},{12,14},{14,0},{1,15},{3,1}... | collective-permute-start | bytes 995336 | tf_op jit(solution)/shard_map/ppermute | solution.py:143
  39.6 7.5 %collective-permute-start.7 = (bf16[432,384]{1,0:T(8,128)(2,1)S(1)}, bf16[432,384]{1,0:T(8,128)(2,1)S(1)}, u32[]{:S(2)}, u32[]{:S(2)}) collective-permute-start(bf16[432,384]{1,0:T(8,128)(2,1)S(1)} %collective-permute-done.6.refs_7_), channel_id=1, source_target_pairs={{0,2},{2,4},{4,6},{6,8},{8,10},{10,12},{12,14},{14,0},{1,15},{3,1}... | collective-permute-start | bytes 995336 | tf_op jit(solution)/shard_map/ppermute | solution.py:143
  43.5 7.5 %collective-permute-start.14 = (bf16[432,384]{1,0:T(8,128)(2,1)S(1)}, bf16[432,384]{1,0:T(8,128)(2,1)S(1)}, u32[]{:S(2)}, u32[]{:S(2)}) collective-permute-start(bf16[432,384]{1,0:T(8,128)(2,1)S(1)} %collective-permute-done.13.refs_15_), channel_id=1, source_target_pairs={{0,2},{2,4},{4,6},{6,8},{8,10},{10,12},{12,14},{14,0},{1,15},{3,1}... | collective-permute-start | bytes 995336 | tf_op jit(solution)/shard_map/ppermute | solution.py:143
  47.1 7.5 %collective-permute-start.8 = (bf16[432,384]{1,0:T(8,128)(2,1)S(1)}, bf16[432,384]{1,0:T(8,128)(2,1)S(1)}, u32[]{:S(2)}, u32[]{:S(2)}) collective-permute-start(bf16[432,384]{1,0:T(8,128)(2,1)S(1)} %collective-permute-done.7.refs_8_), channel_id=1, source_target_pairs={{0,2},{2,4},{4,6},{6,8},{8,10},{10,12},{12,14},{14,0},{1,15},{3,1}... | collective-permute-start | bytes 995336 | tf_op jit(solution)/shard_map/ppermute | solution.py:143
  51.0 7.5 %collective-permute-start.15 = (bf16[432,384]{1,0:T(8,128)(2,1)S(1)}, bf16[432,384]{1,0:T(8,128)(2,1)S(1)}, u32[]{:S(2)}, u32[]{:S(2)}) collective-permute-start(bf16[432,384]{1,0:T(8,128)(2,1)S(1)} %collective-permute-done.14.refs_16_), channel_id=1, source_target_pairs={{0,2},{2,4},{4,6},{6,8},{8,10},{10,12},{12,14},{14,0},{1,15},{3,1}... | collective-permute-start | bytes 995336 | tf_op jit(solution)/shard_map/ppermute | solution.py:143
  54.5 7.5 %collective-permute-start.9 = (bf16[432,384]{1,0:T(8,128)(2,1)S(1)}, bf16[432,384]{1,0:T(8,128)(2,1)S(1)}, u32[]{:S(2)}, u32[]{:S(2)}) collective-permute-start(bf16[432,384]{1,0:T(8,128)(2,1)S(1)} %collective-permute-done.8.refs_9_), channel_id=1, source_target_pairs={{0,2},{2,4},{4,6},{6,8},{8,10},{10,12},{12,14},{14,0},{1,15},{3,1}... | collective-permute-start | bytes 995336 | tf_op jit(solution)/shard_map/ppermute | solution.py:143
  58.5 7.5 %collective-permute-start.16 = (bf16[432,384]{1,0:T(8,128)(2,1)S(1)}, bf16[432,384]{1,0:T(8,128)(2,1)S(1)}, u32[]{:S(2)}, u32[]{:S(2)}) collective-permute-start(bf16[432,384]{1,0:T(8,128)(2,1)S(1)} %collective-permute-done.15.refs_17_), channel_id=1, source_target_pairs={{0,2},{2,4},{4,6},{6,8},{8,10},{10,12},{12,14},{14,0},{1,15},{3,1}... | collective-permute-start | bytes 995336 | tf_op jit(solution)/shard_map/ppermute | solution.py:143
  62.0 9.7 %collective-permute-start.10 = (bf16[432,384]{1,0:T(8,128)(2,1)S(1)}, bf16[432,384]{1,0:T(8,128)(2,1)S(1)}, u32[]{:S(2)}, u32[]{:S(2)}) collective-permute-start(bf16[432,384]{1,0:T(8,128)(2,1)S(1)} %collective-permute-done.9.refs_10_), channel_id=1, source_target_pairs={{0,2},{2,4},{4,6},{6,8},{8,10},{10,12},{12,14},{14,0},{1,15},{3,1}... | collective-permute-start | bytes 995336 | tf_op jit(solution)/shard_map/ppermute | solution.py:143
  65.9 7.5 %collective-permute-start.17 = (bf16[432,384]{1,0:T(8,128)(2,1)S(1)}, bf16[432,384]{1,0:T(8,128)(2,1)S(1)}, u32[]{:S(2)}, u32[]{:S(2)}) collective-permute-start(bf16[432,384]{1,0:T(8,128)(2,1)S(1)} %collective-permute-done.16.refs_18_), channel_id=1, source_target_pairs={{0,2},{2,4},{4,6},{6,8},{8,10},{10,12},{12,14},{14,0},{1,15},{3,1}... | collective-permute-start | bytes 995336 | tf_op jit(solution)/shard_map/ppermute | solution.py:143
  69.3 12.8 %collective-permute-start.3 = (bf16[288,9216]{1,0:T(8,128)(2,1)S(1)}, bf16[288,9216]{1,0:T(8,128)(2,1)S(1)}, u32[]{:S(2)}, u32[]{:S(2)}) collective-permute-start(bf16[288,9216]{1,0:T(8,128)(2,1)S(1)} %bitcast.20), channel_id=1, source_target_pairs={{0,1},{1,0},{2,3},{3,2},{4,5},{5,4},{6,7},{7,6},{8,9},{9,8},{10,11... | collective-permute-start | bytes 15925256 | tf_op jit(solution)/shard_map/ppermute | solution.py:191
  78.0 12.5 %collective-permute-start.18 = (bf16[288,9216]{1,0:T(8,128)(2,1)S(1)}, bf16[288,9216]{1,0:T(8,128)(2,1)}, u32[]{:S(2)}, u32[]{:S(2)}) collective-permute-start(bf16[288,9216]{1,0:T(8,128)(2,1)S(1)} %collective-permute-done.4.refs_2_), channel_id=1, source_target_pairs={{0,1},{1,0},{2,3},{3,2},{4,5},{5,4},{6,7},{7,6},{8,9},{9,8},{10,11... | collective-permute-start | bytes 15925256 | tf_op jit(solution)/shard_map/ppermute | solution.py:191
  115.5 12.8 %collective-permute-start.19 = (f32[2,288,288]{2,1,0:T(8,128)}, f32[2,288,288]{2,1,0:T(8,128)}, u32[]{:S(2)}, u32[]{:S(2)}) collective-permute-start(f32[2,288,288]{2,1,0:T(8,128)} %slice_bitcast_fusion), channel_id=1, source_target_pairs={{0,1},{1,0},{2,3},{3,2},{4,5},{5,4},{6,7},{7,6},{8,9},{9,8},{10,11... | collective-permute-start | bytes 1990664 | tf_op jit(solution)/shard_map/ppermute | solution.py:235
  117.1 37.4 %all-to-all-start = ((f16[256,4,384]{2,1,0:T(4,128)(2,1)}), f16[256,4,384]{2,1,0:T(4,128)(2,1)}, u32[]{:S(2)}, u32[]{:S(2)}) async-start(f16[256,4,384]{2,1,0:T(4,128)(2,1)} %convert_element_type.8), calls=%async_computation | async-start | bytes 1572864 | tf_op jit(solution)/shard_map/all_to_all | solution.py:238
  130.7 26.8 %collective-permute-start.20 = (f32[2,288,288]{2,1,0:T(8,128)}, f32[2,288,288]{2,1,0:T(8,128)}, u32[]{:S(2)}, u32[]{:S(2)}) collective-permute-start(f32[2,288,288]{2,1,0:T(8,128)} %pad_maximum_fusion), channel_id=1, source_target_pairs={{0,16},{16,0},{1,17},{17,1},{2,18},{18,2},{3,19},{19,3},{4,20},{20... | collective-permute-start | bytes 1990664 | tf_op jit(solution)/shard_map/ppermute | solution.py:236
  (8 other events, 102.2 us)

commit v7 on v6

--- a/solution.py
+++ b/solution.py
@@ -46,13 +46,13 @@
 
 
 def product_kernel(place_ref, *refs):
-    t_refs, pieces, refs = refs[:4], refs[4 : 4 + 2 * ZS], refs[4 + 2 * ZS :]
-    row_ref, col_ref, ladder_ref, out_ref, turned_ref, stage_ref, w_ref, sem = refs
+    t_refs, pieces, refs = refs[:6], refs[6 : 6 + 2 * ZS], refs[6 + 2 * ZS :]
+    row_ref, col_ref, ladder_ref, out_ref, acc_ref, turned_ref, stage_ref, w_ref, sem = refs
     step = pl.program_id(0)
 
     @pl.when(step == 0)
     def _():
-        ladder_ref[...] = jnp.zeros_like(ladder_ref)
+        acc_ref[...] = jnp.zeros_like(acc_ref)
         copies = [
             pltpu.make_async_copy(piece, stage_ref.at[n], sem.at[n])
             for n, piece in enumerate(pieces)
@@ -72,14 +72,25 @@
             rest = [stage_ref[n, m * tall : (m + 1) * tall, width:] for m in range(3)]
             w_ref[pl.ds(start + 3 * tall, tall)] = jnp.concatenate(rest, axis=1)
 
-    at = 0
-    for t_ref in t_refs:
-        size = t_ref.shape[0]
-        ladder_ref[at : at + size] += mm(t_ref[...], w_ref[pl.ds(pl.multiple_of(step * CHUNK, CHUNK), CHUNK)])
-        at += size
+    w = w_ref[pl.ds(pl.multiple_of(step * CHUNK, CHUNK), CHUNK)]
+
+    def add(*t_refs):
+        t = jnp.concatenate([t_ref[...] for t_ref in t_refs], axis=0)
+        acc_ref[...] += lax.dot_general(w, t, (((0,), (1,)), ((), ())), preferred_element_type=F32)
+
+    early = step < pl.num_programs(0) // 2
+
+    @pl.when(early)
+    def _():
+        add(*t_refs[:4])
+
+    @pl.when(jnp.logical_not(early))
+    def _():
+        add(*t_refs[:2], *t_refs[4:])
 
     @pl.when(step == pl.num_programs(0) - 1)
     def _():
+        ladder_ref[...] = acc_ref[...].T
         rows = row_ref.shape[0]
         for o in range(4):
             total = 0.0
@@ -128,8 +139,8 @@
             first, jnp.concatenate([x, y], axis=1), jnp.concatenate([y, x], axis=1)
         )
 
-    near = joined(place_ref[1] == 0, own_ref[...], side_ref[...])
-    far = joined(place_ref[1] == 0, far_ref[0], far_ref[1])
+    near = joined(place_ref[1] == 0, own_ref[...], side_ref[0])
+    far = joined(place_ref[1] == 0, far_ref[...], side_ref[1])
     summed = joined(place_ref[2] == 0, near, far) + total * (1 / SCALE)
     col = lax.broadcasted_iota(jnp.int32, summed.shape, 1)
     first = place_ref[0] * SLAB + col // VB
@@ -185,10 +196,15 @@
     ring_near, ring_far = ring(folded(near)), ring(far)
     pieces = ring_near + ring_far
 
-    t, _ = lax.optimization_barrier((amplitudes.reshape(rows, k_all), (far, ring_near[1])))
-    t_x = around(t, ("xh", "xl"), 4)
-    t_x, *_ = lax.optimization_barrier((t_x, ring_near[-1], ring_far[-1]))
-    t_refs = [t, lax.ppermute(t, "c", SWAP), t_x, lax.ppermute(t_x, "c", SWAP)]
+    t = amplitudes.reshape(rows, k_all)
+    t_a, t_b, _ = lax.optimization_barrier(
+        (t[:, : k_all // 2], t[:, k_all // 2 :], (far, ring_near[1]))
+    )
+    x_a, x_b = around(t_a, ("xh", "xl"), 4), around(t_b, ("xh", "xl"), 4)
+    x_a, *_ = lax.optimization_barrier((x_a, ring_near[5], ring_far[4]))
+    x_b, *_ = lax.optimization_barrier((x_b, ring_near[-1], ring_far[-1]))
+    t_c, c_a, c_b = (lax.ppermute(x, "c", SWAP) for x in (t, x_a, x_b))
+    t_refs = [t, t_c, x_a, c_a, x_b, c_b]
 
     out_cols = selector(quarter, lambda r: ((r // SLAB) % GRPS) * PIECE + r // VB * SLAB + r % SLAB)
     in_cols = selector(slab, lambda r: (r % SLAB) * VB + r // SLAB)
@@ -203,12 +219,16 @@
     in_rows = selector(rows, lambda r: r // 48 * 48 + (r // 3 % 2) * 24 + (r % 3) * 8 + r // 6 % ZS)
 
     params = pltpu.CompilerParams(vmem_limit_bytes=48 * 2**20)
+    half = k_all // CHUNK // 2
     fixed = lambda k: (0, 0)
+    full = lambda k: (0, k)
+    early = lambda k: (0, jnp.minimum(k, half - 1))
+    late = lambda k: (0, jnp.maximum(k - half, 0))
     ladder, wire = pl.pallas_call(
         product_kernel,
         grid=(k_all // CHUNK,),
         in_specs=[pl.BlockSpec(memory_space=pltpu.SMEM)]
-        + [pl.BlockSpec((x.shape[0], CHUNK), lambda k: (0, k)) for x in t_refs]
+        + [pl.BlockSpec((rows, CHUNK), chunk) for chunk in (full, full, early, early, late, late)]
         + [pl.BlockSpec(memory_space=pl.ANY)] * len(pieces)
         + [
             pl.BlockSpec((rows, rows), fixed),
@@ -223,6 +243,7 @@
             jax.ShapeDtypeStruct((GRPS * PAIRS, 4, LANES), F32),
         ],
         scratch_shapes=[
+            pltpu.VMEM((quarter, 4 * rows), F32),
             pltpu.VMEM((4, rows, quarter), F32),
             pltpu.VMEM((2 * ZS, *far.shape), BF),
             pltpu.VMEM((k_all, quarter), BF),
@@ -232,8 +253,8 @@
     )(jnp.stack([z, xl, c]), *t_refs, *pieces, out_rows, out_cols)
 
     parts = ladder.reshape(2, 2, rows, quarter)
-    side = lax.ppermute(parts[:, 1], "c", SWAP)
-    fetched = lax.ppermute(jnp.stack([parts[1, 0], side[1]]), "xl", SWAP)
+    fetched = lax.ppermute(parts[1], "xl", SWAP)
+    side = lax.ppermute(jnp.stack([parts[0, 1], fetched[1]]), "c", SWAP)
 
     got = lax.all_to_all(wire.astype(WIRE), ORDER, 0, 0, tiled=True)
     whole = pl.BlockSpec(memory_space=pltpu.VMEM)
@@ -249,8 +270,8 @@
         live_counts,
         got.astype(F32),
         parts[0, 0],
-        side[0],
-        fetched,
+        side,
+        fetched[0],
         in_rows,
         in_cols,
     )

time: 165 us -> 158 us (0.958)
  waiting for transfers between devices: 48.5 us -> 40.5 us
  starting transfers between devices: 72.2 us -> 76.4 us
  Pallas kernels: 28.7 us -> 26.4 us
    all_to_all x1, waiting for transfers between devices: 22.3 us -> 10.4 us  [on_device(): got = lax.all_to_all(wire.astype(WIRE), ORDER, 0, 0, tiled=True)]
    ppermute x4 -> x5, waiting for transfers between devices: 7.76 us -> 13.6 us  [the longest x1 10.6 us: on_device(): fetched = lax.ppermute(parts[1], 'xl', SWAP)]
    ppermute x4 -> x5, starting transfers between devices: 8.22 us -> 11.5 us  [the longest x3 8.23 us: on_device(): t_c, c_a, c_b = (lax.ppermute(x, 'c', SWAP) for x in (t, x_a, x_b))]
    pallas_call x1, Pallas kernels: 22.6 us -> 20.3 us  [on_device(): pl.pallas_call(product_kernel, grid=(k_all // CHUNK,), in_specs=[pl.Block...]
    ppermute x15 -> x16, waiting for transfers between devices: 13.2 us -> 11.6 us  [around(): return lax.ppermute(x, (*axes, 'c'), moves)]
    ppermute x15 -> x16, starting transfers between devices: 49.4 us -> 49.2 us  [around(): return lax.ppermute(x, (*axes, 'c'), moves)]
  transfers between devices with their start and end apart: 22 -> 24, of which waited for: 19 -> 19; matrix products, arithmetic and copies ran while one was open for 3% -> 3% of each run, Pallas kernels for 0% -> 0%
where the time goes in v7:
time: 158 us
  starting transfers between devices  76.4 us (48%)
  waiting for transfers between devices  40.5 us (26%)
  Pallas kernels  26.4 us (17%)
  local copies, waits for them, and re-layouts  7.9 us (5%)
  other arithmetic  6.41 us (4%)
    ppermute x16, starting transfers between devices, around(): return lax.ppermute(x, (*axes, 'c'), moves)  49.2 us
    pallas_call x1, Pallas kernels, on_device(): pl.pallas_call(product_kernel, grid=(k_all // CHUNK,), in_specs=[pl.Block...  20.3 us
    all_to_all x1, starting transfers between devices, on_device(): got = lax.all_to_all(wire.astype(WIRE), ORDER, 0, 0, tiled=True)  12.3 us
    ppermute x16, waiting for transfers between devices, around(): return lax.ppermute(x, (*axes, 'c'), moves)  11.6 us
    ppermute x1, waiting for transfers between devices, on_device(): fetched = lax.ppermute(parts[1], 'xl', SWAP)  10.6 us
    all_to_all x1, waiting for transfers between devices, on_device(): got = lax.all_to_all(wire.astype(WIRE), ORDER, 0, 0, tiled=True)  10.4 us
    ppermute x3, starting transfers between devices, on_device(): t_c, c_a, c_b = (lax.ppermute(x, 'c', SWAP) for x in (t, x_a, x_b))  8.23 us
    pallas_call x1, Pallas kernels, on_device(): pl.pallas_call(unpack_kernel, out_shape=jax.ShapeDtypeStruct((rows, slab)...  6.08 us
  transfers between devices with their start and end apart: 24, of which 19 were waited for; matrix products, arithmetic and copies ran while one was open for 3% of the time, Pallas kernels for 0%

profile of v7, /device:TPU:1, one launch (start us, length us, event | category | flops | bytes accessed | tf_op | source)
XLA Modules:
  0.0 157.8 jit_solution(5215959877017514967)
XLA Ops:
  3.4 3.3 %collective-permute-start.1 = (bf16[576,288]{1,0:T(8,128)(2,1)S(1)}, bf16[576,288]{1,0:T(8,128)(2,1)S(1)}, u32[]{:S(2)}, u32[]{:S(2)}) collective-permute-start(bf16[576,288]{1,0:T(8,128)(2,1)S(1)} %pad_maximum_fusion.1), channel_id=1, source_target_pairs={{0,1},{1,0},{2,3},{3,2},{4,5},{5,4},{6,7},{7,6},{8,9},{9,8},{10,11... | collective-permute-start | bytes 995336 | tf_op jit(solution)/shard_map/ppermute | solution.py:183
  9.1 5.1 %collective-permute-start.3 = (bf16[432,384]{1,0:T(8,128)(2,1)S(1)}, bf16[432,384]{1,0:T(8,128)(2,1)S(1)}, u32[]{:S(2)}, u32[]{:S(2)}) collective-permute-start(bf16[432,384]{1,0:T(8,128)(2,1)S(1)} %maximum_maximum_fusion.1.refs_6_), channel_id=1, source_target_pairs={{0,2},{2,4},{4,6},{6,8},{8,10},{10,12},{12,14},{14,0},{1,15},{3,1}... | collective-permute-start | bytes 995336 | tf_op jit(solution)/shard_map/ppermute | solution.py:154
  14.6 3.4 %collective-permute-done.2.refs_14_ = bf16[432,384]{1,0:T(8,128)(2,1)S(1)} collective-permute-done((bf16[432,384]{1,0:T(8,128)(2,1)S(1)}, bf16[432,384]{1,0:T(8,128)(2,1)S(1)}, u32[]{:S(2)}, u32[]{:S(2)}) %collective-permute-start.2) | collective-permute-done | bytes 331808 | tf_op jit(solution)/shard_map/ppermute | solution.py:195
  23.0 3.1 %collective-permute-start.9 = (bf16[432,384]{1,0:T(8,128)(2,1)S(1)}, bf16[432,384]{1,0:T(8,128)(2,1)S(1)}, u32[]{:S(2)}, u32[]{:S(2)}) collective-permute-start(bf16[432,384]{1,0:T(8,128)(2,1)S(1)} %collective-permute-done.2.refs_14_), channel_id=1, source_target_pairs={{0,2},{2,4},{4,6},{6,8},{8,10},{10,12},{12,14},{14,0},{1,15},{3,1}... | collective-permute-start | bytes 995336 | tf_op jit(solution)/shard_map/ppermute | solution.py:154
  26.8 3.3 %collective-permute-done.9.refs_15_ = bf16[432,384]{1,0:T(8,128)(2,1)S(1)} collective-permute-done((bf16[432,384]{1,0:T(8,128)(2,1)S(1)}, bf16[432,384]{1,0:T(8,128)(2,1)S(1)}, u32[]{:S(2)}, u32[]{:S(2)}) %collective-permute-start.9) | collective-permute-done | bytes 331808 | tf_op jit(solution)/shard_map/ppermute | solution.py:154
  30.1 3.4 %collective-permute-start.10 = (bf16[432,384]{1,0:T(8,128)(2,1)S(1)}, bf16[432,384]{1,0:T(8,128)(2,1)S(1)}, u32[]{:S(2)}, u32[]{:S(2)}) collective-permute-start(bf16[432,384]{1,0:T(8,128)(2,1)S(1)} %collective-permute-done.9.refs_15_), channel_id=1, source_target_pairs={{0,2},{2,4},{4,6},{6,8},{8,10},{10,12},{12,14},{14,0},{1,15},{3,1}... | collective-permute-start | bytes 995336 | tf_op jit(solution)/shard_map/ppermute | solution.py:154
  33.7 3.4 %collective-permute-start.6 = (bf16[432,384]{1,0:T(8,128)(2,1)S(1)}, bf16[432,384]{1,0:T(8,128)(2,1)S(1)}, u32[]{:S(2)}, u32[]{:S(2)}) collective-permute-start(bf16[432,384]{1,0:T(8,128)(2,1)S(1)} %collective-permute-done.5.refs_8_), channel_id=1, source_target_pairs={{0,2},{2,4},{4,6},{6,8},{8,10},{10,12},{12,14},{14,0},{1,15},{3,1}... | collective-permute-start | bytes 995336 | tf_op jit(solution)/shard_map/ppermute | solution.py:154
  37.6 3.4 %collective-permute-start.11 = (bf16[432,384]{1,0:T(8,128)(2,1)S(1)}, bf16[432,384]{1,0:T(8,128)(2,1)S(1)}, u32[]{:S(2)}, u32[]{:S(2)}) collective-permute-start(bf16[432,384]{1,0:T(8,128)(2,1)S(1)} %collective-permute-done.10.refs_16_), channel_id=1, source_target_pairs={{0,2},{2,4},{4,6},{6,8},{8,10},{10,12},{12,14},{14,0},{1,15},{3,1}... | collective-permute-start | bytes 995336 | tf_op jit(solution)/shard_map/ppermute | solution.py:154
  41.2 3.4 %collective-permute-start.7 = (bf16[432,384]{1,0:T(8,128)(2,1)S(1)}, bf16[432,384]{1,0:T(8,128)(2,1)S(1)}, u32[]{:S(2)}, u32[]{:S(2)}) collective-permute-start(bf16[432,384]{1,0:T(8,128)(2,1)S(1)} %collective-permute-done.6.refs_9_), channel_id=1, source_target_pairs={{0,2},{2,4},{4,6},{6,8},{8,10},{10,12},{12,14},{14,0},{1,15},{3,1}... | collective-permute-start | bytes 995336 | tf_op jit(solution)/shard_map/ppermute | solution.py:154
  45.1 3.4 %collective-permute-start.12 = (bf16[432,384]{1,0:T(8,128)(2,1)S(1)}, bf16[432,384]{1,0:T(8,128)(2,1)S(1)}, u32[]{:S(2)}, u32[]{:S(2)}) collective-permute-start(bf16[432,384]{1,0:T(8,128)(2,1)S(1)} %collective-permute-done.11.refs_17_), channel_id=1, source_target_pairs={{0,2},{2,4},{4,6},{6,8},{8,10},{10,12},{12,14},{14,0},{1,15},{3,1}... | collective-permute-start | bytes 995336 | tf_op jit(solution)/shard_map/ppermute | solution.py:154
  48.6 3.4 %collective-permute-start.8 = (bf16[432,384]{1,0:T(8,128)(2,1)S(1)}, bf16[432,384]{1,0:T(8,128)(2,1)S(1)}, u32[]{:S(2)}, u32[]{:S(2)}) collective-permute-start(bf16[432,384]{1,0:T(8,128)(2,1)S(1)} %collective-permute-done.7.refs_10_), channel_id=1, source_target_pairs={{0,2},{2,4},{4,6},{6,8},{8,10},{10,12},{12,14},{14,0},{1,15},{3,1}... | collective-permute-start | bytes 995336 | tf_op jit(solution)/shard_map/ppermute | solution.py:154
  52.5 3.4 %collective-permute-start.17 = (bf16[432,384]{1,0:T(8,128)(2,1)S(1)}, bf16[432,384]{1,0:T(8,128)(2,1)S(1)}, u32[]{:S(2)}, u32[]{:S(2)}) collective-permute-start(bf16[432,384]{1,0:T(8,128)(2,1)S(1)} %collective-permute-done.12.refs_18_), channel_id=1, source_target_pairs={{0,2},{2,4},{4,6},{6,8},{8,10},{10,12},{12,14},{14,0},{1,15},{3,1}... | collective-permute-start | bytes 995336 | tf_op jit(solution)/shard_map/ppermute | solution.py:154
  56.1 3.4 %collective-permute-start.15 = (bf16[432,384]{1,0:T(8,128)(2,1)S(1)}, bf16[432,384]{1,0:T(8,128)(2,1)S(1)}, u32[]{:S(2)}, u32[]{:S(2)}) collective-permute-start(bf16[432,384]{1,0:T(8,128)(2,1)S(1)} %collective-permute-done.8.refs_11_), channel_id=1, source_target_pairs={{0,2},{2,4},{4,6},{6,8},{8,10},{10,12},{12,14},{14,0},{1,15},{3,1}... | collective-permute-start | bytes 995336 | tf_op jit(solution)/shard_map/ppermute | solution.py:154
  60.0 3.4 %collective-permute-start.18 = (bf16[432,384]{1,0:T(8,128)(2,1)S(1)}, bf16[432,384]{1,0:T(8,128)(2,1)S(1)}, u32[]{:S(2)}, u32[]{:S(2)}) collective-permute-start(bf16[432,384]{1,0:T(8,128)(2,1)S(1)} %collective-permute-done.17.refs_19_), channel_id=1, source_target_pairs={{0,2},{2,4},{4,6},{6,8},{8,10},{10,12},{12,14},{14,0},{1,15},{3,1}... | collective-permute-start | bytes 995336 | tf_op jit(solution)/shard_map/ppermute | solution.py:154
  63.6 3.4 %collective-permute-start.16 = (bf16[432,384]{1,0:T(8,128)(2,1)S(1)}, bf16[432,384]{1,0:T(8,128)(2,1)S(1)}, u32[]{:S(2)}, u32[]{:S(2)}) collective-permute-start(bf16[432,384]{1,0:T(8,128)(2,1)S(1)} %collective-permute-done.15.refs_12_), channel_id=1, source_target_pairs={{0,2},{2,4},{4,6},{6,8},{8,10},{10,12},{12,14},{14,0},{1,15},{3,1}... | collective-permute-start | bytes 995336 | tf_op jit(solution)/shard_map/ppermute | solution.py:154
  67.5 3.4 %collective-permute-start.19 = (bf16[432,384]{1,0:T(8,128)(2,1)S(1)}, bf16[432,384]{1,0:T(8,128)(2,1)S(1)}, u32[]{:S(2)}, u32[]{:S(2)}) collective-permute-start(bf16[432,384]{1,0:T(8,128)(2,1)S(1)} %collective-permute-done.18.refs_20_), channel_id=1, source_target_pairs={{0,2},{2,4},{4,6},{6,8},{8,10},{10,12},{12,14},{14,0},{1,15},{3,1}... | collective-permute-start | bytes 995336 | tf_op jit(solution)/shard_map/ppermute | solution.py:154
  75.0 2.9 %collective-permute-done.14.refs_4_ = bf16[288,4608]{1,0:T(8,128)(2,1)S(1)} collective-permute-done((bf16[288,4608]{1,0:T(8,128)(2,1)S(1)}, bf16[288,4608]{1,0:T(8,128)(2,1)S(1)}, u32[]{:S(2)}, u32[]{:S(2)}) %collective-permute-start.14) | collective-permute-done | bytes 2654240 | tf_op jit(solution)/shard_map/ppermute | solution.py:154
  77.9 4.0 %collective-permute-start.20 = (bf16[288,4608]{1,0:T(8,128)(2,1)S(1)}, bf16[288,4608]{1,0:T(8,128)(2,1)}, u32[]{:S(2)}, u32[]{:S(2)}) collective-permute-start(bf16[288,4608]{1,0:T(8,128)(2,1)S(1)} %collective-permute-done.14.refs_4_), channel_id=1, source_target_pairs={{0,1},{1,0},{2,3},{3,2},{4,5},{5,4},{6,7},{7,6},{8,9},{9,8},{10,11... | collective-permute-start | bytes 7962632 | tf_op jit(solution)/shard_map/ppermute | solution.py:206
  83.6 3.1 %collective-permute-done.20.refs_5_ = bf16[288,4608]{1,0:T(8,128)(2,1)} collective-permute-done((bf16[288,4608]{1,0:T(8,128)(2,1)S(1)}, bf16[288,4608]{1,0:T(8,128)(2,1)}, u32[]{:S(2)}, u32[]{:S(2)}) %collective-permute-start.20) | collective-permute-done | bytes 2654240 | tf_op jit(solution)/shard_map/ppermute | solution.py:206
  86.7 20.3 %shard_map.73 = (f32[1152,288]{1,0:T(8,128)}, f32[256,4,384]{2,1,0:T(4,128)}) custom-call(s32[3]{0:T(128)S(1)} %pad_add_fusion.1.place_ref, bf16[288,9216]{1,0:T(8,128)(2,1)} %bitcast.15, bf16[288,9216]{1,0:T(8,128)(2,1)} %copy-done.6, bf16[288,4608]{1,0:T(8,128)(2,1)} %copy-done.7, bf16[288,4608]{1,0:T(8,128)(2,1)} %copy-done.9, ...), custom_call_target="tpu_custom_call" | custom-call | tf_op jit(solution)/shard_map/pallas_call | solution.py:227
  110.8 12.3 %all-to-all-start = ((f16[256,4,384]{2,1,0:T(4,128)(2,1)}), f16[256,4,384]{2,1,0:T(4,128)(2,1)}, u32[]{:S(2)}, u32[]{:S(2)}) async-start(f16[256,4,384]{2,1,0:T(4,128)(2,1)} %convert_element_type.8), calls=%async_computation | async-start | bytes 1572864 | tf_op jit(solution)/shard_map/all_to_all | solution.py:259
  123.2 10.6 %collective-permute-done.21 = f32[2,288,288]{2,1,0:T(8,128)} collective-permute-done((f32[2,288,288]{2,1,0:T(8,128)}, f32[2,288,288]{2,1,0:T(8,128)}, u32[]{:S(2)}, u32[]{:S(2)}) %collective-permute-start.21) | collective-permute-done | bytes 663584 | tf_op jit(solution)/shard_map/ppermute | solution.py:256
  138.9 10.4 %all-to-all-done = f16[256,4,384]{2,1,0:T(4,128)(2,1)} async-done(((f16[256,4,384]{2,1,0:T(4,128)(2,1)}), f16[256,4,384]{2,1,0:T(4,128)(2,1)}, u32[]{:S(2)}, u32[]{:S(2)}) %all-to-all-start) | async-done | bytes 786464 | tf_op jit(solution)/shard_map/all_to_all | solution.py:259
  151.7 6.1 %shard_map.74 = bf16[288,1152]{1,0:T(8,128)(2,1)} custom-call(s32[3]{0:T(128)S(1)} %pad_add_fusion.place_ref, s32[2]{0:T(128)S(1)} %copy-done.4, f32[256,4,384]{2,1,0:T(4,128)S(1)} %convert_element_type.9.got_ref, f32[288,288]{1,0:T(8,128)S(1)} %get-tuple-element.20.own_ref, f32[2,288,288]{2,1,0:T(8,128)} %collective-permute-done.22.side_ref, ...), custom_call_target="tpu_custom_call" | custom-call | tf_op jit(solution)/shard_map/pallas_call | solution.py:262
  (72 shorter events, 32.1 us)
Async XLA Ops:
  3.4 4.7 %collective-permute-start.1 = (bf16[576,288]{1,0:T(8,128)(2,1)S(1)}, bf16[576,288]{1,0:T(8,128)(2,1)S(1)}, u32[]{:S(2)}, u32[]{:S(2)}) collective-permute-start(bf16[576,288]{1,0:T(8,128)(2,1)S(1)} %pad_maximum_fusion.1), channel_id=1, source_target_pairs={{0,1},{1,0},{2,3},{3,2},{4,5},{5,4},{6,7},{7,6},{8,9},{9,8},{10,11... | collective-permute-start | bytes 995336 | tf_op jit(solution)/shard_map/ppermute | solution.py:183
  8.9 9.1 %collective-permute-start.2 = (bf16[432,384]{1,0:T(8,128)(2,1)S(1)}, bf16[432,384]{1,0:T(8,128)(2,1)S(1)}, u32[]{:S(2)}, u32[]{:S(2)}) collective-permute-start(bf16[432,384]{1,0:T(8,128)(2,1)S(1)} %maximum_maximum_fusion), channel_id=1, source_target_pairs={{0,16},{16,0},{1,17},{17,1},{2,18},{18,2},{3,19},{19,3},{4,20},{20... | collective-permute-start | bytes 995336 | tf_op jit(solution)/shard_map/ppermute | solution.py:195
  9.1 9.2 %collective-permute-start.3 = (bf16[432,384]{1,0:T(8,128)(2,1)S(1)}, bf16[432,384]{1,0:T(8,128)(2,1)S(1)}, u32[]{:S(2)}, u32[]{:S(2)}) collective-permute-start(bf16[432,384]{1,0:T(8,128)(2,1)S(1)} %maximum_maximum_fusion.1.refs_6_), channel_id=1, source_target_pairs={{0,2},{2,4},{4,6},{6,8},{8,10},{10,12},{12,14},{14,0},{1,15},{3,1}... | collective-permute-start | bytes 995336 | tf_op jit(solution)/shard_map/ppermute | solution.py:154
  18.3 52.6 %collective-permute-start.4 = (bf16[288,4608]{1,0:T(8,128)(2,1)S(1)}, bf16[288,4608]{1,0:T(8,128)(2,1)S(1)}, u32[]{:S(2)}, u32[]{:S(2)}) collective-permute-start(bf16[288,4608]{1,0:T(8,128)(2,1)S(1)} %get-tuple-element.11), channel_id=1, source_target_pairs={{0,16},{16,32},{32,48},{48,0},{1,49},{17,1},{33,17},{49,33},{2,18}... | collective-permute-start | bytes 7962632 | tf_op jit(solution)/shard_map/ppermute | solution.py:154
  20.1 57.8 %collective-permute-start.14 = (bf16[288,4608]{1,0:T(8,128)(2,1)S(1)}, bf16[288,4608]{1,0:T(8,128)(2,1)S(1)}, u32[]{:S(2)}, u32[]{:S(2)}) collective-permute-start(bf16[288,4608]{1,0:T(8,128)(2,1)S(1)} %get-tuple-element.13), channel_id=1, source_target_pairs={{0,16},{16,32},{32,48},{48,0},{1,49},{17,1},{33,17},{49,33},{2,18}... | collective-permute-start | bytes 7962632 | tf_op jit(solution)/shard_map/ppermute | solution.py:154
  21.1 61.0 %collective-permute-start = (bf16[288,9216]{1,0:T(8,128)(2,1)S(1)}, bf16[288,9216]{1,0:T(8,128)(2,1)S(1)}, u32[]{:S(2)}, u32[]{:S(2)}) collective-permute-start(bf16[288,9216]{1,0:T(8,128)(2,1)S(1)} %bitcast.17), channel_id=1, source_target_pairs={{0,1},{1,0},{2,3},{3,2},{4,5},{5,4},{6,7},{7,6},{8,9},{9,8},{10,11... | collective-permute-start | bytes 15925256 | tf_op jit(solution)/shard_map/ppermute | solution.py:206
  23.0 7.1 %collective-permute-start.9 = (bf16[432,384]{1,0:T(8,128)(2,1)S(1)}, bf16[432,384]{1,0:T(8,128)(2,1)S(1)}, u32[]{:S(2)}, u32[]{:S(2)}) collective-permute-start(bf16[432,384]{1,0:T(8,128)(2,1)S(1)} %collective-permute-done.2.refs_14_), channel_id=1, source_target_pairs={{0,2},{2,4},{4,6},{6,8},{8,10},{10,12},{12,14},{14,0},{1,15},{3,1}... | collective-permute-start | bytes 995336 | tf_op jit(solution)/shard_map/ppermute | solution.py:154
  26.1 7.6 %collective-permute-start.5 = (bf16[432,384]{1,0:T(8,128)(2,1)S(1)}, bf16[432,384]{1,0:T(8,128)(2,1)S(1)}, u32[]{:S(2)}, u32[]{:S(2)}) collective-permute-start(bf16[432,384]{1,0:T(8,128)(2,1)S(1)} %collective-permute-done.3.refs_7_), channel_id=1, source_target_pairs={{0,2},{2,4},{4,6},{6,8},{8,10},{10,12},{12,14},{14,0},{1,15},{3,1}... | collective-permute-start | bytes 995336 | tf_op jit(solution)/shard_map/ppermute | solution.py:154
  30.1 7.5 %collective-permute-start.10 = (bf16[432,384]{1,0:T(8,128)(2,1)S(1)}, bf16[432,384]{1,0:T(8,128)(2,1)S(1)}, u32[]{:S(2)}, u32[]{:S(2)}) collective-permute-start(bf16[432,384]{1,0:T(8,128)(2,1)S(1)} %collective-permute-done.9.refs_15_), channel_id=1, source_target_pairs={{0,2},{2,4},{4,6},{6,8},{8,10},{10,12},{12,14},{14,0},{1,15},{3,1}... | collective-permute-start | bytes 995336 | tf_op jit(solution)/shard_map/ppermute | solution.py:154
  33.7 7.5 %collective-permute-start.6 = (bf16[432,384]{1,0:T(8,128)(2,1)S(1)}, bf16[432,384]{1,0:T(8,128)(2,1)S(1)}, u32[]{:S(2)}, u32[]{:S(2)}) collective-permute-start(bf16[432,384]{1,0:T(8,128)(2,1)S(1)} %collective-permute-done.5.refs_8_), channel_id=1, source_target_pairs={{0,2},{2,4},{4,6},{6,8},{8,10},{10,12},{12,14},{14,0},{1,15},{3,1}... | collective-permute-start | bytes 995336 | tf_op jit(solution)/shard_map/ppermute | solution.py:154
  37.6 7.5 %collective-permute-start.11 = (bf16[432,384]{1,0:T(8,128)(2,1)S(1)}, bf16[432,384]{1,0:T(8,128)(2,1)S(1)}, u32[]{:S(2)}, u32[]{:S(2)}) collective-permute-start(bf16[432,384]{1,0:T(8,128)(2,1)S(1)} %collective-permute-done.10.refs_16_), channel_id=1, source_target_pairs={{0,2},{2,4},{4,6},{6,8},{8,10},{10,12},{12,14},{14,0},{1,15},{3,1}... | collective-permute-start | bytes 995336 | tf_op jit(solution)/shard_map/ppermute | solution.py:154
  41.2 7.5 %collective-permute-start.7 = (bf16[432,384]{1,0:T(8,128)(2,1)S(1)}, bf16[432,384]{1,0:T(8,128)(2,1)S(1)}, u32[]{:S(2)}, u32[]{:S(2)}) collective-permute-start(bf16[432,384]{1,0:T(8,128)(2,1)S(1)} %collective-permute-done.6.refs_9_), channel_id=1, source_target_pairs={{0,2},{2,4},{4,6},{6,8},{8,10},{10,12},{12,14},{14,0},{1,15},{3,1}... | collective-permute-start | bytes 995336 | tf_op jit(solution)/shard_map/ppermute | solution.py:154
  45.1 7.5 %collective-permute-start.12 = (bf16[432,384]{1,0:T(8,128)(2,1)S(1)}, bf16[432,384]{1,0:T(8,128)(2,1)S(1)}, u32[]{:S(2)}, u32[]{:S(2)}) collective-permute-start(bf16[432,384]{1,0:T(8,128)(2,1)S(1)} %collective-permute-done.11.refs_17_), channel_id=1, source_target_pairs={{0,2},{2,4},{4,6},{6,8},{8,10},{10,12},{12,14},{14,0},{1,15},{3,1}... | collective-permute-start | bytes 995336 | tf_op jit(solution)/shard_map/ppermute | solution.py:154
  48.6 7.5 %collective-permute-start.8 = (bf16[432,384]{1,0:T(8,128)(2,1)S(1)}, bf16[432,384]{1,0:T(8,128)(2,1)S(1)}, u32[]{:S(2)}, u32[]{:S(2)}) collective-permute-start(bf16[432,384]{1,0:T(8,128)(2,1)S(1)} %collective-permute-done.7.refs_10_), channel_id=1, source_target_pairs={{0,2},{2,4},{4,6},{6,8},{8,10},{10,12},{12,14},{14,0},{1,15},{3,1}... | collective-permute-start | bytes 995336 | tf_op jit(solution)/shard_map/ppermute | solution.py:154
  52.5 7.5 %collective-permute-start.17 = (bf16[432,384]{1,0:T(8,128)(2,1)S(1)}, bf16[432,384]{1,0:T(8,128)(2,1)S(1)}, u32[]{:S(2)}, u32[]{:S(2)}) collective-permute-start(bf16[432,384]{1,0:T(8,128)(2,1)S(1)} %collective-permute-done.12.refs_18_), channel_id=1, source_target_pairs={{0,2},{2,4},{4,6},{6,8},{8,10},{10,12},{12,14},{14,0},{1,15},{3,1}... | collective-permute-start | bytes 995336 | tf_op jit(solution)/shard_map/ppermute | solution.py:154
  56.1 7.5 %collective-permute-start.15 = (bf16[432,384]{1,0:T(8,128)(2,1)S(1)}, bf16[432,384]{1,0:T(8,128)(2,1)S(1)}, u32[]{:S(2)}, u32[]{:S(2)}) collective-permute-start(bf16[432,384]{1,0:T(8,128)(2,1)S(1)} %collective-permute-done.8.refs_11_), channel_id=1, source_target_pairs={{0,2},{2,4},{4,6},{6,8},{8,10},{10,12},{12,14},{14,0},{1,15},{3,1}... | collective-permute-start | bytes 995336 | tf_op jit(solution)/shard_map/ppermute | solution.py:154
  60.0 7.5 %collective-permute-start.18 = (bf16[432,384]{1,0:T(8,128)(2,1)S(1)}, bf16[432,384]{1,0:T(8,128)(2,1)S(1)}, u32[]{:S(2)}, u32[]{:S(2)}) collective-permute-start(bf16[432,384]{1,0:T(8,128)(2,1)S(1)} %collective-permute-done.17.refs_19_), channel_id=1, source_target_pairs={{0,2},{2,4},{4,6},{6,8},{8,10},{10,12},{12,14},{14,0},{1,15},{3,1}... | collective-permute-start | bytes 995336 | tf_op jit(solution)/shard_map/ppermute | solution.py:154
  63.6 9.6 %collective-permute-start.16 = (bf16[432,384]{1,0:T(8,128)(2,1)S(1)}, bf16[432,384]{1,0:T(8,128)(2,1)S(1)}, u32[]{:S(2)}, u32[]{:S(2)}) collective-permute-start(bf16[432,384]{1,0:T(8,128)(2,1)S(1)} %collective-permute-done.15.refs_12_), channel_id=1, source_target_pairs={{0,2},{2,4},{4,6},{6,8},{8,10},{10,12},{12,14},{14,0},{1,15},{3,1}... | collective-permute-start | bytes 995336 | tf_op jit(solution)/shard_map/ppermute | solution.py:154
  67.5 7.5 %collective-permute-start.19 = (bf16[432,384]{1,0:T(8,128)(2,1)S(1)}, bf16[432,384]{1,0:T(8,128)(2,1)S(1)}, u32[]{:S(2)}, u32[]{:S(2)}) collective-permute-start(bf16[432,384]{1,0:T(8,128)(2,1)S(1)} %collective-permute-done.18.refs_20_), channel_id=1, source_target_pairs={{0,2},{2,4},{4,6},{6,8},{8,10},{10,12},{12,14},{14,0},{1,15},{3,1}... | collective-permute-start | bytes 995336 | tf_op jit(solution)/shard_map/ppermute | solution.py:154
  70.9 11.1 %collective-permute-start.13 = (bf16[288,4608]{1,0:T(8,128)(2,1)S(1)}, bf16[288,4608]{1,0:T(8,128)(2,1)S(1)}, u32[]{:S(2)}, u32[]{:S(2)}) collective-permute-start(bf16[288,4608]{1,0:T(8,128)(2,1)S(1)} %collective-permute-done.4.refs_2_), channel_id=1, source_target_pairs={{0,1},{1,0},{2,3},{3,2},{4,5},{5,4},{6,7},{7,6},{8,9},{9,8},{10,11... | collective-permute-start | bytes 7962632 | tf_op jit(solution)/shard_map/ppermute | solution.py:206
  77.9 8.7 %collective-permute-start.20 = (bf16[288,4608]{1,0:T(8,128)(2,1)S(1)}, bf16[288,4608]{1,0:T(8,128)(2,1)}, u32[]{:S(2)}, u32[]{:S(2)}) collective-permute-start(bf16[288,4608]{1,0:T(8,128)(2,1)S(1)} %collective-permute-done.14.refs_4_), channel_id=1, source_target_pairs={{0,1},{1,0},{2,3},{3,2},{4,5},{5,4},{6,7},{7,6},{8,9},{9,8},{10,11... | collective-permute-start | bytes 7962632 | tf_op jit(solution)/shard_map/ppermute | solution.py:206
  109.3 24.5 %collective-permute-start.21 = (f32[2,288,288]{2,1,0:T(8,128)}, f32[2,288,288]{2,1,0:T(8,128)}, u32[]{:S(2)}, u32[]{:S(2)}) collective-permute-start(f32[2,288,288]{2,1,0:T(8,128)} %bitcast.9), channel_id=1, source_target_pairs={{0,16},{16,0},{1,17},{17,1},{2,18},{18,2},{3,19},{19,3},{4,20},{20... | collective-permute-start | bytes 1990664 | tf_op jit(solution)/shard_map/ppermute | solution.py:256
  110.8 38.5 %all-to-all-start = ((f16[256,4,384]{2,1,0:T(4,128)(2,1)}), f16[256,4,384]{2,1,0:T(4,128)(2,1)}, u32[]{:S(2)}, u32[]{:S(2)}) async-start(f16[256,4,384]{2,1,0:T(4,128)(2,1)} %convert_element_type.8), calls=%async_computation | async-start | bytes 1572864 | tf_op jit(solution)/shard_map/all_to_all | solution.py:259
  135.9 14.8 %collective-permute-start.22 = (f32[2,288,288]{2,1,0:T(8,128)}, f32[2,288,288]{2,1,0:T(8,128)}, u32[]{:S(2)}, u32[]{:S(2)}) collective-permute-start(f32[2,288,288]{2,1,0:T(8,128)} %pad_maximum_fusion), channel_id=1, source_target_pairs={{0,1},{1,0},{2,3},{3,2},{4,5},{5,4},{6,7},{7,6},{8,9},{9,8},{10,11... | collective-permute-start | bytes 1990664 | tf_op jit(solution)/shard_map/ppermute | solution.py:257
  (12 other events, 247.3 us)

commit v8 on v7

--- a/solution.py
+++ b/solution.py
@@ -15,7 +15,7 @@
 SLAB = VB // GRPS
 PIECE = SLAB // 4 * SLAB
 LANES = 384
-CHUNK = 2304
+CHUNK = 1152
 WIRE = jnp.float16
 SCALE = 16.0
 BF, F32 = jnp.bfloat16, jnp.float32
@@ -47,7 +47,7 @@
 
 def product_kernel(place_ref, *refs):
     t_refs, pieces, refs = refs[:6], refs[6 : 6 + 2 * ZS], refs[6 + 2 * ZS :]
-    row_ref, col_ref, ladder_ref, out_ref, acc_ref, turned_ref, stage_ref, w_ref, sem = refs
+    row_ref, col_ref, near_ref, far_ref, out_ref, acc_ref, turned_ref, stage_ref, w_ref, sem = refs
     step = pl.program_id(0)
 
     @pl.when(step == 0)
@@ -72,6 +72,7 @@
             rest = [stage_ref[n, m * tall : (m + 1) * tall, width:] for m in range(3)]
             w_ref[pl.ds(start + 3 * tall, tall)] = jnp.concatenate(rest, axis=1)
 
+    size = row_ref.shape[0]
     w = w_ref[pl.ds(pl.multiple_of(step * CHUNK, CHUNK), CHUNK)]
 
     def add(*t_refs):
@@ -90,11 +91,11 @@
 
     @pl.when(step == pl.num_programs(0) - 1)
     def _():
-        ladder_ref[...] = acc_ref[...].T
-        rows = row_ref.shape[0]
+        ladder = acc_ref[...].T
+        near_ref[...], far_ref[...] = ladder[: 2 * size], ladder[2 * size :]
         for o in range(4):
             total = 0.0
-            for part in halves(ladder_ref[o * rows : (o + 1) * rows] * SCALE):
+            for part in halves(ladder[o * size : (o + 1) * size] * SCALE):
                 total += mm(mm(row_ref[...], part).astype(BF), col_ref[...])
             turned_ref[o] = total
         fill = jnp.zeros((PAIRS, LANES - OCC * OCC * PIECE), F32)
@@ -166,13 +167,9 @@
     shard, slab = integrals.shape
     rows, quarter = occ * nocc, slab // 4
     xl, z, c = lax.axis_index("xl"), lax.axis_index("z"), lax.axis_index("c")
-    pair = (xl * ZS + z) * 2 + c
     grp = lax.axis_index("y") * 2 + lax.axis_index("xh")
 
-    at = pair * shard + jnp.arange(shard)
-    live = (at // VB < live_counts[1]) & (at % VB < live_counts[1])
-    w = jnp.where(live[:, None], integrals, 0)
-    cols = [w[:, n * quarter : (n + 1) * quarter] for n in range(4)]
+    cols = [integrals[:, n * quarter : (n + 1) * quarter] for n in range(4)]
     first = c == 0
     w_keep = jnp.concatenate(
         [jnp.where(first, cols[0], cols[1]), jnp.where(first, cols[2], cols[3])], axis=0
@@ -181,16 +178,17 @@
         [jnp.where(first, cols[1], cols[0]), jnp.where(first, cols[3], cols[2])], axis=0
     )
     w_side = lax.ppermute(w_send, "c", SWAP)
+    at = (xl * ZS + z) * 2 * shard + jnp.arange(2 * shard)
+    live = ((at // VB < live_counts[1]) & (at % VB < live_counts[1]))[:, None]
     both = []
     for n in range(2):
         keep, side = w_keep[n * shard : (n + 1) * shard], w_side[n * shard : (n + 1) * shard]
-        both.append(
-            jnp.where(
-                first,
-                jnp.concatenate([keep, side], axis=0),
-                jnp.concatenate([side, keep], axis=0),
-            )
+        stacked = jnp.where(
+            first,
+            jnp.concatenate([keep, side], axis=0),
+            jnp.concatenate([side, keep], axis=0),
         )
+        both.append(jnp.where(live, stacked, 0))
     near = jnp.where(xl == 0, both[0], both[1])
     far = lax.ppermute(folded(jnp.where(xl == 0, both[1], both[0])), "xl", SWAP)
     ring_near, ring_far = ring(folded(near)), ring(far)
@@ -218,13 +216,13 @@
     )
     in_rows = selector(rows, lambda r: r // 48 * 48 + (r // 3 % 2) * 24 + (r % 3) * 8 + r // 6 % ZS)
 
-    params = pltpu.CompilerParams(vmem_limit_bytes=48 * 2**20)
+    params = pltpu.CompilerParams(vmem_limit_bytes=34 * 2**20)
     half = k_all // CHUNK // 2
     fixed = lambda k: (0, 0)
     full = lambda k: (0, k)
     early = lambda k: (0, jnp.minimum(k, half - 1))
     late = lambda k: (0, jnp.maximum(k - half, 0))
-    ladder, wire = pl.pallas_call(
+    p_near, p_far, wire = pl.pallas_call(
         product_kernel,
         grid=(k_all // CHUNK,),
         in_specs=[pl.BlockSpec(memory_space=pltpu.SMEM)]
@@ -235,11 +233,13 @@
             pl.BlockSpec((quarter, quarter), fixed),
         ],
         out_specs=[
-            pl.BlockSpec((4 * rows, quarter), fixed),
+            pl.BlockSpec((2 * rows, quarter), fixed),
+            pl.BlockSpec((2 * rows, quarter), fixed),
             pl.BlockSpec((GRPS * PAIRS, 4, LANES), lambda k: (0, 0, 0)),
         ],
         out_shape=[
-            jax.ShapeDtypeStruct((4 * rows, quarter), F32),
+            jax.ShapeDtypeStruct((2 * rows, quarter), F32),
+            jax.ShapeDtypeStruct((2 * rows, quarter), F32),
             jax.ShapeDtypeStruct((GRPS * PAIRS, 4, LANES), F32),
         ],
         scratch_shapes=[
@@ -252,9 +252,8 @@
         compiler_params=params,
     )(jnp.stack([z, xl, c]), *t_refs, *pieces, out_rows, out_cols)
 
-    parts = ladder.reshape(2, 2, rows, quarter)
-    fetched = lax.ppermute(parts[1], "xl", SWAP)
-    side = lax.ppermute(jnp.stack([parts[0, 1], fetched[1]]), "c", SWAP)
+    fetched = lax.ppermute(p_far, "xl", SWAP)
+    side = lax.ppermute(jnp.stack([p_near[rows:], fetched[rows:]]), "c", SWAP)
 
     got = lax.all_to_all(wire.astype(WIRE), ORDER, 0, 0, tiled=True)
     whole = pl.BlockSpec(memory_space=pltpu.VMEM)
@@ -269,9 +268,9 @@
         jnp.stack([grp, c, xl]),
         live_counts,
         got.astype(F32),
-        parts[0, 0],
+        p_near[:rows],
         side,
-        fetched[0],
+        fetched[:rows],
         in_rows,
         in_cols,
     )

time: 158 us -> 153 us (0.968)
  waiting for transfers between devices: 40.5 us -> 36.5 us
  Pallas kernels: 26.4 us -> 24.6 us
    ppermute x2, waiting for transfers between devices: 10.6 us -> 4.89 us  [the longest x1 4.89 us: on_device(): fetched = lax.ppermute(p_far, 'xl', SWAP)]
    pallas_call x1, Pallas kernels: 20.3 us -> 18.5 us  [on_device(): pl.pallas_call(product_kernel, grid=(k_all // CHUNK,), in_specs=[pl.Block...]
  transfers between devices with their start and end apart: 24 -> 24, of which waited for: 19 -> 19; matrix products, arithmetic and copies ran while one was open for 3% -> 7% of each run, Pallas kernels for 0% -> 0%
where the time goes in v8:
time: 153 us
  starting transfers between devices  76.3 us (50%)
  waiting for transfers between devices  36.5 us (24%)
  Pallas kernels  24.6 us (16%)
  local copies, waits for them, and re-layouts  7.74 us (5%)
  other arithmetic  7.65 us (5%)
    ppermute x16, starting transfers between devices, around(): return lax.ppermute(x, (*axes, 'c'), moves)  49.2 us
    pallas_call x1, Pallas kernels, on_device(): pl.pallas_call(product_kernel, grid=(k_all // CHUNK,), in_specs=[pl.Block...  18.5 us
    all_to_all x1, starting transfers between devices, on_device(): got = lax.all_to_all(wire.astype(WIRE), ORDER, 0, 0, tiled=True)  12.2 us
    all_to_all x1, waiting for transfers between devices, on_device(): got = lax.all_to_all(wire.astype(WIRE), ORDER, 0, 0, tiled=True)  11.9 us
    ppermute x16, waiting for transfers between devices, around(): return lax.ppermute(x, (*axes, 'c'), moves)  11.7 us
    ppermute x3, starting transfers between devices, on_device(): t_c, c_a, c_b = (lax.ppermute(x, 'c', SWAP) for x in (t, x_a, x_b))  8.14 us
    pallas_call x1, Pallas kernels, on_device(): pl.pallas_call(unpack_kernel, out_shape=jax.ShapeDtypeStruct((rows, slab)...  6.09 us
    ppermute x1, waiting for transfers between devices, on_device(): fetched = lax.ppermute(p_far, 'xl', SWAP)  4.89 us
  transfers between devices with their start and end apart: 24, of which 19 were waited for; matrix products, arithmetic and copies ran while one was open for 7% of the time, Pallas kernels for 0%

profile of v8, /device:TPU:1, one launch (start us, length us, event | category | flops | bytes accessed | tf_op | source)
XLA Modules:
  0.0 153.0 jit_solution(2357006490436907580)
XLA Ops:
  1.6 3.3 %collective-permute-start.1 = (bf16[576,288]{1,0:T(8,128)(2,1)S(1)}, bf16[576,288]{1,0:T(8,128)(2,1)S(1)}, u32[]{:S(2)}, u32[]{:S(2)}) collective-permute-start(bf16[576,288]{1,0:T(8,128)(2,1)S(1)} %pad_maximum_fusion.1), channel_id=1, source_target_pairs={{0,1},{1,0},{2,3},{3,2},{4,5},{5,4},{6,7},{7,6},{8,9},{9,8},{10,11... | collective-permute-start | bytes 995336 | tf_op jit(solution)/shard_map/ppermute | solution.py:180
  7.4 5.1 %collective-permute-start.3 = (bf16[432,384]{1,0:T(8,128)(2,1)S(1)}, bf16[432,384]{1,0:T(8,128)(2,1)S(1)}, u32[]{:S(2)}, u32[]{:S(2)}) collective-permute-start(bf16[432,384]{1,0:T(8,128)(2,1)S(1)} %maximum_maximum_fusion.1.refs_6_), channel_id=1, source_target_pairs={{0,2},{2,4},{4,6},{6,8},{8,10},{10,12},{12,14},{14,0},{1,15},{3,1}... | collective-permute-start | bytes 995336 | tf_op jit(solution)/shard_map/ppermute | solution.py:155
  12.9 3.4 %collective-permute-done.2.refs_14_ = bf16[432,384]{1,0:T(8,128)(2,1)S(1)} collective-permute-done((bf16[432,384]{1,0:T(8,128)(2,1)S(1)}, bf16[432,384]{1,0:T(8,128)(2,1)S(1)}, u32[]{:S(2)}, u32[]{:S(2)}) %collective-permute-start.2) | collective-permute-done | bytes 331808 | tf_op jit(solution)/shard_map/ppermute | solution.py:193
  21.2 3.1 %collective-permute-start.9 = (bf16[432,384]{1,0:T(8,128)(2,1)S(1)}, bf16[432,384]{1,0:T(8,128)(2,1)S(1)}, u32[]{:S(2)}, u32[]{:S(2)}) collective-permute-start(bf16[432,384]{1,0:T(8,128)(2,1)S(1)} %collective-permute-done.2.refs_14_), channel_id=1, source_target_pairs={{0,2},{2,4},{4,6},{6,8},{8,10},{10,12},{12,14},{14,0},{1,15},{3,1}... | collective-permute-start | bytes 995336 | tf_op jit(solution)/shard_map/ppermute | solution.py:155
  25.0 3.3 %collective-permute-done.9.refs_15_ = bf16[432,384]{1,0:T(8,128)(2,1)S(1)} collective-permute-done((bf16[432,384]{1,0:T(8,128)(2,1)S(1)}, bf16[432,384]{1,0:T(8,128)(2,1)S(1)}, u32[]{:S(2)}, u32[]{:S(2)}) %collective-permute-start.9) | collective-permute-done | bytes 331808 | tf_op jit(solution)/shard_map/ppermute | solution.py:155
  28.4 3.4 %collective-permute-start.10 = (bf16[432,384]{1,0:T(8,128)(2,1)S(1)}, bf16[432,384]{1,0:T(8,128)(2,1)S(1)}, u32[]{:S(2)}, u32[]{:S(2)}) collective-permute-start(bf16[432,384]{1,0:T(8,128)(2,1)S(1)} %collective-permute-done.9.refs_15_), channel_id=1, source_target_pairs={{0,2},{2,4},{4,6},{6,8},{8,10},{10,12},{12,14},{14,0},{1,15},{3,1}... | collective-permute-start | bytes 995336 | tf_op jit(solution)/shard_map/ppermute | solution.py:155
  31.9 3.4 %collective-permute-start.6 = (bf16[432,384]{1,0:T(8,128)(2,1)S(1)}, bf16[432,384]{1,0:T(8,128)(2,1)S(1)}, u32[]{:S(2)}, u32[]{:S(2)}) collective-permute-start(bf16[432,384]{1,0:T(8,128)(2,1)S(1)} %collective-permute-done.5.refs_8_), channel_id=1, source_target_pairs={{0,2},{2,4},{4,6},{6,8},{8,10},{10,12},{12,14},{14,0},{1,15},{3,1}... | collective-permute-start | bytes 995336 | tf_op jit(solution)/shard_map/ppermute | solution.py:155
  35.8 3.4 %collective-permute-start.11 = (bf16[432,384]{1,0:T(8,128)(2,1)S(1)}, bf16[432,384]{1,0:T(8,128)(2,1)S(1)}, u32[]{:S(2)}, u32[]{:S(2)}) collective-permute-start(bf16[432,384]{1,0:T(8,128)(2,1)S(1)} %collective-permute-done.10.refs_16_), channel_id=1, source_target_pairs={{0,2},{2,4},{4,6},{6,8},{8,10},{10,12},{12,14},{14,0},{1,15},{3,1}... | collective-permute-start | bytes 995336 | tf_op jit(solution)/shard_map/ppermute | solution.py:155
  39.4 3.4 %collective-permute-start.7 = (bf16[432,384]{1,0:T(8,128)(2,1)S(1)}, bf16[432,384]{1,0:T(8,128)(2,1)S(1)}, u32[]{:S(2)}, u32[]{:S(2)}) collective-permute-start(bf16[432,384]{1,0:T(8,128)(2,1)S(1)} %collective-permute-done.6.refs_9_), channel_id=1, source_target_pairs={{0,2},{2,4},{4,6},{6,8},{8,10},{10,12},{12,14},{14,0},{1,15},{3,1}... | collective-permute-start | bytes 995336 | tf_op jit(solution)/shard_map/ppermute | solution.py:155
  43.3 3.4 %collective-permute-start.12 = (bf16[432,384]{1,0:T(8,128)(2,1)S(1)}, bf16[432,384]{1,0:T(8,128)(2,1)S(1)}, u32[]{:S(2)}, u32[]{:S(2)}) collective-permute-start(bf16[432,384]{1,0:T(8,128)(2,1)S(1)} %collective-permute-done.11.refs_17_), channel_id=1, source_target_pairs={{0,2},{2,4},{4,6},{6,8},{8,10},{10,12},{12,14},{14,0},{1,15},{3,1}... | collective-permute-start | bytes 995336 | tf_op jit(solution)/shard_map/ppermute | solution.py:155
  46.9 3.4 %collective-permute-start.8 = (bf16[432,384]{1,0:T(8,128)(2,1)S(1)}, bf16[432,384]{1,0:T(8,128)(2,1)S(1)}, u32[]{:S(2)}, u32[]{:S(2)}) collective-permute-start(bf16[432,384]{1,0:T(8,128)(2,1)S(1)} %collective-permute-done.7.refs_10_), channel_id=1, source_target_pairs={{0,2},{2,4},{4,6},{6,8},{8,10},{10,12},{12,14},{14,0},{1,15},{3,1}... | collective-permute-start | bytes 995336 | tf_op jit(solution)/shard_map/ppermute | solution.py:155
  50.8 3.4 %collective-permute-start.17 = (bf16[432,384]{1,0:T(8,128)(2,1)S(1)}, bf16[432,384]{1,0:T(8,128)(2,1)S(1)}, u32[]{:S(2)}, u32[]{:S(2)}) collective-permute-start(bf16[432,384]{1,0:T(8,128)(2,1)S(1)} %collective-permute-done.12.refs_18_), channel_id=1, source_target_pairs={{0,2},{2,4},{4,6},{6,8},{8,10},{10,12},{12,14},{14,0},{1,15},{3,1}... | collective-permute-start | bytes 995336 | tf_op jit(solution)/shard_map/ppermute | solution.py:155
  54.3 3.4 %collective-permute-start.15 = (bf16[432,384]{1,0:T(8,128)(2,1)S(1)}, bf16[432,384]{1,0:T(8,128)(2,1)S(1)}, u32[]{:S(2)}, u32[]{:S(2)}) collective-permute-start(bf16[432,384]{1,0:T(8,128)(2,1)S(1)} %collective-permute-done.8.refs_11_), channel_id=1, source_target_pairs={{0,2},{2,4},{4,6},{6,8},{8,10},{10,12},{12,14},{14,0},{1,15},{3,1}... | collective-permute-start | bytes 995336 | tf_op jit(solution)/shard_map/ppermute | solution.py:155
  58.3 3.4 %collective-permute-start.18 = (bf16[432,384]{1,0:T(8,128)(2,1)S(1)}, bf16[432,384]{1,0:T(8,128)(2,1)S(1)}, u32[]{:S(2)}, u32[]{:S(2)}) collective-permute-start(bf16[432,384]{1,0:T(8,128)(2,1)S(1)} %collective-permute-done.17.refs_19_), channel_id=1, source_target_pairs={{0,2},{2,4},{4,6},{6,8},{8,10},{10,12},{12,14},{14,0},{1,15},{3,1}... | collective-permute-start | bytes 995336 | tf_op jit(solution)/shard_map/ppermute | solution.py:155
  61.8 3.4 %collective-permute-start.16 = (bf16[432,384]{1,0:T(8,128)(2,1)S(1)}, bf16[432,384]{1,0:T(8,128)(2,1)S(1)}, u32[]{:S(2)}, u32[]{:S(2)}) collective-permute-start(bf16[432,384]{1,0:T(8,128)(2,1)S(1)} %collective-permute-done.15.refs_12_), channel_id=1, source_target_pairs={{0,2},{2,4},{4,6},{6,8},{8,10},{10,12},{12,14},{14,0},{1,15},{3,1}... | collective-permute-start | bytes 995336 | tf_op jit(solution)/shard_map/ppermute | solution.py:155
  65.7 3.4 %collective-permute-start.19 = (bf16[432,384]{1,0:T(8,128)(2,1)S(1)}, bf16[432,384]{1,0:T(8,128)(2,1)S(1)}, u32[]{:S(2)}, u32[]{:S(2)}) collective-permute-start(bf16[432,384]{1,0:T(8,128)(2,1)S(1)} %collective-permute-done.18.refs_20_), channel_id=1, source_target_pairs={{0,2},{2,4},{4,6},{6,8},{8,10},{10,12},{12,14},{14,0},{1,15},{3,1}... | collective-permute-start | bytes 995336 | tf_op jit(solution)/shard_map/ppermute | solution.py:155
  73.2 2.9 %collective-permute-done.14.refs_4_ = bf16[288,4608]{1,0:T(8,128)(2,1)S(1)} collective-permute-done((bf16[288,4608]{1,0:T(8,128)(2,1)S(1)}, bf16[288,4608]{1,0:T(8,128)(2,1)S(1)}, u32[]{:S(2)}, u32[]{:S(2)}) %collective-permute-start.14) | collective-permute-done | bytes 2654240 | tf_op jit(solution)/shard_map/ppermute | solution.py:155
  76.1 4.0 %collective-permute-start.20 = (bf16[288,4608]{1,0:T(8,128)(2,1)S(1)}, bf16[288,4608]{1,0:T(8,128)(2,1)S(1)}, u32[]{:S(2)}, u32[]{:S(2)}) collective-permute-start(bf16[288,4608]{1,0:T(8,128)(2,1)S(1)} %collective-permute-done.14.refs_4_), channel_id=1, source_target_pairs={{0,1},{1,0},{2,3},{3,2},{4,5},{5,4},{6,7},{7,6},{8,9},{9,8},{10,11... | collective-permute-start | bytes 7962632 | tf_op jit(solution)/shard_map/ppermute | solution.py:204
  80.3 4.5 %collective-permute-done.20.refs_5_ = bf16[288,4608]{1,0:T(8,128)(2,1)S(1)} collective-permute-done((bf16[288,4608]{1,0:T(8,128)(2,1)S(1)}, bf16[288,4608]{1,0:T(8,128)(2,1)S(1)}, u32[]{:S(2)}, u32[]{:S(2)}) %collective-permute-start.20) | collective-permute-done | bytes 2654240 | tf_op jit(solution)/shard_map/ppermute | solution.py:204
  84.8 18.5 %shard_map.73 = (f32[576,288]{1,0:T(8,128)S(1)}, f32[576,288]{1,0:T(8,128)S(1)}, f32[256,4,384]{2,1,0:T(4,128)S(1)}) custom-call(s32[3]{0:T(128)S(1)} %pad_add_fusion.1.place_ref, bf16[288,9216]{1,0:T(8,128)(2,1)} %bitcast.10, bf16[288,9216]{1,0:T(8,128)(2,1)} %copy-done.6, bf16[288,4608]{1,0:T(8,128)(2,1)S(1)} %collective-permute-done.4.refs_2_, ...), custom_call_target="tpu_custom_call" | custom-call | tf_op jit(solution)/shard_map/pallas_call | solution.py:225
  106.0 12.2 %all-to-all-start = ((f16[256,4,384]{2,1,0:T(4,128)(2,1)}), f16[256,4,384]{2,1,0:T(4,128)(2,1)}, u32[]{:S(2)}, u32[]{:S(2)}) async-start(f16[256,4,384]{2,1,0:T(4,128)(2,1)} %convert_element_type.9), calls=%async_computation | async-start | bytes 1572864 | tf_op jit(solution)/shard_map/all_to_all | solution.py:258
  118.3 4.9 %collective-permute-done.21 = f32[576,288]{0,1:T(8,128)} collective-permute-done((f32[576,288]{0,1:T(8,128)}, f32[576,288]{0,1:T(8,128)}, u32[]{:S(2)}, u32[]{:S(2)}) %collective-permute-start.21) | collective-permute-done | bytes 663584 | tf_op jit(solution)/shard_map/ppermute | solution.py:255
  132.6 11.9 %all-to-all-done = f16[256,4,384]{2,1,0:T(4,128)(2,1)} async-done(((f16[256,4,384]{2,1,0:T(4,128)(2,1)}), f16[256,4,384]{2,1,0:T(4,128)(2,1)}, u32[]{:S(2)}, u32[]{:S(2)}) %all-to-all-start) | async-done | bytes 786464 | tf_op jit(solution)/shard_map/all_to_all | solution.py:258
  146.9 6.1 %shard_map.74 = bf16[288,1152]{1,0:T(8,128)(2,1)} custom-call(s32[3]{0:T(128)S(1)} %pad_add_fusion.place_ref, s32[2]{0:T(128)S(1)} %copy-done.4, f32[256,4,384]{2,1,0:T(4,128)S(1)} %convert_element_type.10.got_ref, f32[288,288]{1,0:T(8,128)S(1)} %get-tuple-element.24.own_ref, f32[2,288,288]{2,1,0:T(8,128)} %collective-permute-done.22.side_ref, ...), custom_call_target="tpu_custom_call" | custom-call | tf_op jit(solution)/shard_map/pallas_call | solution.py:261
  (63 shorter events, 31.9 us)
Async XLA Ops:
  1.6 4.7 %collective-permute-start.1 = (bf16[576,288]{1,0:T(8,128)(2,1)S(1)}, bf16[576,288]{1,0:T(8,128)(2,1)S(1)}, u32[]{:S(2)}, u32[]{:S(2)}) collective-permute-start(bf16[576,288]{1,0:T(8,128)(2,1)S(1)} %pad_maximum_fusion.1), channel_id=1, source_target_pairs={{0,1},{1,0},{2,3},{3,2},{4,5},{5,4},{6,7},{7,6},{8,9},{9,8},{10,11... | collective-permute-start | bytes 995336 | tf_op jit(solution)/shard_map/ppermute | solution.py:180
  7.2 9.1 %collective-permute-start.2 = (bf16[432,384]{1,0:T(8,128)(2,1)S(1)}, bf16[432,384]{1,0:T(8,128)(2,1)S(1)}, u32[]{:S(2)}, u32[]{:S(2)}) collective-permute-start(bf16[432,384]{1,0:T(8,128)(2,1)S(1)} %maximum_maximum_fusion), channel_id=1, source_target_pairs={{0,16},{16,0},{1,17},{17,1},{2,18},{18,2},{3,19},{19,3},{4,20},{20... | collective-permute-start | bytes 995336 | tf_op jit(solution)/shard_map/ppermute | solution.py:193
  7.4 9.2 %collective-permute-start.3 = (bf16[432,384]{1,0:T(8,128)(2,1)S(1)}, bf16[432,384]{1,0:T(8,128)(2,1)S(1)}, u32[]{:S(2)}, u32[]{:S(2)}) collective-permute-start(bf16[432,384]{1,0:T(8,128)(2,1)S(1)} %maximum_maximum_fusion.1.refs_6_), channel_id=1, source_target_pairs={{0,2},{2,4},{4,6},{6,8},{8,10},{10,12},{12,14},{14,0},{1,15},{3,1}... | collective-permute-start | bytes 995336 | tf_op jit(solution)/shard_map/ppermute | solution.py:155
  16.6 52.6 %collective-permute-start.4 = (bf16[288,4608]{1,0:T(8,128)(2,1)S(1)}, bf16[288,4608]{1,0:T(8,128)(2,1)S(1)}, u32[]{:S(2)}, u32[]{:S(2)}) collective-permute-start(bf16[288,4608]{1,0:T(8,128)(2,1)S(1)} %get-tuple-element.12), channel_id=1, source_target_pairs={{0,16},{16,32},{32,48},{48,0},{1,49},{17,1},{33,17},{49,33},{2,18}... | collective-permute-start | bytes 7962632 | tf_op jit(solution)/shard_map/ppermute | solution.py:155
  18.4 57.8 %collective-permute-start.14 = (bf16[288,4608]{1,0:T(8,128)(2,1)S(1)}, bf16[288,4608]{1,0:T(8,128)(2,1)S(1)}, u32[]{:S(2)}, u32[]{:S(2)}) collective-permute-start(bf16[288,4608]{1,0:T(8,128)(2,1)S(1)} %get-tuple-element.14), channel_id=1, source_target_pairs={{0,16},{16,32},{32,48},{48,0},{1,49},{17,1},{33,17},{49,33},{2,18}... | collective-permute-start | bytes 7962632 | tf_op jit(solution)/shard_map/ppermute | solution.py:155
  19.3 61.0 %collective-permute-start = (bf16[288,9216]{1,0:T(8,128)(2,1)S(1)}, bf16[288,9216]{1,0:T(8,128)(2,1)S(1)}, u32[]{:S(2)}, u32[]{:S(2)}) collective-permute-start(bf16[288,9216]{1,0:T(8,128)(2,1)S(1)} %bitcast.12), channel_id=1, source_target_pairs={{0,1},{1,0},{2,3},{3,2},{4,5},{5,4},{6,7},{7,6},{8,9},{9,8},{10,11... | collective-permute-start | bytes 15925256 | tf_op jit(solution)/shard_map/ppermute | solution.py:204
  21.2 7.1 %collective-permute-start.9 = (bf16[432,384]{1,0:T(8,128)(2,1)S(1)}, bf16[432,384]{1,0:T(8,128)(2,1)S(1)}, u32[]{:S(2)}, u32[]{:S(2)}) collective-permute-start(bf16[432,384]{1,0:T(8,128)(2,1)S(1)} %collective-permute-done.2.refs_14_), channel_id=1, source_target_pairs={{0,2},{2,4},{4,6},{6,8},{8,10},{10,12},{12,14},{14,0},{1,15},{3,1}... | collective-permute-start | bytes 995336 | tf_op jit(solution)/shard_map/ppermute | solution.py:155
  24.3 7.6 %collective-permute-start.5 = (bf16[432,384]{1,0:T(8,128)(2,1)S(1)}, bf16[432,384]{1,0:T(8,128)(2,1)S(1)}, u32[]{:S(2)}, u32[]{:S(2)}) collective-permute-start(bf16[432,384]{1,0:T(8,128)(2,1)S(1)} %collective-permute-done.3.refs_7_), channel_id=1, source_target_pairs={{0,2},{2,4},{4,6},{6,8},{8,10},{10,12},{12,14},{14,0},{1,15},{3,1}... | collective-permute-start | bytes 995336 | tf_op jit(solution)/shard_map/ppermute | solution.py:155
  28.4 7.5 %collective-permute-start.10 = (bf16[432,384]{1,0:T(8,128)(2,1)S(1)}, bf16[432,384]{1,0:T(8,128)(2,1)S(1)}, u32[]{:S(2)}, u32[]{:S(2)}) collective-permute-start(bf16[432,384]{1,0:T(8,128)(2,1)S(1)} %collective-permute-done.9.refs_15_), channel_id=1, source_target_pairs={{0,2},{2,4},{4,6},{6,8},{8,10},{10,12},{12,14},{14,0},{1,15},{3,1}... | collective-permute-start | bytes 995336 | tf_op jit(solution)/shard_map/ppermute | solution.py:155
  31.9 7.5 %collective-permute-start.6 = (bf16[432,384]{1,0:T(8,128)(2,1)S(1)}, bf16[432,384]{1,0:T(8,128)(2,1)S(1)}, u32[]{:S(2)}, u32[]{:S(2)}) collective-permute-start(bf16[432,384]{1,0:T(8,128)(2,1)S(1)} %collective-permute-done.5.refs_8_), channel_id=1, source_target_pairs={{0,2},{2,4},{4,6},{6,8},{8,10},{10,12},{12,14},{14,0},{1,15},{3,1}... | collective-permute-start | bytes 995336 | tf_op jit(solution)/shard_map/ppermute | solution.py:155
  35.8 7.5 %collective-permute-start.11 = (bf16[432,384]{1,0:T(8,128)(2,1)S(1)}, bf16[432,384]{1,0:T(8,128)(2,1)S(1)}, u32[]{:S(2)}, u32[]{:S(2)}) collective-permute-start(bf16[432,384]{1,0:T(8,128)(2,1)S(1)} %collective-permute-done.10.refs_16_), channel_id=1, source_target_pairs={{0,2},{2,4},{4,6},{6,8},{8,10},{10,12},{12,14},{14,0},{1,15},{3,1}... | collective-permute-start | bytes 995336 | tf_op jit(solution)/shard_map/ppermute | solution.py:155
  39.4 7.5 %collective-permute-start.7 = (bf16[432,384]{1,0:T(8,128)(2,1)S(1)}, bf16[432,384]{1,0:T(8,128)(2,1)S(1)}, u32[]{:S(2)}, u32[]{:S(2)}) collective-permute-start(bf16[432,384]{1,0:T(8,128)(2,1)S(1)} %collective-permute-done.6.refs_9_), channel_id=1, source_target_pairs={{0,2},{2,4},{4,6},{6,8},{8,10},{10,12},{12,14},{14,0},{1,15},{3,1}... | collective-permute-start | bytes 995336 | tf_op jit(solution)/shard_map/ppermute | solution.py:155
  43.3 7.5 %collective-permute-start.12 = (bf16[432,384]{1,0:T(8,128)(2,1)S(1)}, bf16[432,384]{1,0:T(8,128)(2,1)S(1)}, u32[]{:S(2)}, u32[]{:S(2)}) collective-permute-start(bf16[432,384]{1,0:T(8,128)(2,1)S(1)} %collective-permute-done.11.refs_17_), channel_id=1, source_target_pairs={{0,2},{2,4},{4,6},{6,8},{8,10},{10,12},{12,14},{14,0},{1,15},{3,1}... | collective-permute-start | bytes 995336 | tf_op jit(solution)/shard_map/ppermute | solution.py:155
  46.9 7.5 %collective-permute-start.8 = (bf16[432,384]{1,0:T(8,128)(2,1)S(1)}, bf16[432,384]{1,0:T(8,128)(2,1)S(1)}, u32[]{:S(2)}, u32[]{:S(2)}) collective-permute-start(bf16[432,384]{1,0:T(8,128)(2,1)S(1)} %collective-permute-done.7.refs_10_), channel_id=1, source_target_pairs={{0,2},{2,4},{4,6},{6,8},{8,10},{10,12},{12,14},{14,0},{1,15},{3,1}... | collective-permute-start | bytes 995336 | tf_op jit(solution)/shard_map/ppermute | solution.py:155
  50.8 7.5 %collective-permute-start.17 = (bf16[432,384]{1,0:T(8,128)(2,1)S(1)}, bf16[432,384]{1,0:T(8,128)(2,1)S(1)}, u32[]{:S(2)}, u32[]{:S(2)}) collective-permute-start(bf16[432,384]{1,0:T(8,128)(2,1)S(1)} %collective-permute-done.12.refs_18_), channel_id=1, source_target_pairs={{0,2},{2,4},{4,6},{6,8},{8,10},{10,12},{12,14},{14,0},{1,15},{3,1}... | collective-permute-start | bytes 995336 | tf_op jit(solution)/shard_map/ppermute | solution.py:155
  54.3 7.5 %collective-permute-start.15 = (bf16[432,384]{1,0:T(8,128)(2,1)S(1)}, bf16[432,384]{1,0:T(8,128)(2,1)S(1)}, u32[]{:S(2)}, u32[]{:S(2)}) collective-permute-start(bf16[432,384]{1,0:T(8,128)(2,1)S(1)} %collective-permute-done.8.refs_11_), channel_id=1, source_target_pairs={{0,2},{2,4},{4,6},{6,8},{8,10},{10,12},{12,14},{14,0},{1,15},{3,1}... | collective-permute-start | bytes 995336 | tf_op jit(solution)/shard_map/ppermute | solution.py:155
  58.3 7.5 %collective-permute-start.18 = (bf16[432,384]{1,0:T(8,128)(2,1)S(1)}, bf16[432,384]{1,0:T(8,128)(2,1)S(1)}, u32[]{:S(2)}, u32[]{:S(2)}) collective-permute-start(bf16[432,384]{1,0:T(8,128)(2,1)S(1)} %collective-permute-done.17.refs_19_), channel_id=1, source_target_pairs={{0,2},{2,4},{4,6},{6,8},{8,10},{10,12},{12,14},{14,0},{1,15},{3,1}... | collective-permute-start | bytes 995336 | tf_op jit(solution)/shard_map/ppermute | solution.py:155
  61.8 9.5 %collective-permute-start.16 = (bf16[432,384]{1,0:T(8,128)(2,1)S(1)}, bf16[432,384]{1,0:T(8,128)(2,1)S(1)}, u32[]{:S(2)}, u32[]{:S(2)}) collective-permute-start(bf16[432,384]{1,0:T(8,128)(2,1)S(1)} %collective-permute-done.15.refs_12_), channel_id=1, source_target_pairs={{0,2},{2,4},{4,6},{6,8},{8,10},{10,12},{12,14},{14,0},{1,15},{3,1}... | collective-permute-start | bytes 995336 | tf_op jit(solution)/shard_map/ppermute | solution.py:155
  65.7 7.5 %collective-permute-start.19 = (bf16[432,384]{1,0:T(8,128)(2,1)S(1)}, bf16[432,384]{1,0:T(8,128)(2,1)S(1)}, u32[]{:S(2)}, u32[]{:S(2)}) collective-permute-start(bf16[432,384]{1,0:T(8,128)(2,1)S(1)} %collective-permute-done.18.refs_20_), channel_id=1, source_target_pairs={{0,2},{2,4},{4,6},{6,8},{8,10},{10,12},{12,14},{14,0},{1,15},{3,1}... | collective-permute-start | bytes 995336 | tf_op jit(solution)/shard_map/ppermute | solution.py:155
  69.1 11.1 %collective-permute-start.13 = (bf16[288,4608]{1,0:T(8,128)(2,1)S(1)}, bf16[288,4608]{1,0:T(8,128)(2,1)S(1)}, u32[]{:S(2)}, u32[]{:S(2)}) collective-permute-start(bf16[288,4608]{1,0:T(8,128)(2,1)S(1)} %collective-permute-done.4.refs_2_), channel_id=1, source_target_pairs={{0,1},{1,0},{2,3},{3,2},{4,5},{5,4},{6,7},{7,6},{8,9},{9,8},{10,11... | collective-permute-start | bytes 7962632 | tf_op jit(solution)/shard_map/ppermute | solution.py:204
  76.1 8.6 %collective-permute-start.20 = (bf16[288,4608]{1,0:T(8,128)(2,1)S(1)}, bf16[288,4608]{1,0:T(8,128)(2,1)S(1)}, u32[]{:S(2)}, u32[]{:S(2)}) collective-permute-start(bf16[288,4608]{1,0:T(8,128)(2,1)S(1)} %collective-permute-done.14.refs_4_), channel_id=1, source_target_pairs={{0,1},{1,0},{2,3},{3,2},{4,5},{5,4},{6,7},{7,6},{8,9},{9,8},{10,11... | collective-permute-start | bytes 7962632 | tf_op jit(solution)/shard_map/ppermute | solution.py:204
  104.5 18.7 %collective-permute-start.21 = (f32[576,288]{0,1:T(8,128)}, f32[576,288]{0,1:T(8,128)}, u32[]{:S(2)}, u32[]{:S(2)}) collective-permute-start(f32[576,288]{0,1:T(8,128)} %copy.8), channel_id=1, source_target_pairs={{0,16},{16,0},{1,17},{17,1},{2,18},{18,2},{3,19},{19,3},{4,20},{20... | collective-permute-start | bytes 1990664 | tf_op jit(solution)/shard_map/ppermute | solution.py:255
  106.0 38.5 %all-to-all-start = ((f16[256,4,384]{2,1,0:T(4,128)(2,1)}), f16[256,4,384]{2,1,0:T(4,128)(2,1)}, u32[]{:S(2)}, u32[]{:S(2)}) async-start(f16[256,4,384]{2,1,0:T(4,128)(2,1)} %convert_element_type.9), calls=%async_computation | async-start | bytes 1572864 | tf_op jit(solution)/shard_map/all_to_all | solution.py:258
  128.4 17.5 %collective-permute-start.22 = (f32[2,288,288]{2,1,0:T(8,128)}, f32[2,288,288]{2,1,0:T(8,128)}, u32[]{:S(2)}, u32[]{:S(2)}) collective-permute-start(f32[2,288,288]{2,1,0:T(8,128)} %pad_maximum_fusion), channel_id=1, source_target_pairs={{0,1},{1,0},{2,3},{3,2},{4,5},{5,4},{6,7},{7,6},{8,9},{9,8},{10,11... | collective-permute-start | bytes 1990664 | tf_op jit(solution)/shard_map/ppermute | solution.py:256
  (7 other events, 180.8 us)

commit v9 on v8

--- a/solution.py
+++ b/solution.py
@@ -15,7 +15,8 @@
 SLAB = VB // GRPS
 PIECE = SLAB // 4 * SLAB
 LANES = 384
-CHUNK = 1152
+TILE = 128
+CHUNK = 1536
 WIRE = jnp.float16
 SCALE = 16.0
 BF, F32 = jnp.bfloat16, jnp.float32
@@ -40,9 +41,10 @@
 
 
 def folded(block):
-    tall, third = block.shape[0] // 4, block.shape[1] // 3
-    rest = [block[3 * tall :, n * third : (n + 1) * third] for n in range(3)]
-    return jnp.concatenate([block[: 3 * tall], jnp.concatenate(rest, axis=0)], axis=1)
+    tall, full = block.shape[0] // 4, block.shape[1] // TILE * TILE
+    rest = [block[n * tall : (n + 1) * tall, full:] for n in range(4)]
+    tiles = [block[:, n : n + TILE] for n in range(0, full, TILE)]
+    return jnp.concatenate([*tiles, jnp.concatenate(rest, axis=1)], axis=0)
 
 
 def product_kernel(place_ref, *refs):
@@ -53,24 +55,39 @@
     @pl.when(step == 0)
     def _():
         acc_ref[...] = jnp.zeros_like(acc_ref)
-        copies = [
-            pltpu.make_async_copy(piece, stage_ref.at[n], sem.at[n])
-            for n, piece in enumerate(pieces)
-        ]
+        z, xl, c = place_ref[0], place_ref[1], place_ref[2]
+        tall, width = stage_ref.shape[1], w_ref.shape[1]
+        tiles = width // TILE
+        starts, copies = [], []
+        for n, piece in enumerate(pieces):
+            k = n % ZS
+            back = jnp.where(c == 0, k, ZS - k)
+            of = jnp.where(n < ZS, xl, 1 - xl) * ZS + lax.rem(z + ZS - back, ZS)
+            start = pl.multiple_of(of * (4 * tall), 4 * tall)
+            starts.append(start)
+            for m in range(tiles):
+                copies.append(
+                    pltpu.make_async_copy(
+                        piece.at[pl.ds(m * 4 * tall, 4 * tall)],
+                        w_ref.at[pl.ds(start, 4 * tall), pl.ds(m * TILE, TILE)],
+                        sem.at[n, m],
+                    )
+                )
+            copies.append(
+                pltpu.make_async_copy(
+                    piece.at[pl.ds(tiles * 4 * tall, tall)], stage_ref.at[n], sem.at[n, tiles]
+                )
+            )
         for copy in copies:
             copy.start()
         for copy in copies:
             copy.wait()
-        z, xl, c = place_ref[0], place_ref[1], place_ref[2]
-        tall, width = stage_ref.shape[1] // 3, w_ref.shape[1]
-        for n in range(2 * ZS):
-            k = n % ZS
-            back = jnp.where(c == 0, k, ZS - k)
-            of = jnp.where(n < ZS, xl, 1 - xl) * ZS + lax.rem(z + ZS - back, ZS)
-            start = pl.multiple_of(of * (4 * tall), 4 * tall)
-            w_ref[pl.ds(start, 3 * tall)] = stage_ref[n, :, :width]
-            rest = [stage_ref[n, m * tall : (m + 1) * tall, width:] for m in range(3)]
-            w_ref[pl.ds(start + 3 * tall, tall)] = jnp.concatenate(rest, axis=1)
+        wide = width - tiles * TILE
+        for n, start in enumerate(starts):
+            for m in range(4):
+                w_ref[pl.ds(start + m * tall, tall), tiles * TILE :] = stage_ref[
+                    n, :, m * wide : (m + 1) * wide
+                ]
 
     size = row_ref.shape[0]
     w = w_ref[pl.ds(pl.multiple_of(step * CHUNK, CHUNK), CHUNK)]
@@ -245,9 +262,9 @@
         scratch_shapes=[
             pltpu.VMEM((quarter, 4 * rows), F32),
             pltpu.VMEM((4, rows, quarter), F32),
-            pltpu.VMEM((2 * ZS, *far.shape), BF),
+            pltpu.VMEM((2 * ZS, shard // 2, TILE), BF),
             pltpu.VMEM((k_all, quarter), BF),
-            pltpu.SemaphoreType.DMA((len(pieces),)),
+            pltpu.SemaphoreType.DMA((len(pieces), quarter // TILE + 1)),
         ],
         compiler_params=params,
     )(jnp.stack([z, xl, c]), *t_refs, *pieces, out_rows, out_cols)

time: 153 us -> 152 us (level)
  no operation moved by 1% of the time
where the time goes in v9:
time: 152 us
  starting transfers between devices  76.3 us (50%)
  waiting for transfers between devices  36.5 us (24%)
  Pallas kernels  23.4 us (15%)
  other arithmetic  7.65 us (5%)
  local copies, waits for them, and re-layouts  7.64 us (5%)
    ppermute x16, starting transfers between devices, around(): return lax.ppermute(x, (*axes, 'c'), moves)  49.2 us
    pallas_call x1, Pallas kernels, on_device(): pl.pallas_call(product_kernel, grid=(k_all // CHUNK,), in_specs=[pl.Block...  17.3 us
    all_to_all x1, starting transfers between devices, on_device(): got = lax.all_to_all(wire.astype(WIRE), ORDER, 0, 0, tiled=True)  12.2 us
    all_to_all x1, waiting for transfers between devices, on_device(): got = lax.all_to_all(wire.astype(WIRE), ORDER, 0, 0, tiled=True)  11.9 us
    ppermute x16, waiting for transfers between devices, around(): return lax.ppermute(x, (*axes, 'c'), moves)  11.7 us
    ppermute x3, starting transfers between devices, on_device(): t_c, c_a, c_b = (lax.ppermute(x, 'c', SWAP) for x in (t, x_a, x_b))  8.14 us
    pallas_call x1, Pallas kernels, on_device(): pl.pallas_call(unpack_kernel, out_shape=jax.ShapeDtypeStruct((rows, slab)...  6.09 us
    ppermute x1, waiting for transfers between devices, on_device(): fetched = lax.ppermute(p_far, 'xl', SWAP)  4.89 us
  transfers between devices with their start and end apart: 24, of which 19 were waited for; matrix products, arithmetic and copies ran while one was open for 7% of the time, Pallas kernels for 0%

profile of v9, /device:TPU:1, one launch (start us, length us, event | category | flops | bytes accessed | tf_op | source)
XLA Modules:
  0.0 151.7 jit_solution(12267978112164463088)
XLA Ops:
  1.6 3.3 %collective-permute-start.1 = (bf16[576,288]{1,0:T(8,128)(2,1)S(1)}, bf16[576,288]{1,0:T(8,128)(2,1)S(1)}, u32[]{:S(2)}, u32[]{:S(2)}) collective-permute-start(bf16[576,288]{1,0:T(8,128)(2,1)S(1)} %pad_maximum_fusion.1), channel_id=1, source_target_pairs={{0,1},{1,0},{2,3},{3,2},{4,5},{5,4},{6,7},{7,6},{8,9},{9,8},{10,11... | collective-permute-start | bytes 995336 | tf_op jit(solution)/shard_map/ppermute | solution.py:197
  7.3 5.1 %collective-permute-start.3 = (bf16[1296,128]{1,0:T(8,128)(2,1)S(1)}, bf16[1296,128]{1,0:T(8,128)(2,1)S(1)}, u32[]{:S(2)}, u32[]{:S(2)}) collective-permute-start(bf16[1296,128]{1,0:T(8,128)(2,1)S(1)} %maximum_maximum_fusion.1.refs_6_), channel_id=1, source_target_pairs={{0,2},{2,4},{4,6},{6,8},{8,10},{10,12},{12,14},{14,0},{1,15},{3,1}... | collective-permute-start | bytes 995336 | tf_op jit(solution)/shard_map/ppermute | solution.py:172
  12.8 3.4 %collective-permute-done.2.refs_14_ = bf16[1296,128]{1,0:T(8,128)(2,1)S(1)} collective-permute-done((bf16[1296,128]{1,0:T(8,128)(2,1)S(1)}, bf16[1296,128]{1,0:T(8,128)(2,1)S(1)}, u32[]{:S(2)}, u32[]{:S(2)}) %collective-permute-start.2) | collective-permute-done | bytes 331808 | tf_op jit(solution)/shard_map/ppermute | solution.py:210
  21.1 3.1 %collective-permute-start.9 = (bf16[1296,128]{1,0:T(8,128)(2,1)S(1)}, bf16[1296,128]{1,0:T(8,128)(2,1)S(1)}, u32[]{:S(2)}, u32[]{:S(2)}) collective-permute-start(bf16[1296,128]{1,0:T(8,128)(2,1)S(1)} %collective-permute-done.2.refs_14_), channel_id=1, source_target_pairs={{0,2},{2,4},{4,6},{6,8},{8,10},{10,12},{12,14},{14,0},{1,15},{3,1}... | collective-permute-start | bytes 995336 | tf_op jit(solution)/shard_map/ppermute | solution.py:172
  24.9 3.3 %collective-permute-done.9.refs_15_ = bf16[1296,128]{1,0:T(8,128)(2,1)S(1)} collective-permute-done((bf16[1296,128]{1,0:T(8,128)(2,1)S(1)}, bf16[1296,128]{1,0:T(8,128)(2,1)S(1)}, u32[]{:S(2)}, u32[]{:S(2)}) %collective-permute-start.9) | collective-permute-done | bytes 331808 | tf_op jit(solution)/shard_map/ppermute | solution.py:172
  28.3 3.4 %collective-permute-start.10 = (bf16[1296,128]{1,0:T(8,128)(2,1)S(1)}, bf16[1296,128]{1,0:T(8,128)(2,1)S(1)}, u32[]{:S(2)}, u32[]{:S(2)}) collective-permute-start(bf16[1296,128]{1,0:T(8,128)(2,1)S(1)} %collective-permute-done.9.refs_15_), channel_id=1, source_target_pairs={{0,2},{2,4},{4,6},{6,8},{8,10},{10,12},{12,14},{14,0},{1,15},{3,1}... | collective-permute-start | bytes 995336 | tf_op jit(solution)/shard_map/ppermute | solution.py:172
  31.8 3.4 %collective-permute-start.6 = (bf16[1296,128]{1,0:T(8,128)(2,1)S(1)}, bf16[1296,128]{1,0:T(8,128)(2,1)S(1)}, u32[]{:S(2)}, u32[]{:S(2)}) collective-permute-start(bf16[1296,128]{1,0:T(8,128)(2,1)S(1)} %collective-permute-done.5.refs_8_), channel_id=1, source_target_pairs={{0,2},{2,4},{4,6},{6,8},{8,10},{10,12},{12,14},{14,0},{1,15},{3,1}... | collective-permute-start | bytes 995336 | tf_op jit(solution)/shard_map/ppermute | solution.py:172
  35.7 3.4 %collective-permute-start.11 = (bf16[1296,128]{1,0:T(8,128)(2,1)S(1)}, bf16[1296,128]{1,0:T(8,128)(2,1)S(1)}, u32[]{:S(2)}, u32[]{:S(2)}) collective-permute-start(bf16[1296,128]{1,0:T(8,128)(2,1)S(1)} %collective-permute-done.10.refs_16_), channel_id=1, source_target_pairs={{0,2},{2,4},{4,6},{6,8},{8,10},{10,12},{12,14},{14,0},{1,15},{3,1}... | collective-permute-start | bytes 995336 | tf_op jit(solution)/shard_map/ppermute | solution.py:172
  39.3 3.4 %collective-permute-start.7 = (bf16[1296,128]{1,0:T(8,128)(2,1)S(1)}, bf16[1296,128]{1,0:T(8,128)(2,1)S(1)}, u32[]{:S(2)}, u32[]{:S(2)}) collective-permute-start(bf16[1296,128]{1,0:T(8,128)(2,1)S(1)} %collective-permute-done.6.refs_9_), channel_id=1, source_target_pairs={{0,2},{2,4},{4,6},{6,8},{8,10},{10,12},{12,14},{14,0},{1,15},{3,1}... | collective-permute-start | bytes 995336 | tf_op jit(solution)/shard_map/ppermute | solution.py:172
  43.2 3.4 %collective-permute-start.12 = (bf16[1296,128]{1,0:T(8,128)(2,1)S(1)}, bf16[1296,128]{1,0:T(8,128)(2,1)S(1)}, u32[]{:S(2)}, u32[]{:S(2)}) collective-permute-start(bf16[1296,128]{1,0:T(8,128)(2,1)S(1)} %collective-permute-done.11.refs_17_), channel_id=1, source_target_pairs={{0,2},{2,4},{4,6},{6,8},{8,10},{10,12},{12,14},{14,0},{1,15},{3,1}... | collective-permute-start | bytes 995336 | tf_op jit(solution)/shard_map/ppermute | solution.py:172
  46.8 3.4 %collective-permute-start.8 = (bf16[1296,128]{1,0:T(8,128)(2,1)S(1)}, bf16[1296,128]{1,0:T(8,128)(2,1)S(1)}, u32[]{:S(2)}, u32[]{:S(2)}) collective-permute-start(bf16[1296,128]{1,0:T(8,128)(2,1)S(1)} %collective-permute-done.7.refs_10_), channel_id=1, source_target_pairs={{0,2},{2,4},{4,6},{6,8},{8,10},{10,12},{12,14},{14,0},{1,15},{3,1}... | collective-permute-start | bytes 995336 | tf_op jit(solution)/shard_map/ppermute | solution.py:172
  50.7 3.4 %collective-permute-start.17 = (bf16[1296,128]{1,0:T(8,128)(2,1)S(1)}, bf16[1296,128]{1,0:T(8,128)(2,1)S(1)}, u32[]{:S(2)}, u32[]{:S(2)}) collective-permute-start(bf16[1296,128]{1,0:T(8,128)(2,1)S(1)} %collective-permute-done.12.refs_18_), channel_id=1, source_target_pairs={{0,2},{2,4},{4,6},{6,8},{8,10},{10,12},{12,14},{14,0},{1,15},{3,1}... | collective-permute-start | bytes 995336 | tf_op jit(solution)/shard_map/ppermute | solution.py:172
  54.2 3.4 %collective-permute-start.15 = (bf16[1296,128]{1,0:T(8,128)(2,1)S(1)}, bf16[1296,128]{1,0:T(8,128)(2,1)S(1)}, u32[]{:S(2)}, u32[]{:S(2)}) collective-permute-start(bf16[1296,128]{1,0:T(8,128)(2,1)S(1)} %collective-permute-done.8.refs_11_), channel_id=1, source_target_pairs={{0,2},{2,4},{4,6},{6,8},{8,10},{10,12},{12,14},{14,0},{1,15},{3,1}... | collective-permute-start | bytes 995336 | tf_op jit(solution)/shard_map/ppermute | solution.py:172
  58.2 3.4 %collective-permute-start.18 = (bf16[1296,128]{1,0:T(8,128)(2,1)S(1)}, bf16[1296,128]{1,0:T(8,128)(2,1)S(1)}, u32[]{:S(2)}, u32[]{:S(2)}) collective-permute-start(bf16[1296,128]{1,0:T(8,128)(2,1)S(1)} %collective-permute-done.17.refs_19_), channel_id=1, source_target_pairs={{0,2},{2,4},{4,6},{6,8},{8,10},{10,12},{12,14},{14,0},{1,15},{3,1}... | collective-permute-start | bytes 995336 | tf_op jit(solution)/shard_map/ppermute | solution.py:172
  61.7 3.4 %collective-permute-start.16 = (bf16[1296,128]{1,0:T(8,128)(2,1)S(1)}, bf16[1296,128]{1,0:T(8,128)(2,1)S(1)}, u32[]{:S(2)}, u32[]{:S(2)}) collective-permute-start(bf16[1296,128]{1,0:T(8,128)(2,1)S(1)} %collective-permute-done.15.refs_12_), channel_id=1, source_target_pairs={{0,2},{2,4},{4,6},{6,8},{8,10},{10,12},{12,14},{14,0},{1,15},{3,1}... | collective-permute-start | bytes 995336 | tf_op jit(solution)/shard_map/ppermute | solution.py:172
  65.6 3.4 %collective-permute-start.19 = (bf16[1296,128]{1,0:T(8,128)(2,1)S(1)}, bf16[1296,128]{1,0:T(8,128)(2,1)S(1)}, u32[]{:S(2)}, u32[]{:S(2)}) collective-permute-start(bf16[1296,128]{1,0:T(8,128)(2,1)S(1)} %collective-permute-done.18.refs_20_), channel_id=1, source_target_pairs={{0,2},{2,4},{4,6},{6,8},{8,10},{10,12},{12,14},{14,0},{1,15},{3,1}... | collective-permute-start | bytes 995336 | tf_op jit(solution)/shard_map/ppermute | solution.py:172
  73.1 2.9 %collective-permute-done.14.refs_4_ = bf16[288,4608]{1,0:T(8,128)(2,1)S(1)} collective-permute-done((bf16[288,4608]{1,0:T(8,128)(2,1)S(1)}, bf16[288,4608]{1,0:T(8,128)(2,1)S(1)}, u32[]{:S(2)}, u32[]{:S(2)}) %collective-permute-start.14) | collective-permute-done | bytes 2654240 | tf_op jit(solution)/shard_map/ppermute | solution.py:172
  76.0 4.0 %collective-permute-start.20 = (bf16[288,4608]{1,0:T(8,128)(2,1)S(1)}, bf16[288,4608]{1,0:T(8,128)(2,1)S(1)}, u32[]{:S(2)}, u32[]{:S(2)}) collective-permute-start(bf16[288,4608]{1,0:T(8,128)(2,1)S(1)} %collective-permute-done.14.refs_4_), channel_id=1, source_target_pairs={{0,1},{1,0},{2,3},{3,2},{4,5},{5,4},{6,7},{7,6},{8,9},{9,8},{10,11... | collective-permute-start | bytes 7962632 | tf_op jit(solution)/shard_map/ppermute | solution.py:221
  80.2 4.5 %collective-permute-done.20.refs_5_ = bf16[288,4608]{1,0:T(8,128)(2,1)S(1)} collective-permute-done((bf16[288,4608]{1,0:T(8,128)(2,1)S(1)}, bf16[288,4608]{1,0:T(8,128)(2,1)S(1)}, u32[]{:S(2)}, u32[]{:S(2)}) %collective-permute-start.20) | collective-permute-done | bytes 2654240 | tf_op jit(solution)/shard_map/ppermute | solution.py:221
  84.7 17.3 %shard_map.73 = (f32[576,288]{1,0:T(8,128)S(1)}, f32[576,288]{1,0:T(8,128)S(1)}, f32[256,4,384]{2,1,0:T(4,128)S(1)}) custom-call(s32[3]{0:T(128)S(1)} %pad_add_fusion.1.place_ref, bf16[288,9216]{1,0:T(8,128)(2,1)} %bitcast.10, bf16[288,9216]{1,0:T(8,128)(2,1)} %copy-done.6, bf16[288,4608]{1,0:T(8,128)(2,1)S(1)} %collective-permute-done.4.refs_2_, ...), custom_call_target="tpu_custom_call" | custom-call | tf_op jit(solution)/shard_map/pallas_call | solution.py:242
  104.7 12.2 %all-to-all-start = ((f16[256,4,384]{2,1,0:T(4,128)(2,1)}), f16[256,4,384]{2,1,0:T(4,128)(2,1)}, u32[]{:S(2)}, u32[]{:S(2)}) async-start(f16[256,4,384]{2,1,0:T(4,128)(2,1)} %convert_element_type.9), calls=%async_computation | async-start | bytes 1572864 | tf_op jit(solution)/shard_map/all_to_all | solution.py:275
  117.1 4.9 %collective-permute-done.21 = f32[576,288]{0,1:T(8,128)} collective-permute-done((f32[576,288]{0,1:T(8,128)}, f32[576,288]{0,1:T(8,128)}, u32[]{:S(2)}, u32[]{:S(2)}) %collective-permute-start.21) | collective-permute-done | bytes 663584 | tf_op jit(solution)/shard_map/ppermute | solution.py:272
  131.3 11.9 %all-to-all-done = f16[256,4,384]{2,1,0:T(4,128)(2,1)} async-done(((f16[256,4,384]{2,1,0:T(4,128)(2,1)}), f16[256,4,384]{2,1,0:T(4,128)(2,1)}, u32[]{:S(2)}, u32[]{:S(2)}) %all-to-all-start) | async-done | bytes 786464 | tf_op jit(solution)/shard_map/all_to_all | solution.py:275
  145.6 6.1 %shard_map.74 = bf16[288,1152]{1,0:T(8,128)(2,1)} custom-call(s32[3]{0:T(128)S(1)} %pad_add_fusion.place_ref, s32[2]{0:T(128)S(1)} %copy-done.4, f32[256,4,384]{2,1,0:T(4,128)S(1)} %convert_element_type.10.got_ref, f32[288,288]{1,0:T(8,128)S(1)} %get-tuple-element.24.own_ref, f32[2,288,288]{2,1,0:T(8,128)} %collective-permute-done.22.side_ref, ...), custom_call_target="tpu_custom_call" | custom-call | tf_op jit(solution)/shard_map/pallas_call | solution.py:278
  (61 shorter events, 31.8 us)
Async XLA Ops:
  1.6 4.7 %collective-permute-start.1 = (bf16[576,288]{1,0:T(8,128)(2,1)S(1)}, bf16[576,288]{1,0:T(8,128)(2,1)S(1)}, u32[]{:S(2)}, u32[]{:S(2)}) collective-permute-start(bf16[576,288]{1,0:T(8,128)(2,1)S(1)} %pad_maximum_fusion.1), channel_id=1, source_target_pairs={{0,1},{1,0},{2,3},{3,2},{4,5},{5,4},{6,7},{7,6},{8,9},{9,8},{10,11... | collective-permute-start | bytes 995336 | tf_op jit(solution)/shard_map/ppermute | solution.py:197
  7.1 9.1 %collective-permute-start.2 = (bf16[1296,128]{1,0:T(8,128)(2,1)S(1)}, bf16[1296,128]{1,0:T(8,128)(2,1)S(1)}, u32[]{:S(2)}, u32[]{:S(2)}) collective-permute-start(bf16[1296,128]{1,0:T(8,128)(2,1)S(1)} %maximum_maximum_fusion), channel_id=1, source_target_pairs={{0,16},{16,0},{1,17},{17,1},{2,18},{18,2},{3,19},{19,3},{4,20},{20... | collective-permute-start | bytes 995336 | tf_op jit(solution)/shard_map/ppermute | solution.py:210
  7.3 9.2 %collective-permute-start.3 = (bf16[1296,128]{1,0:T(8,128)(2,1)S(1)}, bf16[1296,128]{1,0:T(8,128)(2,1)S(1)}, u32[]{:S(2)}, u32[]{:S(2)}) collective-permute-start(bf16[1296,128]{1,0:T(8,128)(2,1)S(1)} %maximum_maximum_fusion.1.refs_6_), channel_id=1, source_target_pairs={{0,2},{2,4},{4,6},{6,8},{8,10},{10,12},{12,14},{14,0},{1,15},{3,1}... | collective-permute-start | bytes 995336 | tf_op jit(solution)/shard_map/ppermute | solution.py:172
  16.4 52.6 %collective-permute-start.4 = (bf16[288,4608]{1,0:T(8,128)(2,1)S(1)}, bf16[288,4608]{1,0:T(8,128)(2,1)S(1)}, u32[]{:S(2)}, u32[]{:S(2)}) collective-permute-start(bf16[288,4608]{1,0:T(8,128)(2,1)S(1)} %get-tuple-element.12), channel_id=1, source_target_pairs={{0,16},{16,32},{32,48},{48,0},{1,49},{17,1},{33,17},{49,33},{2,18}... | collective-permute-start | bytes 7962632 | tf_op jit(solution)/shard_map/ppermute | solution.py:172
  18.3 57.8 %collective-permute-start.14 = (bf16[288,4608]{1,0:T(8,128)(2,1)S(1)}, bf16[288,4608]{1,0:T(8,128)(2,1)S(1)}, u32[]{:S(2)}, u32[]{:S(2)}) collective-permute-start(bf16[288,4608]{1,0:T(8,128)(2,1)S(1)} %get-tuple-element.14), channel_id=1, source_target_pairs={{0,16},{16,32},{32,48},{48,0},{1,49},{17,1},{33,17},{49,33},{2,18}... | collective-permute-start | bytes 7962632 | tf_op jit(solution)/shard_map/ppermute | solution.py:172
  19.2 61.0 %collective-permute-start = (bf16[288,9216]{1,0:T(8,128)(2,1)S(1)}, bf16[288,9216]{1,0:T(8,128)(2,1)S(1)}, u32[]{:S(2)}, u32[]{:S(2)}) collective-permute-start(bf16[288,9216]{1,0:T(8,128)(2,1)S(1)} %bitcast.12), channel_id=1, source_target_pairs={{0,1},{1,0},{2,3},{3,2},{4,5},{5,4},{6,7},{7,6},{8,9},{9,8},{10,11... | collective-permute-start | bytes 15925256 | tf_op jit(solution)/shard_map/ppermute | solution.py:221
  21.1 7.1 %collective-permute-start.9 = (bf16[1296,128]{1,0:T(8,128)(2,1)S(1)}, bf16[1296,128]{1,0:T(8,128)(2,1)S(1)}, u32[]{:S(2)}, u32[]{:S(2)}) collective-permute-start(bf16[1296,128]{1,0:T(8,128)(2,1)S(1)} %collective-permute-done.2.refs_14_), channel_id=1, source_target_pairs={{0,2},{2,4},{4,6},{6,8},{8,10},{10,12},{12,14},{14,0},{1,15},{3,1}... | collective-permute-start | bytes 995336 | tf_op jit(solution)/shard_map/ppermute | solution.py:172
  24.2 7.6 %collective-permute-start.5 = (bf16[1296,128]{1,0:T(8,128)(2,1)S(1)}, bf16[1296,128]{1,0:T(8,128)(2,1)S(1)}, u32[]{:S(2)}, u32[]{:S(2)}) collective-permute-start(bf16[1296,128]{1,0:T(8,128)(2,1)S(1)} %collective-permute-done.3.refs_7_), channel_id=1, source_target_pairs={{0,2},{2,4},{4,6},{6,8},{8,10},{10,12},{12,14},{14,0},{1,15},{3,1}... | collective-permute-start | bytes 995336 | tf_op jit(solution)/shard_map/ppermute | solution.py:172
  28.3 7.5 %collective-permute-start.10 = (bf16[1296,128]{1,0:T(8,128)(2,1)S(1)}, bf16[1296,128]{1,0:T(8,128)(2,1)S(1)}, u32[]{:S(2)}, u32[]{:S(2)}) collective-permute-start(bf16[1296,128]{1,0:T(8,128)(2,1)S(1)} %collective-permute-done.9.refs_15_), channel_id=1, source_target_pairs={{0,2},{2,4},{4,6},{6,8},{8,10},{10,12},{12,14},{14,0},{1,15},{3,1}... | collective-permute-start | bytes 995336 | tf_op jit(solution)/shard_map/ppermute | solution.py:172
  31.8 7.5 %collective-permute-start.6 = (bf16[1296,128]{1,0:T(8,128)(2,1)S(1)}, bf16[1296,128]{1,0:T(8,128)(2,1)S(1)}, u32[]{:S(2)}, u32[]{:S(2)}) collective-permute-start(bf16[1296,128]{1,0:T(8,128)(2,1)S(1)} %collective-permute-done.5.refs_8_), channel_id=1, source_target_pairs={{0,2},{2,4},{4,6},{6,8},{8,10},{10,12},{12,14},{14,0},{1,15},{3,1}... | collective-permute-start | bytes 995336 | tf_op jit(solution)/shard_map/ppermute | solution.py:172
  35.7 7.5 %collective-permute-start.11 = (bf16[1296,128]{1,0:T(8,128)(2,1)S(1)}, bf16[1296,128]{1,0:T(8,128)(2,1)S(1)}, u32[]{:S(2)}, u32[]{:S(2)}) collective-permute-start(bf16[1296,128]{1,0:T(8,128)(2,1)S(1)} %collective-permute-done.10.refs_16_), channel_id=1, source_target_pairs={{0,2},{2,4},{4,6},{6,8},{8,10},{10,12},{12,14},{14,0},{1,15},{3,1}... | collective-permute-start | bytes 995336 | tf_op jit(solution)/shard_map/ppermute | solution.py:172
  39.3 7.5 %collective-permute-start.7 = (bf16[1296,128]{1,0:T(8,128)(2,1)S(1)}, bf16[1296,128]{1,0:T(8,128)(2,1)S(1)}, u32[]{:S(2)}, u32[]{:S(2)}) collective-permute-start(bf16[1296,128]{1,0:T(8,128)(2,1)S(1)} %collective-permute-done.6.refs_9_), channel_id=1, source_target_pairs={{0,2},{2,4},{4,6},{6,8},{8,10},{10,12},{12,14},{14,0},{1,15},{3,1}... | collective-permute-start | bytes 995336 | tf_op jit(solution)/shard_map/ppermute | solution.py:172
  43.2 7.5 %collective-permute-start.12 = (bf16[1296,128]{1,0:T(8,128)(2,1)S(1)}, bf16[1296,128]{1,0:T(8,128)(2,1)S(1)}, u32[]{:S(2)}, u32[]{:S(2)}) collective-permute-start(bf16[1296,128]{1,0:T(8,128)(2,1)S(1)} %collective-permute-done.11.refs_17_), channel_id=1, source_target_pairs={{0,2},{2,4},{4,6},{6,8},{8,10},{10,12},{12,14},{14,0},{1,15},{3,1}... | collective-permute-start | bytes 995336 | tf_op jit(solution)/shard_map/ppermute | solution.py:172
  46.8 7.5 %collective-permute-start.8 = (bf16[1296,128]{1,0:T(8,128)(2,1)S(1)}, bf16[1296,128]{1,0:T(8,128)(2,1)S(1)}, u32[]{:S(2)}, u32[]{:S(2)}) collective-permute-start(bf16[1296,128]{1,0:T(8,128)(2,1)S(1)} %collective-permute-done.7.refs_10_), channel_id=1, source_target_pairs={{0,2},{2,4},{4,6},{6,8},{8,10},{10,12},{12,14},{14,0},{1,15},{3,1}... | collective-permute-start | bytes 995336 | tf_op jit(solution)/shard_map/ppermute | solution.py:172
  50.7 7.5 %collective-permute-start.17 = (bf16[1296,128]{1,0:T(8,128)(2,1)S(1)}, bf16[1296,128]{1,0:T(8,128)(2,1)S(1)}, u32[]{:S(2)}, u32[]{:S(2)}) collective-permute-start(bf16[1296,128]{1,0:T(8,128)(2,1)S(1)} %collective-permute-done.12.refs_18_), channel_id=1, source_target_pairs={{0,2},{2,4},{4,6},{6,8},{8,10},{10,12},{12,14},{14,0},{1,15},{3,1}... | collective-permute-start | bytes 995336 | tf_op jit(solution)/shard_map/ppermute | solution.py:172
  54.2 7.5 %collective-permute-start.15 = (bf16[1296,128]{1,0:T(8,128)(2,1)S(1)}, bf16[1296,128]{1,0:T(8,128)(2,1)S(1)}, u32[]{:S(2)}, u32[]{:S(2)}) collective-permute-start(bf16[1296,128]{1,0:T(8,128)(2,1)S(1)} %collective-permute-done.8.refs_11_), channel_id=1, source_target_pairs={{0,2},{2,4},{4,6},{6,8},{8,10},{10,12},{12,14},{14,0},{1,15},{3,1}... | collective-permute-start | bytes 995336 | tf_op jit(solution)/shard_map/ppermute | solution.py:172
  58.2 7.5 %collective-permute-start.18 = (bf16[1296,128]{1,0:T(8,128)(2,1)S(1)}, bf16[1296,128]{1,0:T(8,128)(2,1)S(1)}, u32[]{:S(2)}, u32[]{:S(2)}) collective-permute-start(bf16[1296,128]{1,0:T(8,128)(2,1)S(1)} %collective-permute-done.17.refs_19_), channel_id=1, source_target_pairs={{0,2},{2,4},{4,6},{6,8},{8,10},{10,12},{12,14},{14,0},{1,15},{3,1}... | collective-permute-start | bytes 995336 | tf_op jit(solution)/shard_map/ppermute | solution.py:172
  61.7 9.5 %collective-permute-start.16 = (bf16[1296,128]{1,0:T(8,128)(2,1)S(1)}, bf16[1296,128]{1,0:T(8,128)(2,1)S(1)}, u32[]{:S(2)}, u32[]{:S(2)}) collective-permute-start(bf16[1296,128]{1,0:T(8,128)(2,1)S(1)} %collective-permute-done.15.refs_12_), channel_id=1, source_target_pairs={{0,2},{2,4},{4,6},{6,8},{8,10},{10,12},{12,14},{14,0},{1,15},{3,1}... | collective-permute-start | bytes 995336 | tf_op jit(solution)/shard_map/ppermute | solution.py:172
  65.6 7.5 %collective-permute-start.19 = (bf16[1296,128]{1,0:T(8,128)(2,1)S(1)}, bf16[1296,128]{1,0:T(8,128)(2,1)S(1)}, u32[]{:S(2)}, u32[]{:S(2)}) collective-permute-start(bf16[1296,128]{1,0:T(8,128)(2,1)S(1)} %collective-permute-done.18.refs_20_), channel_id=1, source_target_pairs={{0,2},{2,4},{4,6},{6,8},{8,10},{10,12},{12,14},{14,0},{1,15},{3,1}... | collective-permute-start | bytes 995336 | tf_op jit(solution)/shard_map/ppermute | solution.py:172
  69.0 11.1 %collective-permute-start.13 = (bf16[288,4608]{1,0:T(8,128)(2,1)S(1)}, bf16[288,4608]{1,0:T(8,128)(2,1)S(1)}, u32[]{:S(2)}, u32[]{:S(2)}) collective-permute-start(bf16[288,4608]{1,0:T(8,128)(2,1)S(1)} %collective-permute-done.4.refs_2_), channel_id=1, source_target_pairs={{0,1},{1,0},{2,3},{3,2},{4,5},{5,4},{6,7},{7,6},{8,9},{9,8},{10,11... | collective-permute-start | bytes 7962632 | tf_op jit(solution)/shard_map/ppermute | solution.py:221
  76.0 8.6 %collective-permute-start.20 = (bf16[288,4608]{1,0:T(8,128)(2,1)S(1)}, bf16[288,4608]{1,0:T(8,128)(2,1)S(1)}, u32[]{:S(2)}, u32[]{:S(2)}) collective-permute-start(bf16[288,4608]{1,0:T(8,128)(2,1)S(1)} %collective-permute-done.14.refs_4_), channel_id=1, source_target_pairs={{0,1},{1,0},{2,3},{3,2},{4,5},{5,4},{6,7},{7,6},{8,9},{9,8},{10,11... | collective-permute-start | bytes 7962632 | tf_op jit(solution)/shard_map/ppermute | solution.py:221
  103.2 18.7 %collective-permute-start.21 = (f32[576,288]{0,1:T(8,128)}, f32[576,288]{0,1:T(8,128)}, u32[]{:S(2)}, u32[]{:S(2)}) collective-permute-start(f32[576,288]{0,1:T(8,128)} %copy.8), channel_id=1, source_target_pairs={{0,16},{16,0},{1,17},{17,1},{2,18},{18,2},{3,19},{19,3},{4,20},{20... | collective-permute-start | bytes 1990664 | tf_op jit(solution)/shard_map/ppermute | solution.py:272
  104.7 38.5 %all-to-all-start = ((f16[256,4,384]{2,1,0:T(4,128)(2,1)}), f16[256,4,384]{2,1,0:T(4,128)(2,1)}, u32[]{:S(2)}, u32[]{:S(2)}) async-start(f16[256,4,384]{2,1,0:T(4,128)(2,1)} %convert_element_type.9), calls=%async_computation | async-start | bytes 1572864 | tf_op jit(solution)/shard_map/all_to_all | solution.py:275
  127.1 17.6 %collective-permute-start.22 = (f32[2,288,288]{2,1,0:T(8,128)}, f32[2,288,288]{2,1,0:T(8,128)}, u32[]{:S(2)}, u32[]{:S(2)}) collective-permute-start(f32[2,288,288]{2,1,0:T(8,128)} %pad_maximum_fusion), channel_id=1, source_target_pairs={{0,1},{1,0},{2,3},{3,2},{4,5},{5,4},{6,7},{7,6},{8,9},{9,8},{10,11... | collective-permute-start | bytes 1990664 | tf_op jit(solution)/shard_map/ppermute | solution.py:273
  (7 other events, 180.7 us)
